TPU v7x, 1024 devices: a whole 8x8x8 slice. The times are simulated.
1024 devices in a mesh: ctx: 64 (over y, x), head: 16 (over z, core).
Axes of the slice: x: 8, y: 8, z: 8, core: 2. Of those that a mesh axis runs over, the one named last changes fastest.
Arguments:
- queries: bfloat16 [8192, 8192], P('ctx', 'head'), may hold values from -6 to 6
- key_rows: bfloat16 [8192, 8192], P('ctx', 'head'), may hold values from -6 to 6
- value_rows: bfloat16 [8192, 8192], P('ctx', 'head'), may hold values from -6 to 6
- gate_in: bfloat16 [8192, 8192], P('ctx', 'head'), may hold values from -6 to 6
- grad_out: bfloat16 [8192, 8192], P('ctx', 'head'), may hold values from -6 to 6
- decay_ints: int32 [64], P('head'), may hold values from 1 to 32767, as said below
- norm_gain: float32 [8192], P('head'), may hold values from 0.1 to 1.9
Outputs:
- grad_queries: bfloat16 [8192, 8192], P('ctx', 'head')
- grad_keys: bfloat16 [8192, 8192], P('ctx', 'head')
- grad_values: bfloat16 [8192, 8192], P('ctx', 'head')
- grad_gate: bfloat16 [8192, 8192], P('ctx', 'head')
- grad_gain: float32 [8192], P('head')
Inputs may be any that keep to these rules, and one draw needn't show every extreme that they name: Head h forgets as exp(-decay_ints[h] / 1048576) per token.
All inputs are finite; a program needn't handle non-finite values.
Results may differ from a plain program's by a relative error of at most 0.005.
Values sent between devices are 32-bit elements; how exact they have to be, the bound alone decides.
No kernel may reach another device: no remote copies, remote signals or barrier semaphores. Data moves between devices by JAX's collectives and lax.ppermute only.
A program may use at most 128 MiB of HBM per device.

v0:
```python
import jax
import jax.numpy as jnp
from jax import lax
from jax.sharding import PartitionSpec as P

DH = 128
HD = 8192


rate_unit = 2.0 ** (-20)
norm_eps = 1e-06


def from_behind(array, axis, by):
    length = lax.axis_size(axis)
    pairs = [(i, i + by) for i in range(length) if 0 <= i + by < length]
    return lax.ppermute(array, axis, pairs)


def combine(earlier, later):
    return (earlier[0] * later[0], later[0][:, None, None] * earlier[1] + later[1])


def stride_list(members):
    strides = [1]
    stride = 1
    while stride < members:
        strides.append(stride)
        stride = stride * 2
    return strides


def forward_steps(block_span, summary):
    running = (block_span, summary)
    for number, stride in enumerate(stride_list(lax.axis_size("ctx"))):
        arrived = from_behind((running[0], running[1]), "ctx", stride)
        running = arrived if number == 0 else combine(arrived, running)
    return running[1]


def backward_steps(block_span, summary):
    running = (block_span, summary)
    for number, stride in enumerate(stride_list(lax.axis_size("ctx"))):
        arrived = from_behind((running[0], running[1]), "ctx", -stride)
        running = arrived if number == 0 else combine(arrived, running)
    return running[1]


def body(queries, key_rows, value_rows, gate_in, grad_out, decay_ints, norm_gain):
    row_count, feature_count = queries.shape
    head_count = feature_count // DH
    decay_rate = decay_ints.astype(jnp.float32) * rate_unit
    positions = jnp.arange(row_count, dtype=jnp.float32)
    early_decay = jnp.exp(-decay_rate[None, :] * (positions[:, None] + 1.0))
    late_decay = jnp.exp(-decay_rate[None, :] * (row_count - 1.0 - positions[:, None]))
    distance = positions[:, None] - positions[None, :]
    decay_matrix = (
        jnp.where(
            distance[None] >= 0.0,
            jnp.exp(-decay_rate[:, None, None] * jnp.maximum(distance, 0.0)[None]),
            0.0,
        )
        / DH
    )
    block_span = jnp.exp(-decay_rate * row_count)
    q_heads = queries.reshape(row_count, head_count, DH)
    k_heads = key_rows.reshape(row_count, head_count, DH)
    v_heads = value_rows.reshape(row_count, head_count, DH)
    highest = lax.Precision.HIGHEST
    summary = jnp.einsum(
        "shd,she->hde",
        late_decay[:, :, None] * k_heads.astype(jnp.float32),
        v_heads.astype(jnp.float32),
        precision=highest,
    )
    prefix = forward_steps(block_span, summary)
    scores = jnp.einsum("thd,shd->hts", q_heads, k_heads, preferred_element_type=jnp.float32)
    attn_weights = (scores * decay_matrix).astype(jnp.bfloat16)
    attention = jnp.einsum(
        "hts,she->the", attn_weights, v_heads, preferred_element_type=jnp.float32
    )
    carried = jnp.einsum("thd,hde->the", q_heads.astype(jnp.float32), prefix, precision=highest)
    attention = (attention + early_decay[:, :, None] * carried / DH).reshape(
        row_count, feature_count
    )
    gate_value = jax.nn.sigmoid(gate_in.astype(jnp.float32))
    grad_float = grad_out.astype(jnp.float32)
    grad_normed = grad_float * norm_gain * gate_value
    squares, crossed = lax.psum(
        (jnp.sum(attention * attention, axis=1), jnp.sum(grad_normed * attention, axis=1)), "head"
    )
    inverse = lax.rsqrt(squares / HD + norm_eps)[:, None]
    normed = attention * inverse
    grad_gate = (grad_float * normed * norm_gain * gate_value * (1.0 - gate_value)).astype(
        jnp.bfloat16
    )
    grad_gain = lax.psum(jnp.sum(grad_float * normed * gate_value, axis=0), "ctx")
    grad_attention = (inverse * (grad_normed - normed * inverse * crossed[:, None] / HD)).astype(
        jnp.bfloat16
    )
    grad_heads = grad_attention.reshape(row_count, head_count, DH)
    grad_wide = grad_heads.astype(jnp.float32)
    ahead_sum = jnp.einsum(
        "thd,the->hde",
        early_decay[:, :, None] * q_heads.astype(jnp.float32),
        grad_wide,
        precision=highest,
    )
    suffix = backward_steps(block_span, ahead_sum)
    grad_scores = (
        jnp.einsum("the,she->hts", grad_heads, v_heads, preferred_element_type=jnp.float32)
        * decay_matrix
    ).astype(jnp.bfloat16)
    grad_q = jnp.einsum("hts,shd->thd", grad_scores, k_heads, preferred_element_type=jnp.float32)
    grad_q = (
        grad_q
        + early_decay[:, :, None]
        * jnp.einsum("the,hde->thd", grad_wide, prefix, precision=highest)
        / DH
    )
    grad_k = jnp.einsum("hts,thd->shd", grad_scores, q_heads, preferred_element_type=jnp.float32)
    grad_k = (
        grad_k
        + late_decay[:, :, None]
        * jnp.einsum("she,hde->shd", v_heads.astype(jnp.float32), suffix, precision=highest)
        / DH
    )
    grad_v = jnp.einsum(
        "hts,the->she", attn_weights, grad_heads, preferred_element_type=jnp.float32
    )
    grad_v = (
        grad_v
        + late_decay[:, :, None]
        * jnp.einsum("shd,hde->she", k_heads.astype(jnp.float32), suffix, precision=highest)
        / DH
    )
    shape_out = (row_count, feature_count)
    return (
        grad_q.reshape(shape_out).astype(jnp.bfloat16),
        grad_k.reshape(shape_out).astype(jnp.bfloat16),
        grad_v.reshape(shape_out).astype(jnp.bfloat16),
        grad_gate,
        grad_gain,
    )


def solution(mesh):
    placed = (
        P("ctx", "head"),
        P("ctx", "head"),
        P("ctx", "head"),
        P("ctx", "head"),
        P("ctx", "head"),
        P("head"),
        P("head"),
    )
    return jax.shard_map(
        body,
        mesh=mesh,
        in_specs=placed,
        out_specs=(
            P("ctx", "head"),
            P("ctx", "head"),
            P("ctx", "head"),
            P("ctx", "head"),
            P("head"),
        ),
        check_vma=False,
    )
```

profile of v0, /device:TPU:2, one launch (start us, length us, event | category | flops | bytes accessed | tf_op | source)
XLA Modules:
  0.0 421.3 jit_solution(15808952289902778296)
XLA Ops:
  0.7 1.1 copy.13
  2.1 3.4 collective-permute-start.6
  5.5 15.4 %collective-permute-done.6 = f32[4,128,128]{2,1,0:T(8,128)S(1)} collective-permute-done((f32[4,128,128]{2,1,0:T(8,128)S(1)}, f32[4,128,128]{2,1,0:T(8,128)S(1)}, u32[]{:S(2)}, u32[]{:S(2)}) %collective-permute-start.6) | collective-permute-done | bytes 262176 | tf_op jit(solution)/shard_map/ppermute | solution.py:17
  20.9 1.9 collective-permute-start.7
  22.8 1.9 collective-permute-start
  24.8 12.7 %collective-permute-done = f32[4]{0:T(128)S(1)} collective-permute-done((f32[4]{0:T(128)S(1)}, f32[4]{0:T(128)S(1)}, u32[]{:S(2)}, u32[]{:S(2)}) %collective-permute-start) | collective-permute-done | bytes 48 | tf_op jit(solution)/shard_map/ppermute | solution.py:17
  37.6 1.3 collective-permute-start.8
  38.9 1.9 collective-permute-start.1
  40.8 10.8 %collective-permute-done.1 = f32[4]{0:T(128)S(1)} collective-permute-done((f32[4]{0:T(128)S(1)}, f32[4]{0:T(128)S(1)}, u32[]{:S(2)}, u32[]{:S(2)}) %collective-permute-start.1) | collective-permute-done | bytes 48 | tf_op jit(solution)/shard_map/ppermute | solution.py:17
  51.8 1.3 collective-permute-start.9
  53.1 5.3 %collective-permute-start.2 = (f32[4]{0:T(128)S(1)}, f32[4]{0:T(128)S(1)}, u32[]{:S(2)}, u32[]{:S(2)}) collective-permute-start(f32[4]{0:T(128)S(1)} %mul.298), channel_id=1, source_target_pairs={{0,32},{16,48},{32,64},{48,80},{64,96},{80,112},{96,128},{112,144}... | collective-permute-start | bytes 56 | tf_op jit(solution)/shard_map/ppermute | solution.py:17
  58.4 1.3 collective-permute-done.2
  59.8 1.3 collective-permute-start.10
  61.1 5.8 %collective-permute-start.3 = (f32[4]{0:T(128)S(1)}, f32[4]{0:T(128)S(1)}, u32[]{:S(2)}, u32[]{:S(2)}) collective-permute-start(f32[4]{0:T(128)S(1)} %mul.299), channel_id=1, source_target_pairs={{0,64},{16,80},{32,96},{48,112},{64,128},{80,144},{96,160},{112,17... | collective-permute-start | bytes 56 | tf_op jit(solution)/shard_map/ppermute | solution.py:17
  66.8 1.3 collective-permute-done.3
  68.2 3.1 collective-permute-start.11
  71.5 6.1 %collective-permute-start.4 = (f32[4]{0:T(128)S(1)}, f32[4]{0:T(128)S(1)}, u32[]{:S(2)}, u32[]{:S(2)}) collective-permute-start(f32[4]{0:T(128)S(1)} %mul.300), channel_id=1, source_target_pairs={{0,128},{16,144},{32,160},{48,176},{64,192},{80,208},{96,224},{112... | collective-permute-start | bytes 56 | tf_op jit(solution)/shard_map/ppermute | solution.py:17
  77.6 1.3 collective-permute-done.4
  79.0 13.6 %collective-permute-start.12 = (f32[4,128,128]{2,1,0:T(8,128)S(1)}, f32[4,128,128]{2,1,0:T(8,128)S(1)}, u32[]{:S(2)}, u32[]{:S(2)}) collective-permute-start(f32[4,128,128]{2,1,0:T(8,128)S(1)} %multiply_add_fusion.7), channel_id=1, source_target_pairs={{0,512},{16,528},{32,544},{48,560},{64,576},{80,592},{96,608},{112... | collective-permute-start | bytes 786440 | tf_op jit(solution)/shard_map/ppermute | solution.py:17
  93.1 2.0 collective-permute-start.5
  95.1 1.4 collective-permute-done.5
  97.2 35.9 %psum.21 = f32[128]{0:T(128)S(1)} all-reduce(f32[128]{0:T(128)S(1)} %get-tuple-element.17), channel_id=1, replica_groups=mesh['ctx'=64,'head'=16] {'head'}, use_global_device_ids=true, to_apply=%region_1.2 | all-reduce | flops 128 | bytes 1024 | tf_op jit(solution)/shard_map/psum | solution.py:89
  133.1 0.8 multiply_reduce_fusion
  133.9 23.9 %psum.22 = f32[128]{0:T(128)S(1)} all-reduce(f32[128]{0:T(128)S(1)} %get-tuple-element.11), channel_id=1, replica_groups=mesh['ctx'=64,'head'=16] {'head'}, use_global_device_ids=true, to_apply=%region_3.4 | all-reduce | flops 128 | bytes 1024 | tf_op jit(solution)/shard_map/psum | solution.py:89
  158.4 12.9 %collective-permute-start.19 = (f32[4,128,128]{2,1,0:T(8,128)S(1)}, f32[4,128,128]{2,1,0:T(8,128)S(1)}, u32[]{:S(2)}, u32[]{:S(2)}) collective-permute-start(f32[4,128,128]{2,1,0:T(8,128)S(1)} %fusion.18), channel_id=1, source_target_pairs={{16,0},{32,16},{48,32},{64,48},{80,64},{96,80},{112,96},{128,112},... | collective-permute-start | bytes 786440 | tf_op jit(solution)/shard_map/ppermute | solution.py:17
  171.3 5.6 %collective-permute-done.19 = f32[4,128,128]{2,1,0:T(8,128)S(1)} collective-permute-done((f32[4,128,128]{2,1,0:T(8,128)S(1)}, f32[4,128,128]{2,1,0:T(8,128)S(1)}, u32[]{:S(2)}, u32[]{:S(2)}) %collective-permute-start.19) | collective-permute-done | bytes 262176 | tf_op jit(solution)/shard_map/ppermute | solution.py:17
  176.9 4.4 %collective-permute-start.20 = (f32[4,128,128]{2,1,0:T(8,128)S(1)}, f32[4,128,128]{2,1,0:T(8,128)S(1)}, u32[]{:S(2)}, u32[]{:S(2)}) collective-permute-start(f32[4,128,128]{2,1,0:T(8,128)S(1)} %collective-permute-done.19), channel_id=1, source_target_pairs={{16,0},{32,16},{48,32},{64,48},{80,64},{96,80},{112,96},{128,112},... | collective-permute-start | bytes 786440 | tf_op jit(solution)/shard_map/ppermute | solution.py:17
  181.3 1.9 collective-permute-start.13
  183.2 3.5 collective-permute-done.13
  186.8 1.3 collective-permute-start.21
  188.1 3.7 collective-permute-start.14
  191.8 9.0 %collective-permute-done.14 = f32[4]{0:T(128)S(1)} collective-permute-done((f32[4]{0:T(128)S(1)}, f32[4]{0:T(128)S(1)}, u32[]{:S(2)}, u32[]{:S(2)}) %collective-permute-start.14) | collective-permute-done | bytes 48 | tf_op jit(solution)/shard_map/ppermute | solution.py:17
  201.5 1.3 collective-permute-start.22
  202.8 1.3 collective-permute-start.15
  204.1 5.1 %collective-permute-done.15 = f32[4]{0:T(128)S(1)} collective-permute-done((f32[4]{0:T(128)S(1)}, f32[4]{0:T(128)S(1)}, u32[]{:S(2)}, u32[]{:S(2)}) %collective-permute-start.15) | collective-permute-done | bytes 48 | tf_op jit(solution)/shard_map/ppermute | solution.py:17
  209.2 11.0 %collective-permute-done.22 = f32[4,128,128]{2,1,0:T(8,128)S(1)} collective-permute-done((f32[4,128,128]{2,1,0:T(8,128)S(1)}, f32[4,128,128]{2,1,0:T(8,128)S(1)}, u32[]{:S(2)}, u32[]{:S(2)}) %collective-permute-start.22) | collective-permute-done | bytes 262176 | tf_op jit(solution)/shard_map/ppermute | solution.py:17
  220.3 1.3 collective-permute-start.23
  221.6 1.3 collective-permute-start.16
  222.9 8.0 %collective-permute-done.16 = f32[4]{0:T(128)S(1)} collective-permute-done((f32[4]{0:T(128)S(1)}, f32[4]{0:T(128)S(1)}, u32[]{:S(2)}, u32[]{:S(2)}) %collective-permute-start.16) | collective-permute-done | bytes 48 | tf_op jit(solution)/shard_map/ppermute | solution.py:17
  230.9 1.3 collective-permute-start.17
  232.2 7.7 %collective-permute-done.17 = f32[4]{0:T(128)S(1)} collective-permute-done((f32[4]{0:T(128)S(1)}, f32[4]{0:T(128)S(1)}, u32[]{:S(2)}, u32[]{:S(2)}) %collective-permute-start.17) | collective-permute-done | bytes 48 | tf_op jit(solution)/shard_map/ppermute | solution.py:17
  239.9 1.3 collective-permute-start.18
  241.2 6.4 %collective-permute-done.18 = f32[4]{0:T(128)S(1)} collective-permute-done((f32[4]{0:T(128)S(1)}, f32[4]{0:T(128)S(1)}, u32[]{:S(2)}, u32[]{:S(2)}) %collective-permute-start.18) | collective-permute-done | bytes 48 | tf_op jit(solution)/shard_map/ppermute | solution.py:17
  248.0 1.3 collective-permute-start.24
  249.9 13.2 %collective-permute-done.24 = f32[4,128,128]{2,1,0:T(8,128)S(1)} collective-permute-done((f32[4,128,128]{2,1,0:T(8,128)S(1)}, f32[4,128,128]{2,1,0:T(8,128)S(1)}, u32[]{:S(2)}, u32[]{:S(2)}) %collective-permute-start.24) | collective-permute-done | bytes 262176 | tf_op jit(solution)/shard_map/ppermute | solution.py:17
  263.1 1.3 collective-permute-start.25
  264.6 0.8 copy.30
  265.4 153.3 %psum.23 = f32[512]{0:T(512)} all-reduce(f32[512]{0:T(512)S(1)} %get-tuple-element.10), channel_id=1, replica_groups=mesh['ctx'=64,'head'=16] {'ctx'}, use_global_device_ids=true, to_apply=%region_5.6 | all-reduce | flops 512 | bytes 4096 | tf_op jit(solution)/shard_map/psum | solution.py:97
  (66 shorter events, 7.5 us)
Async XLA Ops:
  0.6 1.2 copy-start
  0.7 1.1 copy-start.5
  2.1 18.8 %collective-permute-start.6 = (f32[4,128,128]{2,1,0:T(8,128)S(1)}, f32[4,128,128]{2,1,0:T(8,128)S(1)}, u32[]{:S(2)}, u32[]{:S(2)}) collective-permute-start(f32[4,128,128]{2,1,0:T(8,128)S(1)} %fusion.21), channel_id=1, source_target_pairs={{0,16},{16,32},{32,48},{48,64},{64,80},{80,96},{96,112},{112,128},... | collective-permute-start | bytes 786440 | tf_op jit(solution)/shard_map/ppermute | solution.py:17
  20.9 16.6 %collective-permute-start.7 = (f32[4,128,128]{2,1,0:T(8,128)S(1)}, f32[4,128,128]{2,1,0:T(8,128)S(1)}, u32[]{:S(2)}, u32[]{:S(2)}) collective-permute-start(f32[4,128,128]{2,1,0:T(8,128)S(1)} %collective-permute-done.6), channel_id=1, source_target_pairs={{0,16},{16,32},{32,48},{48,64},{64,80},{80,96},{96,112},{112,128},... | collective-permute-start | bytes 786440 | tf_op jit(solution)/shard_map/ppermute | solution.py:17
  22.8 14.6 %collective-permute-start = (f32[4]{0:T(128)S(1)}, f32[4]{0:T(128)S(1)}, u32[]{:S(2)}, u32[]{:S(2)}) collective-permute-start(f32[4]{0:T(128)S(1)} %get-tuple-element.13), channel_id=1, source_target_pairs={{0,16},{16,32},{32,48},{48,64},{64,80},{80,96},{96,112},{112,128},... | collective-permute-start | bytes 56 | tf_op jit(solution)/shard_map/ppermute | solution.py:17
  37.6 14.1 %collective-permute-start.8 = (f32[4,128,128]{2,1,0:T(8,128)S(1)}, f32[4,128,128]{2,1,0:T(8,128)S(1)}, u32[]{:S(2)}, u32[]{:S(2)}) collective-permute-start(f32[4,128,128]{2,1,0:T(8,128)S(1)} %multiply_add_fusion.11), channel_id=1, source_target_pairs={{0,32},{16,48},{32,64},{48,80},{64,96},{80,112},{96,128},{112,144}... | collective-permute-start | bytes 786440 | tf_op jit(solution)/shard_map/ppermute | solution.py:17
  38.9 12.8 %collective-permute-start.1 = (f32[4]{0:T(128)S(1)}, f32[4]{0:T(128)S(1)}, u32[]{:S(2)}, u32[]{:S(2)}) collective-permute-start(f32[4]{0:T(128)S(1)} %collective-permute-done), channel_id=1, source_target_pairs={{0,16},{16,32},{32,48},{48,64},{64,80},{80,96},{96,112},{112,128},... | collective-permute-start | bytes 56 | tf_op jit(solution)/shard_map/ppermute | solution.py:17
  51.8 7.9 %collective-permute-start.9 = (f32[4,128,128]{2,1,0:T(8,128)S(1)}, f32[4,128,128]{2,1,0:T(8,128)S(1)}, u32[]{:S(2)}, u32[]{:S(2)}) collective-permute-start(f32[4,128,128]{2,1,0:T(8,128)S(1)} %multiply_add_fusion.10), channel_id=1, source_target_pairs={{0,64},{16,80},{32,96},{48,112},{64,128},{80,144},{96,160},{112,17... | collective-permute-start | bytes 786440 | tf_op jit(solution)/shard_map/ppermute | solution.py:17
  53.1 6.6 %collective-permute-start.2 = (f32[4]{0:T(128)S(1)}, f32[4]{0:T(128)S(1)}, u32[]{:S(2)}, u32[]{:S(2)}) collective-permute-start(f32[4]{0:T(128)S(1)} %mul.298), channel_id=1, source_target_pairs={{0,32},{16,48},{32,64},{48,80},{64,96},{80,112},{96,128},{112,144}... | collective-permute-start | bytes 56 | tf_op jit(solution)/shard_map/ppermute | solution.py:17
  59.8 8.4 %collective-permute-start.10 = (f32[4,128,128]{2,1,0:T(8,128)S(1)}, f32[4,128,128]{2,1,0:T(8,128)S(1)}, u32[]{:S(2)}, u32[]{:S(2)}) collective-permute-start(f32[4,128,128]{2,1,0:T(8,128)S(1)} %multiply_add_fusion.9), channel_id=1, source_target_pairs={{0,128},{16,144},{32,160},{48,176},{64,192},{80,208},{96,224},{112... | collective-permute-start | bytes 786440 | tf_op jit(solution)/shard_map/ppermute | solution.py:17
  61.1 7.0 %collective-permute-start.3 = (f32[4]{0:T(128)S(1)}, f32[4]{0:T(128)S(1)}, u32[]{:S(2)}, u32[]{:S(2)}) collective-permute-start(f32[4]{0:T(128)S(1)} %mul.299), channel_id=1, source_target_pairs={{0,64},{16,80},{32,96},{48,112},{64,128},{80,144},{96,160},{112,17... | collective-permute-start | bytes 56 | tf_op jit(solution)/shard_map/ppermute | solution.py:17
  68.1 3.2 copy-start.3
  68.2 10.7 %collective-permute-start.11 = (f32[4,128,128]{2,1,0:T(8,128)S(1)}, f32[4,128,128]{2,1,0:T(8,128)S(1)}, u32[]{:S(2)}, u32[]{:S(2)}) collective-permute-start(f32[4,128,128]{2,1,0:T(8,128)S(1)} %multiply_add_fusion.8), channel_id=1, source_target_pairs={{0,256},{16,272},{32,288},{48,304},{64,320},{80,336},{96,352},{112... | collective-permute-start | bytes 786440 | tf_op jit(solution)/shard_map/ppermute | solution.py:17
  71.5 7.4 %collective-permute-start.4 = (f32[4]{0:T(128)S(1)}, f32[4]{0:T(128)S(1)}, u32[]{:S(2)}, u32[]{:S(2)}) collective-permute-start(f32[4]{0:T(128)S(1)} %mul.300), channel_id=1, source_target_pairs={{0,128},{16,144},{32,160},{48,176},{64,192},{80,208},{96,224},{112... | collective-permute-start | bytes 56 | tf_op jit(solution)/shard_map/ppermute | solution.py:17
  79.0 17.5 %collective-permute-start.12 = (f32[4,128,128]{2,1,0:T(8,128)S(1)}, f32[4,128,128]{2,1,0:T(8,128)S(1)}, u32[]{:S(2)}, u32[]{:S(2)}) collective-permute-start(f32[4,128,128]{2,1,0:T(8,128)S(1)} %multiply_add_fusion.7), channel_id=1, source_target_pairs={{0,512},{16,528},{32,544},{48,560},{64,576},{80,592},{96,608},{112... | collective-permute-start | bytes 786440 | tf_op jit(solution)/shard_map/ppermute | solution.py:17
  93.1 3.4 collective-permute-start.5
  97.0 36.0 %copy-start.1 = (bf16[128,512]{1,0:T(8,128)(2,1)S(1)}, bf16[128,512]{1,0:T(8,128)(2,1)}, u32[]{:S(2)}) copy-start(bf16[128,512]{1,0:T(8,128)(2,1)} %param.11) | copy-start | bytes 393220
  97.0 36.0 %copy-start.2 = (bf16[128,512]{1,0:T(8,128)(2,1)S(1)}, bf16[128,512]{1,0:T(8,128)(2,1)}, u32[]{:S(2)}) copy-start(bf16[128,512]{1,0:T(8,128)(2,1)} %param.10) | copy-start | bytes 393220
  97.2 35.9 %copy-start.4 = (f32[512]{0:T(512)S(1)}, f32[512]{0:T(512)}, u32[]{:S(2)}) copy-start(f32[512]{0:T(512)} %param.13) | copy-start | bytes 6148
  158.4 18.4 %collective-permute-start.19 = (f32[4,128,128]{2,1,0:T(8,128)S(1)}, f32[4,128,128]{2,1,0:T(8,128)S(1)}, u32[]{:S(2)}, u32[]{:S(2)}) collective-permute-start(f32[4,128,128]{2,1,0:T(8,128)S(1)} %fusion.18), channel_id=1, source_target_pairs={{16,0},{32,16},{48,32},{64,48},{80,64},{96,80},{112,96},{128,112},... | collective-permute-start | bytes 786440 | tf_op jit(solution)/shard_map/ppermute | solution.py:17
  176.9 9.8 %collective-permute-start.20 = (f32[4,128,128]{2,1,0:T(8,128)S(1)}, f32[4,128,128]{2,1,0:T(8,128)S(1)}, u32[]{:S(2)}, u32[]{:S(2)}) collective-permute-start(f32[4,128,128]{2,1,0:T(8,128)S(1)} %collective-permute-done.19), channel_id=1, source_target_pairs={{16,0},{32,16},{48,32},{64,48},{80,64},{96,80},{112,96},{128,112},... | collective-permute-start | bytes 786440 | tf_op jit(solution)/shard_map/ppermute | solution.py:17
  181.3 5.4 %collective-permute-start.13 = (f32[4]{0:T(128)S(1)}, f32[4]{0:T(128)S(1)}, u32[]{:S(2)}, u32[]{:S(2)}) collective-permute-start(f32[4]{0:T(128)S(1)} %get-tuple-element.13), channel_id=1, source_target_pairs={{16,0},{32,16},{48,32},{64,48},{80,64},{96,80},{112,96},{128,112},... | collective-permute-start | bytes 56 | tf_op jit(solution)/shard_map/ppermute | solution.py:17
  186.8 14.6 %collective-permute-start.21 = (f32[4,128,128]{2,1,0:T(8,128)S(1)}, f32[4,128,128]{2,1,0:T(8,128)S(1)}, u32[]{:S(2)}, u32[]{:S(2)}) collective-permute-start(f32[4,128,128]{2,1,0:T(8,128)S(1)} %multiply_add_fusion.5), channel_id=1, source_target_pairs={{32,0},{48,16},{64,32},{80,48},{96,64},{112,80},{128,96},{144,112}... | collective-permute-start | bytes 786440 | tf_op jit(solution)/shard_map/ppermute | solution.py:17
  188.1 12.7 %collective-permute-start.14 = (f32[4]{0:T(128)S(1)}, f32[4]{0:T(128)S(1)}, u32[]{:S(2)}, u32[]{:S(2)}) collective-permute-start(f32[4]{0:T(128)S(1)} %collective-permute-done.13), channel_id=1, source_target_pairs={{16,0},{32,16},{48,32},{64,48},{80,64},{96,80},{112,96},{128,112},... | collective-permute-start | bytes 56 | tf_op jit(solution)/shard_map/ppermute | solution.py:17
  201.5 18.7 %collective-permute-start.22 = (f32[4,128,128]{2,1,0:T(8,128)S(1)}, f32[4,128,128]{2,1,0:T(8,128)S(1)}, u32[]{:S(2)}, u32[]{:S(2)}) collective-permute-start(f32[4,128,128]{2,1,0:T(8,128)S(1)} %multiply_add_fusion.4), channel_id=1, source_target_pairs={{64,0},{80,16},{96,32},{112,48},{128,64},{144,80},{160,96},{176,11... | collective-permute-start | bytes 786440 | tf_op jit(solution)/shard_map/ppermute | solution.py:17
  202.8 6.4 %collective-permute-start.15 = (f32[4]{0:T(128)S(1)}, f32[4]{0:T(128)S(1)}, u32[]{:S(2)}, u32[]{:S(2)}) collective-permute-start(f32[4]{0:T(128)S(1)} %mul.333), channel_id=1, source_target_pairs={{32,0},{48,16},{64,32},{80,48},{96,64},{112,80},{128,96},{144,112}... | collective-permute-start | bytes 56 | tf_op jit(solution)/shard_map/ppermute | solution.py:17
  220.3 27.6 %collective-permute-start.23 = (f32[4,128,128]{2,1,0:T(8,128)S(1)}, f32[4,128,128]{2,1,0:T(8,128)S(1)}, u32[]{:S(2)}, u32[]{:S(2)}) collective-permute-start(f32[4,128,128]{2,1,0:T(8,128)S(1)} %multiply_add_fusion.3), channel_id=1, source_target_pairs={{128,0},{144,16},{160,32},{176,48},{192,64},{208,80},{224,96},{240... | collective-permute-start | bytes 786440 | tf_op jit(solution)/shard_map/ppermute | solution.py:17
  221.6 9.3 %collective-permute-start.16 = (f32[4]{0:T(128)S(1)}, f32[4]{0:T(128)S(1)}, u32[]{:S(2)}, u32[]{:S(2)}) collective-permute-start(f32[4]{0:T(128)S(1)} %mul.334), channel_id=1, source_target_pairs={{64,0},{80,16},{96,32},{112,48},{128,64},{144,80},{160,96},{176,11... | collective-permute-start | bytes 56 | tf_op jit(solution)/shard_map/ppermute | solution.py:17
  230.9 9.0 %collective-permute-start.17 = (f32[4]{0:T(128)S(1)}, f32[4]{0:T(128)S(1)}, u32[]{:S(2)}, u32[]{:S(2)}) collective-permute-start(f32[4]{0:T(128)S(1)} %mul.335), channel_id=1, source_target_pairs={{128,0},{144,16},{160,32},{176,48},{192,64},{208,80},{224,96},{240... | collective-permute-start | bytes 56 | tf_op jit(solution)/shard_map/ppermute | solution.py:17
  239.9 7.7 %collective-permute-start.18 = (f32[4]{0:T(128)S(1)}, f32[4]{0:T(128)S(1)}, u32[]{:S(2)}, u32[]{:S(2)}) collective-permute-start(f32[4]{0:T(128)S(1)} %mul.336), channel_id=1, source_target_pairs={{256,0},{272,16},{288,32},{304,48},{320,64},{336,80},{352,96},{368... | collective-permute-start | bytes 56 | tf_op jit(solution)/shard_map/ppermute | solution.py:17
  248.0 15.1 %collective-permute-start.24 = (f32[4,128,128]{2,1,0:T(8,128)S(1)}, f32[4,128,128]{2,1,0:T(8,128)S(1)}, u32[]{:S(2)}, u32[]{:S(2)}) collective-permute-start(f32[4,128,128]{2,1,0:T(8,128)S(1)} %multiply_add_fusion.2), channel_id=1, source_target_pairs={{256,0},{272,16},{288,32},{304,48},{320,64},{336,80},{352,96},{368... | collective-permute-start | bytes 786440 | tf_op jit(solution)/shard_map/ppermute | solution.py:17
  263.1 155.7 %collective-permute-start.25 = (f32[4,128,128]{2,1,0:T(8,128)S(1)}, f32[4,128,128]{2,1,0:T(8,128)S(1)}, u32[]{:S(2)}, u32[]{:S(2)}) collective-permute-start(f32[4,128,128]{2,1,0:T(8,128)S(1)} %multiply_add_fusion.1), channel_id=1, source_target_pairs={{512,0},{528,16},{544,32},{560,48},{576,64},{592,80},{608,96},{624... | collective-permute-start | bytes 786440 | tf_op jit(solution)/shard_map/ppermute | solution.py:17
where the time goes:
time: 422 us; the launch traced here: 421 us
  blocking collectives  213 us (50%)
  waiting for transfers between devices  114 us (27%)
  starting transfers between devices  83.4 us (20%)
    psum x1, blocking collectives, body(): lax.psum(jnp.sum(grad_float * normed * gate_value, axis=0), 'ctx')  153 us
    ppermute x26, waiting for transfers between devices, from_behind(): return lax.ppermute(array, axis, pairs)  114 us
    ppermute x26, starting transfers between devices, from_behind(): return lax.ppermute(array, axis, pairs)  83.4 us
    psum x2, blocking collectives, body(): lax.psum((jnp.sum(attention * attention, axis=1), jnp.sum(grad_normed * a...  59.7 us
  transfers between devices with their start and end apart: 26, of which 17 were waited for; matrix products, arithmetic and copies ran while one was open for 1% of the time, Pallas kernels for 0%

commit v1 on v0

--- a/solution.py
+++ b/solution.py
@@ -11,45 +11,25 @@
 norm_eps = 1e-06
 
 
-def from_behind(array, axis, by):
-    length = lax.axis_size(axis)
-    pairs = [(i, i + by) for i in range(length) if 0 <= i + by < length]
-    return lax.ppermute(array, axis, pairs)
+def swap(array, axis):
+    return lax.all_to_all(array, axis, 0, 0)
 
 
-def combine(earlier, later):
-    return (earlier[0] * later[0], later[0][:, None, None] * earlier[1] + later[1])
-
-
-def stride_list(members):
-    strides = [1]
-    stride = 1
-    while stride < members:
-        strides.append(stride)
-        stride = stride * 2
-    return strides
-
-
-def forward_steps(block_span, summary):
-    running = (block_span, summary)
-    for number, stride in enumerate(stride_list(lax.axis_size("ctx"))):
-        arrived = from_behind((running[0], running[1]), "ctx", stride)
-        running = arrived if number == 0 else combine(arrived, running)
-    return running[1]
-
-
-def backward_steps(block_span, summary):
-    running = (block_span, summary)
-    for number, stride in enumerate(stride_list(lax.axis_size("ctx"))):
-        arrived = from_behind((running[0], running[1]), "ctx", -stride)
-        running = arrived if number == 0 else combine(arrived, running)
-    return running[1]
+def scan_table(span_rate, members, backward):
+    block = jnp.arange(members, dtype=jnp.float32)
+    gap = block[:, None] - block[None, :]
+    gap = (-gap if backward else gap) - 1.0
+    return jnp.where(gap >= 0.0, jnp.exp(-span_rate * jnp.maximum(gap, 0.0)), 0.0)
 
 
 def body(queries, key_rows, value_rows, gate_in, grad_out, decay_ints, norm_gain):
     row_count, feature_count = queries.shape
     head_count = feature_count // DH
+    members = lax.axis_size("ctx")
+    rows = head_count * DH // members
     decay_rate = decay_ints.astype(jnp.float32) * rate_unit
+    owned_head = lax.axis_index("ctx") * rows // DH
+    span_rate = lax.dynamic_index_in_dim(decay_rate, owned_head, keepdims=False) * row_count
     positions = jnp.arange(row_count, dtype=jnp.float32)
     early_decay = jnp.exp(-decay_rate[None, :] * (positions[:, None] + 1.0))
     late_decay = jnp.exp(-decay_rate[None, :] * (row_count - 1.0 - positions[:, None]))
@@ -62,7 +42,6 @@
         )
         / DH
     )
-    block_span = jnp.exp(-decay_rate * row_count)
     q_heads = queries.reshape(row_count, head_count, DH)
     k_heads = key_rows.reshape(row_count, head_count, DH)
     v_heads = value_rows.reshape(row_count, head_count, DH)
@@ -73,7 +52,11 @@
         v_heads.astype(jnp.float32),
         precision=highest,
     )
-    prefix = forward_steps(block_span, summary)
+    there = swap(summary.reshape(members, rows, DH), "ctx")
+    scanned = jnp.einsum(
+        "cb,brl->crl", scan_table(span_rate, members, False), there, precision=highest
+    )
+    prefix = swap(scanned, "ctx").reshape(head_count, DH, DH)
     scores = jnp.einsum("thd,shd->hts", q_heads, k_heads, preferred_element_type=jnp.float32)
     attn_weights = (scores * decay_matrix).astype(jnp.bfloat16)
     attention = jnp.einsum(
@@ -86,15 +69,19 @@
     gate_value = jax.nn.sigmoid(gate_in.astype(jnp.float32))
     grad_float = grad_out.astype(jnp.float32)
     grad_normed = grad_float * norm_gain * gate_value
-    squares, crossed = lax.psum(
-        (jnp.sum(attention * attention, axis=1), jnp.sum(grad_normed * attention, axis=1)), "head"
+    stats = jnp.stack(
+        [jnp.sum(attention * attention, axis=1), jnp.sum(grad_normed * attention, axis=1)]
     )
+    head_members = lax.axis_size("head")
+    stats = jnp.sum(swap(jnp.broadcast_to(stats, (head_members, 2, row_count)), "head"), axis=0)
+    squares, crossed = stats[0], stats[1]
     inverse = lax.rsqrt(squares / HD + norm_eps)[:, None]
     normed = attention * inverse
     grad_gate = (grad_float * normed * norm_gain * gate_value * (1.0 - gate_value)).astype(
         jnp.bfloat16
     )
-    grad_gain = lax.psum(jnp.sum(grad_float * normed * gate_value, axis=0), "ctx")
+    gain_part = jnp.sum(grad_float * normed * gate_value, axis=0).reshape(1, head_count, DH)
+    gain_rows = jnp.broadcast_to(gain_part, (members // head_count, head_count, DH))
     grad_attention = (inverse * (grad_normed - normed * inverse * crossed[:, None] / HD)).astype(
         jnp.bfloat16
     )
@@ -106,7 +93,18 @@
         grad_wide,
         precision=highest,
     )
-    suffix = backward_steps(block_span, ahead_sum)
+    message = jnp.concatenate(
+        [ahead_sum.reshape(members, rows, DH), gain_rows.reshape(members, 1, DH)], axis=1
+    )
+    there = swap(message[:, :, None, :], "ctx")[:, :, 0, :]
+    scanned = jnp.einsum(
+        "cb,brl->crl", scan_table(span_rate, members, True), there[:, :rows], precision=highest
+    )
+    gain_sum = jnp.broadcast_to(jnp.sum(there[:, rows:], axis=0)[None], (members, 1, DH))
+    message = jnp.concatenate([scanned, gain_sum], axis=1)
+    back = swap(message[:, :, None, :], "ctx")[:, :, 0, :]
+    suffix = back[:, :rows].reshape(head_count, DH, DH)
+    grad_gain = back[:head_count, rows].reshape(feature_count)
     grad_scores = (
         jnp.einsum("the,she->hts", grad_heads, v_heads, preferred_element_type=jnp.float32)
         * decay_matrix

time: 422 us -> 124 us (0.29)
  blocking collectives: 213 us -> 22.1 us
  waiting for transfers between devices: 114 us -> 52.4 us
  starting transfers between devices: 83.4 us -> 32.6 us
  local copies, waits for them, and re-layouts: 3.78 us -> 8.91 us
    psum x3 -> x0, blocking collectives: 213 us -> none  [the longest x1 153 us: body(): lax.psum(jnp.sum(grad_float * normed * gate_value, axis=0), 'ctx')]
    ppermute x26 -> x0, waiting for transfers between devices: 114 us -> none  [from_behind(): return lax.ppermute(array, axis, pairs)]
    ppermute x26 -> x0, starting transfers between devices: 83.4 us -> none  [from_behind(): return lax.ppermute(array, axis, pairs)]
    all_to_all x0 -> x4, waiting for transfers between devices: none -> 52.4 us  [swap(): return lax.all_to_all(array, axis, 0, 0)]
    all_to_all x0 -> x4, starting transfers between devices: none -> 32.6 us  [swap(): return lax.all_to_all(array, axis, 0, 0)]
    all_to_all x0 -> x1, blocking collectives: none -> 22.1 us  [swap(): return lax.all_to_all(array, axis, 0, 0)]
  transfers between devices with their start and end apart: 26 -> 4, of which waited for: 17 -> 4; matrix products, arithmetic and copies ran while one was open for 1% -> 2% of each run, Pallas kernels for 0% -> 0%
where the time goes in v1:
time: 124 us
  waiting for transfers between devices  52.4 us (42%)
  starting transfers between devices  32.6 us (26%)
  blocking collectives  22.1 us (18%)
  local copies, waits for them, and re-layouts  8.91 us (7%)
  matrix products  4.86 us (4%)
  between operations  1.6 us (1%)
  other arithmetic  1.32 us (1%)
    all_to_all x4, waiting for transfers between devices, swap(): return lax.all_to_all(array, axis, 0, 0)  52.4 us
    all_to_all x4, starting transfers between devices, swap(): return lax.all_to_all(array, axis, 0, 0)  32.6 us
    all_to_all x1, blocking collectives, swap(): return lax.all_to_all(array, axis, 0, 0)  22.1 us
    unnamed x17, local copies, waits for them, and re-layouts  4.33 us
  transfers between devices with their start and end apart: 4, of which 4 were waited for; matrix products, arithmetic and copies ran while one was open for 2% of the time, Pallas kernels for 0%

profile of v1, /device:TPU:2, one launch (start us, length us, event | category | flops | bytes accessed | tf_op | source)
XLA Modules:
  0.0 123.7 jit_solution(7220166924223480064)
XLA Ops:
  0.6 0.0 copy-start
  0.7 0.0 copy-start.5
  0.7 1.1 copy.169
  1.7 0.0 copy-done.5
  1.8 0.1 multiply_exponential_fusion.1
  1.8 0.0 copy-done
  1.8 1.0 fusion.25
  2.8 17.2 %all-to-all-start = ((f32[64,8,128]{2,1,0:T(8,128)}), f32[64,8,128]{2,1,0:T(8,128)S(1)}, u32[]{:S(2)}, u32[]{:S(2)}) async-start(f32[64,8,128]{2,1,0:T(8,128)} %bitcast.5), calls=%async_computation | async-start | bytes 524288 | tf_op jit(solution)/shard_map/all_to_all | solution.py:15
  20.1 0.6 dynamic_slice.4
  21.3 11.8 %all-to-all-done = f32[64,8,128]{2,1,0:T(8,128)S(1)} async-done(((f32[64,8,128]{2,1,0:T(8,128)}), f32[64,8,128]{2,1,0:T(8,128)S(1)}, u32[]{:S(2)}, u32[]{:S(2)}) %all-to-all-start) | async-done | bytes 262176 | tf_op jit(solution)/shard_map/all_to_all | solution.py:15
  33.2 0.4 fusion.20
  33.6 0.9 copy.175
  34.4 5.2 %all-to-all-start.1 = ((f32[64,8,128]{2,1,0:T(8,128)}), f32[64,8,128]{2,1,0:T(8,128)S(1)}, u32[]{:S(2)}, u32[]{:S(2)}) async-start(f32[64,8,128]{2,1,0:T(8,128)} %copy.175), calls=%async_computation.1 | async-start | bytes 524288 | tf_op jit(solution)/shard_map/all_to_all | solution.py:15
  39.7 0.1 copy.168
  39.8 0.2 fusion.12
  40.1 0.2 convolution_bitcast_fusion.7
  40.3 12.5 %all-to-all-done.1 = f32[64,8,128]{2,1,0:T(8,128)S(1)} async-done(((f32[64,8,128]{2,1,0:T(8,128)}), f32[64,8,128]{2,1,0:T(8,128)S(1)}, u32[]{:S(2)}, u32[]{:S(2)}) %all-to-all-start.1) | async-done | bytes 262176 | tf_op jit(solution)/shard_map/all_to_all | solution.py:15
  52.8 0.4 multiply_reduce_fusion.2
  53.3 0.0 copy-start.2
  53.3 0.0 copy-start.4
  53.3 0.1 copy.178
  53.4 0.7 copy-done.1
  54.2 0.1 copy-done.2
  54.2 0.2 multiply_reduce_fusion.1
  54.4 22.1 %all_to_all.25 = f32[16,2,128]{2,1,0:T(2,128)S(1)} all-to-all(f32[16,2,128]{2,1,0:T(2,128)S(1)} %broadcast_in_dim.29), channel_id=1, replica_groups=mesh['ctx'=64,'head'=16] {'head'}, dimensions={0} | all-to-all | bytes 32768 | tf_op jit(solution)/shard_map/all_to_all | solution.py:15
  76.5 0.9 multiply_convert_fusion
  77.4 0.1 copy.207
  77.5 0.4 fusion.22
  77.9 0.1 copy.185
  78.0 1.0 copy.186
  79.1 5.1 %all-to-all-start.3 = ((f32[64,9,1,128]{3,2,1,0:T(1,128)}), f32[64,9,1,128]{3,2,1,0:T(1,128)S(1)}, u32[]{:S(2)}, u32[]{:S(2)}) async-start(f32[64,9,1,128]{3,2,1,0:T(1,128)} %copy.186), calls=%async_computation.3 | async-start | bytes 589824 | tf_op jit(solution)/shard_map/all_to_all | solution.py:15
  84.1 0.2 fusion.13
  84.4 0.2 convolution_bitcast_fusion.6
  84.6 15.1 %all-to-all-done.3 = f32[64,9,1,128]{3,2,1,0:T(1,128)S(1)} async-done(((f32[64,9,1,128]{3,2,1,0:T(1,128)}), f32[64,9,1,128]{3,2,1,0:T(1,128)S(1)}, u32[]{:S(2)}, u32[]{:S(2)}) %all-to-all-start.3) | async-done | bytes 294944 | tf_op jit(solution)/shard_map/all_to_all | solution.py:15
  99.7 0.4 fusion.18
  100.2 1.0 copy.188
  101.2 5.1 %all-to-all-start.4 = ((f32[64,9,1,128]{3,2,1,0:T(1,128)}), f32[64,9,1,128]{3,2,1,0:T(1,128)S(1)}, u32[]{:S(2)}, u32[]{:S(2)}) async-start(f32[64,9,1,128]{3,2,1,0:T(1,128)} %copy.188), calls=%async_computation.4 | async-start | bytes 589824 | tf_op jit(solution)/shard_map/all_to_all | solution.py:15
  106.2 0.3 fusion.16
  106.5 0.8 copy.195
  107.3 0.2 convolution_bitcast_fusion.4
  107.5 0.2 convolution_bitcast_fusion.5
  107.6 12.9 %all-to-all-done.4 = f32[64,9,1,128]{3,2,1,0:T(1,128)S(1)} async-done(((f32[64,9,1,128]{3,2,1,0:T(1,128)}), f32[64,9,1,128]{3,2,1,0:T(1,128)S(1)}, u32[]{:S(2)}, u32[]{:S(2)}) %all-to-all-start.4) | async-done | bytes 294944 | tf_op jit(solution)/shard_map/all_to_all | solution.py:15
  120.6 0.6 slice_bitcast_fusion
  121.2 0.2 copy.190
  121.3 0.4 fusion.15
  121.7 0.8 copy.196
  122.5 0.4 fusion.14
  122.9 0.8 copy.197
  (20 shorter events, 0.3 us)
Async XLA Ops:
  0.6 1.2 copy-start
  0.7 1.1 copy-start.5
  2.8 30.4 %all-to-all-start = ((f32[64,8,128]{2,1,0:T(8,128)}), f32[64,8,128]{2,1,0:T(8,128)S(1)}, u32[]{:S(2)}, u32[]{:S(2)}) async-start(f32[64,8,128]{2,1,0:T(8,128)} %bitcast.5), calls=%async_computation | async-start | bytes 524288 | tf_op jit(solution)/shard_map/all_to_all | solution.py:15
  34.4 5.3 %copy-start.3 = (bf16[128,512]{1,0:T(8,128)(2,1)S(1)}, bf16[128,512]{1,0:T(8,128)(2,1)}, u32[]{:S(2)}) copy-start(bf16[128,512]{1,0:T(8,128)(2,1)} %param.7) | copy-start | bytes 393220
  34.4 18.4 %all-to-all-start.1 = ((f32[64,8,128]{2,1,0:T(8,128)}), f32[64,8,128]{2,1,0:T(8,128)S(1)}, u32[]{:S(2)}, u32[]{:S(2)}) async-start(f32[64,8,128]{2,1,0:T(8,128)} %copy.175), calls=%async_computation.1 | async-start | bytes 524288 | tf_op jit(solution)/shard_map/all_to_all | solution.py:15
  53.2 0.9 copy-start.1
  53.3 1.0 copy-start.2
  53.3 1.0 copy-start.4
  79.1 20.6 %all-to-all-start.3 = ((f32[64,9,1,128]{3,2,1,0:T(1,128)}), f32[64,9,1,128]{3,2,1,0:T(1,128)S(1)}, u32[]{:S(2)}, u32[]{:S(2)}) async-start(f32[64,9,1,128]{3,2,1,0:T(1,128)} %copy.186), calls=%async_computation.3 | async-start | bytes 589824 | tf_op jit(solution)/shard_map/all_to_all | solution.py:15
  101.2 19.4 %all-to-all-start.4 = ((f32[64,9,1,128]{3,2,1,0:T(1,128)}), f32[64,9,1,128]{3,2,1,0:T(1,128)S(1)}, u32[]{:S(2)}, u32[]{:S(2)}) async-start(f32[64,9,1,128]{3,2,1,0:T(1,128)} %copy.188), calls=%async_computation.4 | async-start | bytes 589824 | tf_op jit(solution)/shard_map/all_to_all | solution.py:15

commit v2 on v1

v2 whole, which is shorter than its diff:
```python
import jax
import jax.numpy as jnp
from jax import lax
from jax.experimental import pallas as pl
from jax.experimental.pallas import tpu as pltpu
from jax.sharding import PartitionSpec as P

DH = 128
HD = 8192


rate_unit = 2.0 ** (-20)
norm_eps = 1e-06
wide = jnp.float32
half = jnp.bfloat16


def swap(array, axis):
    return lax.all_to_all(array, axis, 0, 0)


def halves(array, axis):
    high = array.astype(half)
    low = (array - high.astype(wide)).astype(half)
    return jnp.concatenate([high, low], axis=axis)


def twice(array, axis):
    return jnp.concatenate([array, array], axis=axis)


def dot(left, right):
    return jnp.dot(left, right, preferred_element_type=wide)


def dot_nt(left, right):
    return lax.dot_general(left, right, (((1,), (1,)), ((), ())), preferred_element_type=wide)


def dot_tn(left, right):
    return lax.dot_general(left, right, (((0,), (0,)), ((), ())), preferred_element_type=wide)


def rate_of(ints_ref, head):
    return ints_ref[head].astype(wide) * rate_unit


def decay_column(rate, rows, late):
    place = lax.broadcasted_iota(jnp.int32, (rows, DH), 0).astype(wide)
    return jnp.exp(-rate * ((rows - 1.0 - place) if late else (place + 1.0)))


def decay_square(rate, rows):
    later = lax.broadcasted_iota(jnp.int32, (rows, rows), 0)
    sooner = lax.broadcasted_iota(jnp.int32, (rows, rows), 1)
    gap = (later - sooner).astype(wide)
    return jnp.where(gap >= 0.0, jnp.exp(-rate * jnp.maximum(gap, 0.0)), 0.0) * (1.0 / DH)


def cols(head):
    return slice(head * DH, (head + 1) * DH)


def summary_kernel(ints_ref, k_ref, v_ref, out_ref):
    rows, features = k_ref.shape
    for head in range(features // DH):
        late = decay_column(rate_of(ints_ref, head), rows, True)
        values = late * v_ref[:, cols(head)].astype(wide)
        keys = twice(k_ref[:, cols(head)].T, 1)
        out_ref[cols(head), :] = dot(keys, halves(values, 0))


def owned_span(ints_ref, chunk, rows):
    owner = lax.axis_index("ctx") * chunk // DH
    return jnp.exp(jnp.full((1, DH), -rate_of(ints_ref, owner) * rows, wide))


def forward_kernel(members, rows, ints_ref, in_ref, out_ref):
    chunk = in_ref.shape[0] // members
    span = owned_span(ints_ref, chunk, rows)
    state = jnp.zeros((chunk, DH), wide)
    for block in range(members):
        out_ref[block * chunk : (block + 1) * chunk, :] = state
        state = span * state + in_ref[block * chunk : (block + 1) * chunk, :]


def backward_kernel(members, rows, ints_ref, in_ref, out_ref):
    step = in_ref.shape[0] // members
    chunk = step - 1
    span = owned_span(ints_ref, chunk, rows)
    state = jnp.zeros((chunk, DH), wide)
    gains = [jnp.zeros((1, DH), wide)] * 4
    for block in reversed(range(members)):
        out_ref[block * step : block * step + chunk, :] = state
        state = span * state + in_ref[block * step : block * step + chunk, :]
        gains[block % 4] = gains[block % 4] + in_ref[block * step + chunk : (block + 1) * step, :]
    gain = (gains[0] + gains[1]) + (gains[2] + gains[3])
    for block in range(members):
        out_ref[block * step + chunk : (block + 1) * step, :] = gain


def local_kernel(ints_ref, q_ref, k_ref, v_ref, gate_ref, grad_ref, local_ref, weights_ref, gated_ref, qt_ref):
    rows, features = q_ref.shape
    for head in range(features // DH):
        at = cols(head)
        scores = dot_nt(q_ref[:, at], k_ref[:, at])
        weights = (scores * decay_square(rate_of(ints_ref, head), rows)).astype(half)
        weights_ref[:, at] = weights
        local_ref[:, at] = dot(weights, v_ref[:, at])
        qt_ref[at, :] = q_ref[:, at].T
        gated_ref[:, at] = grad_ref[:, at].astype(wide) * jax.nn.sigmoid(gate_ref[:, at].astype(wide))


def attend_kernel(ints_ref, q_ref, prefix_ref, local_ref, gated_ref, gain_ref, attention_ref, stats_ref):
    rows, features = q_ref.shape
    squares = jnp.zeros((rows, DH), wide)
    crossed = jnp.zeros((rows, DH), wide)
    for head in range(features // DH):
        at = cols(head)
        early = decay_column(rate_of(ints_ref, head), rows, False) * (1.0 / DH)
        carried = dot(twice(q_ref[:, at], 1), halves(prefix_ref[at, :], 0))
        attention = local_ref[:, at] + early * carried
        attention_ref[:, at] = attention
        squares = squares + attention * attention
        crossed = crossed + gated_ref[:, at] * gain_ref[:, at] * attention
    squares = jnp.sum(squares.T, axis=0, keepdims=True)
    crossed = jnp.sum(crossed.T, axis=0, keepdims=True)
    line = lax.broadcasted_iota(jnp.int32, (8, DH), 0)
    pair = jnp.where(line == 0, squares, jnp.where(line == 1, crossed, 0.0))
    for member in range(stats_ref.shape[0]):
        stats_ref[member] = pair


def token_scales(stats_ref):
    total = stats_ref[0]
    for member in range(1, stats_ref.shape[0]):
        total = total + stats_ref[member]
    inverse = lax.rsqrt(total[0:1] * (1.0 / HD) + norm_eps)
    pull = inverse * inverse * inverse * total[1:2] * (1.0 / HD)
    line = lax.broadcasted_iota(jnp.int32, (8, DH), 0)
    columns = jnp.where(line == 0, inverse, jnp.where(line == 1, pull, 0.0)).T
    return columns[:, 0:1], columns[:, 1:2]


def ahead_kernel(members, ints_ref, stats_ref, attention_ref, gated_ref, gain_ref, qt_ref, grad_ref, out_ref):
    rows, features = attention_ref.shape
    heads = features // DH
    step = out_ref.shape[0] // members
    chunk = step - 1
    inverse, pull = token_scales(stats_ref)
    for head in range(heads):
        at = cols(head)
        early = decay_column(rate_of(ints_ref, head), rows, False)
        gated = gated_ref[:, at]
        attention = attention_ref[:, at]
        grad = (inverse * (gated * gain_ref[:, at]) - pull * attention).astype(half)
        grad_ref[:, at] = grad
        ahead = dot(twice(qt_ref[at, :], 1), halves(early * grad.astype(wide), 0))
        for piece in range(DH // chunk):
            block = head * (DH // chunk) + piece
            out_ref[block * step : block * step + chunk, :] = ahead[piece * chunk : (piece + 1) * chunk, :]
        gain_row = jnp.sum(gated * (attention * inverse), axis=0, keepdims=True)
        for block in range(head, members, heads):
            out_ref[block * step + chunk : (block + 1) * step, :] = gain_row


def early_grads_kernel(
    ints_ref, stats_ref, attention_ref, gated_ref, gain_ref, gate_ref, grad_ref, q_ref, k_ref, v_ref,
    weights_ref, prefix_ref, grad_q_ref, grad_gate_ref, local_k_ref, local_v_ref,
):
    rows, features = q_ref.shape
    inverse, _ = token_scales(stats_ref)
    for head in range(features // DH):
        at = cols(head)
        rate = rate_of(ints_ref, head)
        normed = attention_ref[:, at] * inverse
        rest = 1.0 - jax.nn.sigmoid(gate_ref[:, at].astype(wide))
        grad_gate_ref[:, at] = (gated_ref[:, at] * normed * gain_ref[:, at] * rest).astype(half)
        grad = grad_ref[:, at]
        grad_scores = (dot_nt(grad, v_ref[:, at]) * decay_square(rate, rows)).astype(half)
        early = decay_column(rate, rows, False) * (1.0 / DH)
        carried = dot_nt(twice(grad, 1), halves(prefix_ref[at, :], 1))
        grad_q_ref[:, at] = (dot(grad_scores, k_ref[:, at]) + early * carried).astype(half)
        local_k_ref[:, at] = dot_tn(grad_scores, q_ref[:, at])
        local_v_ref[:, at] = dot_tn(weights_ref[:, at], grad)


def final_kernel(members, ints_ref, back_ref, k_ref, v_ref, local_k_ref, local_v_ref, grad_k_ref, grad_v_ref, gain_ref):
    rows, features = k_ref.shape
    heads = features // DH
    step = back_ref.shape[0] // members
    chunk = step - 1
    pieces = DH // chunk
    for head in range(heads):
        at = cols(head)
        late = decay_column(rate_of(ints_ref, head), rows, True) * (1.0 / DH)
        suffix = jnp.concatenate(
            [
                back_ref[block * step : block * step + chunk, :]
                for block in range(head * pieces, (head + 1) * pieces)
            ],
            axis=0,
        )
        high = suffix.astype(half)
        low = (suffix - high.astype(wide)).astype(half)
        carried_k = dot_nt(twice(v_ref[:, at], 1), jnp.concatenate([high, low], axis=1))
        carried_v = dot(twice(k_ref[:, at], 1), jnp.concatenate([high, low], axis=0))
        grad_k_ref[:, at] = (local_k_ref[:, at] + late * carried_k).astype(half)
        grad_v_ref[:, at] = (local_v_ref[:, at] + late * carried_v).astype(half)
        gain_ref[:, at] = back_ref[head * step + chunk : (head + 1) * step, :]


def call(kernel, name, shapes, *operands, flops=0, bytes_moved=0):
    vmem = pl.BlockSpec(memory_space=pltpu.VMEM)
    in_specs = [pl.BlockSpec(memory_space=pltpu.SMEM)] + [vmem] * (len(operands) - 1)
    many = isinstance(shapes, (list, tuple))
    out_shape = [jax.ShapeDtypeStruct(*shape) for shape in shapes]
    results = pl.pallas_call(
        kernel,
        out_shape=out_shape,
        in_specs=in_specs,
        out_specs=[vmem] * len(out_shape),
        compiler_params=pltpu.CompilerParams(vmem_limit_bytes=24 * 1024 * 1024),
        cost_estimate=pl.CostEstimate(flops=flops, bytes_accessed=bytes_moved, transcendentals=0),
        name=name,
    )(*operands)
    return results if len(out_shape) > 1 else results[0]


def body(queries, key_rows, value_rows, gate_in, grad_out, decay_ints, norm_gain):
    rows, features = queries.shape
    heads = features // DH
    members = lax.axis_size("ctx")
    head_members = lax.axis_size("head")
    chunk = features // members
    step = chunk + 1
    gain = norm_gain.reshape(1, features)
    square = rows * features
    flat = ((features, DH), wide)
    long = ((members * step, DH), wide)

    def across(array, width):
        shape = (members, width, DH) if width % 8 == 0 else (members, width, 1, DH)
        return swap(array.reshape(shape), "ctx").reshape(members * width, DH)

    summary = call(summary_kernel, "summary", [flat], decay_ints, key_rows, value_rows)
    there = across(summary, chunk)
    local, weights, gated, queries_t = call(
        local_kernel,
        "local_attention",
        [((rows, features), wide), ((rows, features), half), ((rows, features), wide), ((features, rows), half)],
        decay_ints, queries, key_rows, value_rows, gate_in, grad_out,
        flops=8 * square * DH, bytes_moved=20 * square,
    )

    def forward(*refs):
        forward_kernel(members, rows, *refs)

    prefix = across(call(forward, "forward_scan", [flat], decay_ints, there), chunk)
    attention, stats = call(
        attend_kernel,
        "attend",
        [((rows, features), wide), ((head_members, 8, rows), wide)],
        decay_ints, queries, prefix, local, gated, gain,
    )
    stats = swap(stats, "head")

    def ahead(*refs):
        ahead_kernel(members, *refs)

    grad, message = call(
        ahead,
        "ahead",
        [((rows, features), half), long],
        decay_ints, stats, attention, gated, gain, queries_t,
    )
    there = across(message, step)
    grad_q, grad_gate, local_k, local_v = call(
        early_grads_kernel,
        "early_grads",
        [((rows, features), half), ((rows, features), half), ((rows, features), wide), ((rows, features), wide)],
        decay_ints, stats, attention, gated, gain, gate_in, grad, queries, key_rows, value_rows,
        weights, prefix,
        flops=20 * square * DH, bytes_moved=24 * square,
    )

    def backward(*refs):
        backward_kernel(members, rows, *refs)

    back = across(call(backward, "backward_scan", [long], decay_ints, there), step)

    def final(*refs):
        final_kernel(members, *refs)

    grad_k, grad_v, grad_gain = call(
        final,
        "final",
        [((rows, features), half), ((rows, features), half), ((1, features), wide)],
        decay_ints, back, key_rows, value_rows, local_k, local_v,
    )
    return grad_q, grad_k, grad_v, grad_gate, grad_gain.reshape(features)


def solution(mesh):
    placed = (
        P("ctx", "head"),
        P("ctx", "head"),
        P("ctx", "head"),
        P("ctx", "head"),
        P("ctx", "head"),
        P("head"),
        P("head"),
    )
    return jax.shard_map(
        body,
        mesh=mesh,
        in_specs=placed,
        out_specs=(
            P("ctx", "head"),
            P("ctx", "head"),
            P("ctx", "head"),
            P("ctx", "head"),
            P("head"),
        ),
        check_vma=False,
    )
```

time: 124 us -> 122 us (0.984)
  blocking collectives: 22.1 us -> 72.5 us
  waiting for transfers between devices: 52.4 us -> 24.1 us
  starting transfers between devices: 32.6 us -> 10.2 us
  Pallas kernels: 0 us -> 10.5 us
  local copies, waits for them, and re-layouts: 8.91 us -> 3.16 us
  matrix products: 4.86 us -> 0 us
  other arithmetic: 1.32 us -> 0 us
    all_to_all x1 -> x3, blocking collectives: 22.1 us -> 72.5 us  [swap(): return lax.all_to_all(array, axis, 0, 0)]
    all_to_all x4 -> x2, waiting for transfers between devices: 52.4 us -> 24.1 us  [swap(): return lax.all_to_all(array, axis, 0, 0)]
    all_to_all x4 -> x2, starting transfers between devices: 32.6 us -> 10.2 us  [swap(): return lax.all_to_all(array, axis, 0, 0)]
    pallas_call x0 -> x8, Pallas kernels: none -> 10.5 us  [call(): pl.pallas_call(kernel, out_shape=out_shape, in_specs=in_specs, out_specs=...]
    dot_general x14 -> x0, matrix products: 4.86 us -> none  [the longest x1 0.97 us: body(): jnp.einsum('shd,she->hde', late_decay[:, :, None] * k_heads.astype(jnp.fl...]
    broadcast_in_dim x5 -> x0, local copies, waits for them, and re-layouts: 2.04 us -> none  [the longest x1 1.01 us: body(): there = swap(message[:, :, None, :], 'ctx')[:, :, 0, :]]
    unnamed x17 -> x20, local copies, waits for them, and re-layouts: 4.33 us -> 3.16 us
  transfers between devices with their start and end apart: 4 -> 2, of which waited for: 4 -> 2; matrix products, arithmetic and copies ran while one was open for 2% -> 0% of each run, Pallas kernels for 0% -> 3%
where the time goes in v2:
time: 122 us; the launch traced here: 121 us
  blocking collectives  72.5 us (59%)
  waiting for transfers between devices  24.1 us (20%)
  Pallas kernels  10.5 us (9%)
  starting transfers between devices  10.2 us (8%)
  local copies, waits for them, and re-layouts  3.16 us (3%)
    all_to_all x3, blocking collectives, swap(): return lax.all_to_all(array, axis, 0, 0)  72.5 us
    all_to_all x2, waiting for transfers between devices, swap(): return lax.all_to_all(array, axis, 0, 0)  24.1 us
    pallas_call x8, Pallas kernels, call(): pl.pallas_call(kernel, out_shape=out_shape, in_specs=in_specs, out_specs=...  10.5 us
    all_to_all x2, starting transfers between devices, swap(): return lax.all_to_all(array, axis, 0, 0)  10.2 us
    unnamed x20, local copies, waits for them, and re-layouts  3.16 us
  transfers between devices with their start and end apart: 2, of which 2 were waited for; matrix products, arithmetic and copies ran while one was open for 0% of the time, Pallas kernels for 3%

profile of v2, /device:TPU:2, one launch (start us, length us, event | category | flops | bytes accessed | tf_op | source)
XLA Modules:
  0.0 121.2 jit_solution(7097399112657534373)
XLA Ops:
  0.6 0.0 copy-start
  0.6 0.9 copy-done
  1.5 0.0 copy-start.2
  1.5 0.9 copy-done.2
  2.4 0.0 copy-start.7
  2.4 0.7 copy-done.7
  3.1 0.8 summary.1
  3.9 29.6 %all_to_all.25 = f32[64,8,128]{2,1,0:T(8,128)S(1)} all-to-all(f32[64,8,128]{2,1,0:T(8,128)S(1)} %bitcast.15), channel_id=1, replica_groups=mesh['ctx'=64,'head'=16] {'ctx'}, dimensions={0} | all-to-all | bytes 524288 | tf_op jit(solution)/shard_map/all_to_all | solution.py:19
  33.5 0.0 copy-start.6
  33.5 0.0 copy-start.8
  33.5 1.4 %forward_scan.1 = f32[512,128]{1,0:T(8,128)} custom-call(s32[4]{0:T(128)S(1)} %copy-done.7, f32[512,128]{1,0:T(8,128)S(1)} %bitcast.14), custom_call_target="tpu_custom_call" | custom-call | tf_op jit(solution)/shard_map/forward_scan/pallas_call | solution.py:218
  34.9 0.0 copy-start.1
  34.9 0.0 copy-start.3
  34.9 0.0 copy-start.4
  34.9 0.0 copy-start.5
  34.9 5.2 %all-to-all-start.1 = ((f32[64,8,128]{2,1,0:T(8,128)}), f32[64,8,128]{2,1,0:T(8,128)S(1)}, u32[]{:S(2)}, u32[]{:S(2)}) async-start(f32[64,8,128]{2,1,0:T(8,128)} %bitcast.2), calls=%async_computation.1 | async-start | bytes 524288 | tf_op jit(solution)/shard_map/all_to_all | solution.py:19
  40.1 0.0 copy-done.6
  40.1 0.0 copy-done.8
  40.1 0.0 copy-done.1
  40.1 0.0 copy-done.3
  40.2 0.0 copy-done.4
  40.2 0.0 copy-done.5
  40.2 1.3 %local_attention.1 = (f32[128,512]{1,0:T(8,128)S(1)}, bf16[128,512]{1,0:T(8,128)(2,1)S(1)}, f32[128,512]{1,0:T(8,128)S(1)}, bf16[512,128]{1,0:T(8,128)(2,1)S(1)}) custom-call(s32[4]{0:T(128)S(1)} %copy-done.8, bf16[128,512]{1,0:T(8,128)(2,1)S(1)} %copy-done.4, bf16[128,512]{1,0:T(8,128)(2,1)S(1)} %copy-done.1, bf16[128,512]{1,0:T(8,128)(2,1)S(1)} %copy-done.3, ...), custom_call_target="tpu_custom_call" | custom-call | flops 67108864 | bytes 1310720 | tf_op jit(solution)/shard_map/local_attention/pallas_call | solution.py:218
  41.5 11.8 %all-to-all-done.1 = f32[64,8,128]{2,1,0:T(8,128)S(1)} async-done(((f32[64,8,128]{2,1,0:T(8,128)}), f32[64,8,128]{2,1,0:T(8,128)S(1)}, u32[]{:S(2)}, u32[]{:S(2)}) %all-to-all-start.1) | async-done | bytes 262176 | tf_op jit(solution)/shard_map/all_to_all | solution.py:19
  53.2 0.0 copy-start.9
  53.2 0.7 copy-done.9
  53.9 0.8 attend.1
  54.8 23.0 %all_to_all.26.refs_1_.stats_ref = f32[16,8,128]{2,1,0:T(8,128)S(1)} all-to-all(f32[16,8,128]{2,1,0:T(8,128)S(1)} %get-tuple-element.22), channel_id=1, replica_groups=mesh['ctx'=64,'head'=16] {'head'}, dimensions={0} | all-to-all | bytes 131072 | tf_op jit(solution)/shard_map/all_to_all | solution.py:19
  77.8 1.0 ahead.1
  78.8 19.9 %all_to_all.27 = f32[64,9,1,128]{3,2,1,0:T(1,128)S(1)} all-to-all(f32[64,9,1,128]{3,2,1,0:T(1,128)S(1)} %bitcast.16), channel_id=1, replica_groups=mesh['ctx'=64,'head'=16] {'ctx'}, dimensions={0} | all-to-all | bytes 589824 | tf_op jit(solution)/shard_map/all_to_all | solution.py:19
  98.7 1.4 %backward_scan.1 = f32[576,128]{1,0:T(8,128)} custom-call(s32[4]{0:T(128)S(1)} %copy-done.8, f32[576,128]{1,0:T(8,128)S(1)} %bitcast.12), custom_call_target="tpu_custom_call" | custom-call | tf_op jit(solution)/shard_map/backward_scan/pallas_call | solution.py:218
  100.1 5.0 %all-to-all-start.4 = ((f32[64,9,1,128]{3,2,1,0:T(1,128)}), f32[64,9,1,128]{3,2,1,0:T(1,128)S(1)}, u32[]{:S(2)}, u32[]{:S(2)}) async-start(f32[64,9,1,128]{3,2,1,0:T(1,128)} %bitcast.7), calls=%async_computation.4 | async-start | bytes 589824 | tf_op jit(solution)/shard_map/all_to_all | solution.py:19
  105.1 2.2 %early_grads.1 = (bf16[128,512]{1,0:T(8,128)(2,1)}, bf16[128,512]{1,0:T(8,128)(2,1)}, f32[128,512]{1,0:T(8,128)S(1)}, f32[128,512]{1,0:T(8,128)S(1)}) custom-call(s32[4]{0:T(128)S(1)} %copy-done.8, f32[16,8,128]{2,1,0:T(8,128)S(1)} %all_to_all.26.refs_1_.stats_ref, f32[128,512]{1,0:T(8,128)S(1)} %get-tuple-element.23.refs_2_.attention_ref, ...), custom_call_target="tpu_custom_call" | custom-call | flops 167772160 | bytes 1572864 | tf_op jit(solution)/shard_map/early_grads/pallas_call | solution.py:218
  107.4 12.3 %all-to-all-done.4 = f32[64,9,1,128]{3,2,1,0:T(1,128)S(1)} async-done(((f32[64,9,1,128]{3,2,1,0:T(1,128)}), f32[64,9,1,128]{3,2,1,0:T(1,128)S(1)}, u32[]{:S(2)}, u32[]{:S(2)}) %all-to-all-start.4) | async-done | bytes 294944 | tf_op jit(solution)/shard_map/all_to_all | solution.py:19
  119.7 1.5 %final.1 = (bf16[128,512]{1,0:T(8,128)(2,1)}, bf16[128,512]{1,0:T(8,128)(2,1)}, f32[1,512]{1,0:T(1,128)}) custom-call(s32[4]{0:T(128)S(1)} %copy-done.8, f32[576,128]{1,0:T(8,128)S(1)} %bitcast.13, bf16[128,512]{1,0:T(8,128)(2,1)S(1)} %copy-done.1, bf16[128,512]{1,0:T(8,128)(2,1)S(1)} %copy-done.3, f32[128,512]{1,0:T(8,128)S(1)} %get-tuple-element.29.refs_4_, ...), custom_call_target="tpu_custom_call" | custom-call | tf_op jit(solution)/shard_map/final/pallas_call | solution.py:218
Async XLA Ops:
  0.6 0.9 copy-start
  1.5 0.9 copy-start.2
  2.4 0.7 copy-start.7
  33.5 6.6 %copy-start.6 = (bf16[128,512]{1,0:T(8,128)(2,1)S(1)}, bf16[128,512]{1,0:T(8,128)(2,1)}, u32[]{:S(2)}) copy-start(bf16[128,512]{1,0:T(8,128)(2,1)} %grad_ref.1) | copy-start | bytes 393220
  33.5 6.6 %copy-start.8 = (s32[4]{0:T(128)S(1)}, s32[4]{0:T(128)}, u32[]{:S(2)}) copy-start(s32[4]{0:T(128)} %refs_0_.7) | copy-start | bytes 52
  34.9 5.2 %copy-start.1 = (bf16[128,512]{1,0:T(8,128)(2,1)S(1)}, bf16[128,512]{1,0:T(8,128)(2,1)}, u32[]{:S(2)}) copy-start(bf16[128,512]{1,0:T(8,128)(2,1)} %refs_2_.1) | copy-start | bytes 393220
  34.9 5.3 %copy-start.3 = (bf16[128,512]{1,0:T(8,128)(2,1)S(1)}, bf16[128,512]{1,0:T(8,128)(2,1)}, u32[]{:S(2)}) copy-start(bf16[128,512]{1,0:T(8,128)(2,1)} %refs_3_.1) | copy-start | bytes 393220
  34.9 5.3 %copy-start.4 = (bf16[128,512]{1,0:T(8,128)(2,1)S(1)}, bf16[128,512]{1,0:T(8,128)(2,1)}, u32[]{:S(2)}) copy-start(bf16[128,512]{1,0:T(8,128)(2,1)} %q_ref.5) | copy-start | bytes 393220
  34.9 5.3 %copy-start.5 = (bf16[128,512]{1,0:T(8,128)(2,1)S(1)}, bf16[128,512]{1,0:T(8,128)(2,1)}, u32[]{:S(2)}) copy-start(bf16[128,512]{1,0:T(8,128)(2,1)} %gate_ref.3) | copy-start | bytes 393220
  34.9 18.3 %all-to-all-start.1 = ((f32[64,8,128]{2,1,0:T(8,128)}), f32[64,8,128]{2,1,0:T(8,128)S(1)}, u32[]{:S(2)}, u32[]{:S(2)}) async-start(f32[64,8,128]{2,1,0:T(8,128)} %bitcast.2), calls=%async_computation.1 | async-start | bytes 524288 | tf_op jit(solution)/shard_map/all_to_all | solution.py:19
  53.2 0.7 copy-start.9
  100.1 19.6 %all-to-all-start.4 = ((f32[64,9,1,128]{3,2,1,0:T(1,128)}), f32[64,9,1,128]{3,2,1,0:T(1,128)S(1)}, u32[]{:S(2)}, u32[]{:S(2)}) async-start(f32[64,9,1,128]{3,2,1,0:T(1,128)} %bitcast.7), calls=%async_computation.4 | async-start | bytes 589824 | tf_op jit(solution)/shard_map/all_to_all | solution.py:19

commit v3 on v2

v3 whole, which is shorter than its diff:
```python
import functools

import jax
import jax.numpy as jnp
from jax import lax
from jax.experimental import pallas as pl
from jax.experimental.pallas import tpu as pltpu
from jax.sharding import PartitionSpec as P

DH = 128
HD = 8192


rate_unit = 2.0 ** (-20)
norm_eps = 1e-06
wide = jnp.float32
half = jnp.bfloat16


def swap(array, axis):
    return lax.all_to_all(array, axis, 0, 0)


def halves(array, axis):
    high = array.astype(half)
    low = (array - high.astype(wide)).astype(half)
    return jnp.concatenate([high, low], axis=axis)


def twice(array, axis):
    return jnp.concatenate([array, array], axis=axis)


def dot(left, right):
    return jnp.dot(left, right, preferred_element_type=wide)


def dot_nt(left, right):
    return lax.dot_general(left, right, (((1,), (1,)), ((), ())), preferred_element_type=wide)


def dot_tn(left, right):
    return lax.dot_general(left, right, (((0,), (0,)), ((), ())), preferred_element_type=wide)


def rate_of(ints_ref, head):
    return ints_ref[head].astype(wide) * rate_unit


def decay_column(rate, rows, late):
    place = lax.broadcasted_iota(jnp.int32, (rows, DH), 0).astype(wide)
    return jnp.exp(-rate * ((rows - 1.0 - place) if late else (place + 1.0)))


def decay_square(rate, rows):
    later = lax.broadcasted_iota(jnp.int32, (rows, rows), 0)
    sooner = lax.broadcasted_iota(jnp.int32, (rows, rows), 1)
    gap = (later - sooner).astype(wide)
    return jnp.where(gap >= 0.0, jnp.exp(-rate * jnp.maximum(gap, 0.0)), 0.0) * (1.0 / DH)


def cols(head):
    return slice(head * DH, (head + 1) * DH)


def summary_kernel(members, ints_ref, k_ref, v_ref, out_ref, spans_ref, ints, keys, values, arrived):
    rows, features = k_ref.shape
    heads = features // DH
    copies = [
        pltpu.make_async_copy(source, target, arrived.at[number])
        for number, (source, target) in enumerate(((ints_ref, ints), (k_ref, keys), (v_ref, values)))
    ]
    for copy in copies:
        copy.start()
    for copy in copies:
        copy.wait()
    for head in range(heads):
        late = decay_column(rate_of(ints, head), rows, True)
        weighted = late * values[:, cols(head)].astype(wide)
        out_ref[cols(head), :] = dot(twice(keys[:, cols(head)].T, 1), halves(weighted, 0))
    owned = lax.axis_index("ctx") * (features // members) // DH
    power = lax.broadcasted_iota(jnp.int32, (8, DH), 0).astype(wide) + 1.0
    spans_ref[0:8, :] = jnp.exp(-(rate_of(ints, owned) * rows) * power)
    for head in range(heads):
        spans_ref[8 + head : 9 + head, :] = jnp.full((1, DH), rate_of(ints, head), wide)


def scan_blocks(order, span, leap, take, put, zero):
    chains = [order[at : at + 8] for at in range(0, len(order), 8)]
    totals = []
    for chain in chains:
        state = take(chain[0])
        for block in chain[1:]:
            state = span * state + take(block)
        totals.append(state)
    starts = [zero]
    for total in totals[:-1]:
        starts.append(leap * starts[-1] + total)
    for chain, state in zip(chains, starts):
        for block in chain:
            put(block, state)
            state = span * state + take(block)


def forward_kernel(members, spans_ref, in_ref, out_ref):
    chunk = in_ref.shape[0] // members

    def take(block):
        return in_ref[block * chunk : (block + 1) * chunk, :]

    def put(block, state):
        out_ref[block * chunk : (block + 1) * chunk, :] = state

    order = list(range(members))
    scan_blocks(order, spans_ref[0:1, :], spans_ref[7:8, :], take, put, jnp.zeros((chunk, DH), wide))


def backward_kernel(members, spans_ref, in_ref, out_ref):
    step = in_ref.shape[0] // members
    chunk = step - 1

    def take(block):
        return in_ref[block * step : block * step + chunk, :]

    def put(block, state):
        out_ref[block * step : block * step + chunk, :] = state

    order = list(reversed(range(members)))
    scan_blocks(order, spans_ref[0:1, :], spans_ref[7:8, :], take, put, jnp.zeros((chunk, DH), wide))
    gains = [in_ref[block * step + chunk : (block + 1) * step, :] for block in range(members)]
    while len(gains) > 1:
        gains = [gains[at] + gains[at + 1] for at in range(0, len(gains), 2)]
    for block in range(members):
        out_ref[block * step + chunk : (block + 1) * step, :] = gains[0]


def local_kernel(
    spans_ref, q_ref, k_ref, v_ref, gate_ref, grad_ref, gain_ref,
    local_ref, weights_ref, gated_ref, scaled_ref, qt_ref, early_ref, late_ref,
):
    rows, features = q_ref.shape
    for head in range(features // DH):
        at = cols(head)
        rate = spans_ref[8 + head : 9 + head, :]
        scores = dot_nt(q_ref[:, at], k_ref[:, at])
        weights = (scores * decay_square(rate, rows)).astype(half)
        weights_ref[:, at] = weights
        local_ref[:, at] = dot(weights, v_ref[:, at])
        qt_ref[at, :] = q_ref[:, at].T
        gated = grad_ref[:, at].astype(wide) * jax.nn.sigmoid(gate_ref[:, at].astype(wide))
        gated_ref[:, at] = gated
        scaled_ref[:, at] = gated * gain_ref[:, at]
        early_ref[:, at] = decay_column(rate, rows, False)
        late_ref[:, at] = decay_column(rate, rows, True) * (1.0 / DH)


def attend_kernel(q_ref, prefix_ref, local_ref, scaled_ref, early_ref, attention_ref, stats_ref):
    rows, features = q_ref.shape
    squares = jnp.zeros((rows, DH), wide)
    crossed = jnp.zeros((rows, DH), wide)
    for head in range(features // DH):
        at = cols(head)
        carried = dot(twice(q_ref[:, at], 1), halves(prefix_ref[at, :], 0)) * (1.0 / DH)
        attention = local_ref[:, at] + early_ref[:, at] * carried
        attention_ref[:, at] = attention
        squares = squares + attention * attention
        crossed = crossed + scaled_ref[:, at] * attention
    squares = jnp.sum(squares.T, axis=0, keepdims=True)
    crossed = jnp.sum(crossed.T, axis=0, keepdims=True)
    line = lax.broadcasted_iota(jnp.int32, (8, DH), 0)
    pair = jnp.where(line == 0, squares, jnp.where(line == 1, crossed, 0.0))
    for member in range(stats_ref.shape[0]):
        stats_ref[member] = pair


def token_scales(stats_ref):
    total = stats_ref[0]
    for member in range(1, stats_ref.shape[0]):
        total = total + stats_ref[member]
    inverse = lax.rsqrt(total[0:1] * (1.0 / HD) + norm_eps)
    pull = inverse * inverse * inverse * total[1:2] * (1.0 / HD)
    line = lax.broadcasted_iota(jnp.int32, (8, DH), 0)
    columns = jnp.where(line == 0, inverse, jnp.where(line == 1, pull, 0.0)).T
    return columns[:, 0:1], columns[:, 1:2]


def ahead_kernel(
    members, stats_ref, attention_ref, gated_ref, scaled_ref, qt_ref, early_ref, grad_ref, out_ref
):
    rows, features = attention_ref.shape
    heads = features // DH
    step = out_ref.shape[0] // members
    chunk = step - 1
    inverse, pull = token_scales(stats_ref)
    for head in range(heads):
        at = cols(head)
        attention = attention_ref[:, at]
        grad = (inverse * scaled_ref[:, at] - pull * attention).astype(half)
        grad_ref[:, at] = grad
        ahead = dot(twice(qt_ref[at, :], 1), halves(early_ref[:, at] * grad.astype(wide), 0))
        for piece in range(DH // chunk):
            start = (head * (DH // chunk) + piece) * step
            out_ref[start : start + chunk, :] = ahead[piece * chunk : (piece + 1) * chunk, :]
        gain_row = jnp.sum(gated_ref[:, at] * (attention * inverse), axis=0, keepdims=True)
        for block in range(head, members, heads):
            out_ref[block * step + chunk : (block + 1) * step, :] = gain_row


def early_grads_kernel(
    spans_ref, stats_ref, attention_ref, scaled_ref, gate_ref, grad_ref, q_ref, k_ref, v_ref,
    weights_ref, prefix_ref, early_ref, grad_q_ref, grad_gate_ref, local_k_ref, local_v_ref,
):
    rows, features = q_ref.shape
    inverse, _ = token_scales(stats_ref)
    for head in range(features // DH):
        at = cols(head)
        normed = attention_ref[:, at] * inverse
        rest = 1.0 - jax.nn.sigmoid(gate_ref[:, at].astype(wide))
        grad_gate_ref[:, at] = (scaled_ref[:, at] * normed * rest).astype(half)
        grad = grad_ref[:, at]
        square = decay_square(spans_ref[8 + head : 9 + head, :], rows)
        grad_scores = (dot_nt(grad, v_ref[:, at]) * square).astype(half)
        carried = dot_nt(twice(grad, 1), halves(prefix_ref[at, :], 1)) * (1.0 / DH)
        grad_q = dot(grad_scores, k_ref[:, at]) + early_ref[:, at] * carried
        grad_q_ref[:, at] = grad_q.astype(half)
        local_k_ref[:, at] = dot_tn(grad_scores, q_ref[:, at])
        local_v_ref[:, at] = dot_tn(weights_ref[:, at], grad)


def final_kernel(
    members, back_ref, k_ref, v_ref, local_k_ref, local_v_ref, late_ref, grad_k_ref, grad_v_ref, gain_ref,
    keys, values, gain, left,
):
    rows, features = k_ref.shape
    heads = features // DH
    copies = []

    def send(source, target):
        copy = pltpu.make_async_copy(source, target, left.at[len(copies)])
        copy.start()
        copies.append(copy)

    step = back_ref.shape[0] // members
    chunk = step - 1
    pieces = DH // chunk
    for head in range(heads):
        gain[:, cols(head)] = back_ref[head * step + chunk : (head + 1) * step, :]
    send(gain, gain_ref)
    for head in range(heads):
        at = cols(head)
        late = late_ref[:, at]
        starts = [block * step for block in range(head * pieces, (head + 1) * pieces)]
        suffix = jnp.concatenate([back_ref[start : start + chunk, :] for start in starts], axis=0)
        high = suffix.astype(half)
        low = (suffix - high.astype(wide)).astype(half)
        carried_k = dot_nt(twice(v_ref[:, at], 1), jnp.concatenate([high, low], axis=1))
        carried_v = dot(twice(k_ref[:, at], 1), jnp.concatenate([high, low], axis=0))
        keys[:, at] = (local_k_ref[:, at] + late * carried_k).astype(half)
        send(keys.at[:, at], grad_k_ref.at[:, at])
        values[:, at] = (local_v_ref[:, at] + late * carried_v).astype(half)
        send(values.at[:, at], grad_v_ref.at[:, at])
    for copy in copies:
        copy.wait()


def call(kernel, name, shapes, *operands, place=pltpu.VMEM, out_place=pltpu.VMEM, scratch=(), flops=0, bytes_moved=0):
    out_shape = [jax.ShapeDtypeStruct(*shape) for shape in shapes]
    results = pl.pallas_call(
        kernel,
        out_shape=out_shape,
        in_specs=[pl.BlockSpec(memory_space=place)] * len(operands),
        out_specs=[pl.BlockSpec(memory_space=out_place)] * len(out_shape),
        scratch_shapes=list(scratch),
        compiler_params=pltpu.CompilerParams(vmem_limit_bytes=24 * 1024 * 1024),
        cost_estimate=pl.CostEstimate(flops=flops, bytes_accessed=bytes_moved, transcendentals=0),
        name=name,
    )(*operands)
    return results if len(out_shape) > 1 else results[0]


def body(queries, key_rows, value_rows, gate_in, grad_out, decay_ints, norm_gain):
    rows, features = queries.shape
    members = lax.axis_size("ctx")
    head_members = lax.axis_size("head")
    chunk = features // members
    step = chunk + 1
    area = rows * features
    flat = ((features, DH), wide)
    long = ((members * step, DH), wide)
    block_wide = ((rows, features), wide)
    block_half = ((rows, features), half)

    def across(array, width):
        shape = (members, width, DH) if width % 8 == 0 else (members, width, 1, DH)
        return swap(array.reshape(shape), "ctx").reshape(members * width, DH)

    def sized(kernel):
        return functools.partial(kernel, members)

    summary, spans = call(
        sized(summary_kernel),
        "summary",
        [flat, ((16, DH), wide)],
        *[pltpu.with_memory_space_constraint(a, pltpu.HBM) for a in (decay_ints, key_rows, value_rows)],
        place=pltpu.HBM,
        scratch=[
            pltpu.SMEM(decay_ints.shape, jnp.int32),
            pltpu.VMEM((rows, features), half),
            pltpu.VMEM((rows, features), half),
            pltpu.SemaphoreType.DMA((3,)),
        ],
    )
    there = across(summary, chunk)
    local, weights, gated, scaled, queries_t, early, late = call(
        local_kernel,
        "local_attention",
        [block_wide, block_half, block_wide, block_wide, ((features, rows), half), block_wide, block_wide],
        spans, queries, key_rows, value_rows, gate_in, grad_out, norm_gain.reshape(1, features),
        flops=8 * area * DH, bytes_moved=28 * area,
    )
    prefix = across(call(sized(forward_kernel), "forward_scan", [flat], spans, there), chunk)
    attention, stats = call(
        attend_kernel,
        "attend",
        [block_wide, ((head_members, 8, rows), wide)],
        queries, prefix, local, scaled, early,
    )
    stats = swap(stats, "head")
    grad, message = call(
        sized(ahead_kernel),
        "ahead",
        [block_half, long],
        stats, attention, gated, scaled, queries_t, early,
    )
    there = across(message, step)
    grad_q, grad_gate, local_k, local_v = call(
        early_grads_kernel,
        "early_grads",
        [block_half, block_half, block_wide, block_wide],
        spans, stats, attention, scaled, gate_in, grad, queries, key_rows, value_rows,
        weights, prefix, early,
        flops=20 * area * DH, bytes_moved=28 * area,
    )
    back = across(call(sized(backward_kernel), "backward_scan", [long], spans, there), step)
    grad_k, grad_v, grad_gain = call(
        sized(final_kernel),
        "final",
        [block_half, block_half, ((1, features), wide)],
        back, key_rows, value_rows, local_k, local_v, late,
        out_place=pltpu.HBM,
        scratch=[
            pltpu.VMEM((rows, features), half),
            pltpu.VMEM((rows, features), half),
            pltpu.VMEM((1, features), wide),
            pltpu.SemaphoreType.DMA((2 * features // DH + 1,)),
        ],
    )
    return grad_q, grad_k, grad_v, grad_gate, grad_gain.reshape(features)


def solution(mesh):
    placed = (
        P("ctx", "head"),
        P("ctx", "head"),
        P("ctx", "head"),
        P("ctx", "head"),
        P("ctx", "head"),
        P("head"),
        P("head"),
    )
    return jax.shard_map(
        body,
        mesh=mesh,
        in_specs=placed,
        out_specs=(
            P("ctx", "head"),
            P("ctx", "head"),
            P("ctx", "head"),
            P("ctx", "head"),
            P("head"),
        ),
        check_vma=False,
    )
```

time: 122 us -> 116 us (0.951)
  Pallas kernels: 10.5 us -> 6.94 us
  local copies, waits for them, and re-layouts: 3.16 us -> 0.02 us
    pallas_call x8, Pallas kernels: 10.5 us -> 6.94 us  [call(): pl.pallas_call(kernel, out_shape=out_shape, in_specs=[pl.BlockSpec(memory...]
    unnamed x20 -> x12, local copies, waits for them, and re-layouts: 3.16 us -> 0.02 us
  transfers between devices with their start and end apart: 2 -> 2, of which waited for: 2 -> 2; matrix products, arithmetic and copies ran while one was open for 0% -> 0% of each run, Pallas kernels for 3% -> 2%
where the time goes in v3:
time: 116 us
  blocking collectives  72.5 us (62%)
  waiting for transfers between devices  25.1 us (22%)
  starting transfers between devices  10.3 us (9%)
  Pallas kernels  6.94 us (6%)
    all_to_all x3, blocking collectives, swap(): return lax.all_to_all(array, axis, 0, 0)  72.5 us
    all_to_all x2, waiting for transfers between devices, swap(): return lax.all_to_all(array, axis, 0, 0)  25.1 us
    all_to_all x2, starting transfers between devices, swap(): return lax.all_to_all(array, axis, 0, 0)  10.3 us
    pallas_call x8, Pallas kernels, call(): pl.pallas_call(kernel, out_shape=out_shape, in_specs=[pl.BlockSpec(memory...  6.94 us
  transfers between devices with their start and end apart: 2, of which 2 were waited for; matrix products, arithmetic and copies ran while one was open for 0% of the time, Pallas kernels for 2%

profile of v3, /device:TPU:2, one launch (start us, length us, event | category | flops | bytes accessed | tf_op | source)
XLA Modules:
  0.0 115.6 jit_solution(15801694381578818670)
XLA Ops:
  0.6 1.3 %summary.1 = (f32[512,128]{1,0:T(8,128)S(1)}, f32[16,128]{1,0:T(8,128)S(1)}) custom-call(s32[4]{0:T(128)} %ints_ref.1, bf16[128,512]{1,0:T(8,128)(2,1)} %k_ref.7, bf16[128,512]{1,0:T(8,128)(2,1)} %v_ref.7), custom_call_target="tpu_custom_call" | custom-call | tf_op jit(solution)/shard_map/summary/pallas_call | solution.py:268
  1.9 29.6 %all_to_all.25 = f32[64,8,128]{2,1,0:T(8,128)S(1)} all-to-all(f32[64,8,128]{2,1,0:T(8,128)S(1)} %bitcast.16), channel_id=1, replica_groups=mesh['ctx'=64,'head'=16] {'ctx'}, dimensions={0} | all-to-all | bytes 524288 | tf_op jit(solution)/shard_map/all_to_all | solution.py:21
  31.5 0.0 copy-start.4
  31.5 0.0 copy-start.5
  31.5 0.7 forward_scan.1
  32.2 0.0 copy-start
  32.2 0.0 copy-start.1
  32.2 0.0 copy-start.2
  32.2 0.0 copy-start.3
  32.2 5.2 %all-to-all-start.1 = ((f32[64,8,128]{2,1,0:T(8,128)}), f32[64,8,128]{2,1,0:T(8,128)S(1)}, u32[]{:S(2)}, u32[]{:S(2)}) async-start(f32[64,8,128]{2,1,0:T(8,128)} %bitcast.2), calls=%async_computation.1 | async-start | bytes 524288 | tf_op jit(solution)/shard_map/all_to_all | solution.py:21
  37.4 0.0 copy-done.4
  37.4 0.0 copy-done.5
  37.4 0.0 copy-done
  37.5 0.0 copy-done.1
  37.5 0.0 copy-done.2
  37.5 0.0 copy-done.3
  37.5 0.7 local_attention.1
  38.2 12.3 %all-to-all-done.1 = f32[64,8,128]{2,1,0:T(8,128)S(1)} async-done(((f32[64,8,128]{2,1,0:T(8,128)}), f32[64,8,128]{2,1,0:T(8,128)S(1)}, u32[]{:S(2)}, u32[]{:S(2)}) %all-to-all-start.1) | async-done | bytes 262176 | tf_op jit(solution)/shard_map/all_to_all | solution.py:21
  50.6 0.3 attend.1
  50.9 23.0 %all_to_all.26.stats_ref = f32[16,8,128]{2,1,0:T(8,128)S(1)} all-to-all(f32[16,8,128]{2,1,0:T(8,128)S(1)} %get-tuple-element.30), channel_id=1, replica_groups=mesh['ctx'=64,'head'=16] {'head'}, dimensions={0} | all-to-all | bytes 131072 | tf_op jit(solution)/shard_map/all_to_all | solution.py:21
  73.9 0.5 ahead.1
  74.3 20.0 %all_to_all.27 = f32[64,9,1,128]{3,2,1,0:T(1,128)S(1)} all-to-all(f32[64,9,1,128]{3,2,1,0:T(1,128)S(1)} %bitcast.15), channel_id=1, replica_groups=mesh['ctx'=64,'head'=16] {'ctx'}, dimensions={0} | all-to-all | bytes 589824 | tf_op jit(solution)/shard_map/all_to_all | solution.py:21
  94.3 0.8 backward_scan.1
  95.1 5.1 %all-to-all-start.4 = ((f32[64,9,1,128]{3,2,1,0:T(1,128)}), f32[64,9,1,128]{3,2,1,0:T(1,128)S(1)}, u32[]{:S(2)}, u32[]{:S(2)}) async-start(f32[64,9,1,128]{3,2,1,0:T(1,128)} %bitcast.7), calls=%async_computation.4 | async-start | bytes 589824 | tf_op jit(solution)/shard_map/all_to_all | solution.py:21
  100.2 1.7 %early_grads.1 = (bf16[128,512]{1,0:T(8,128)(2,1)}, bf16[128,512]{1,0:T(8,128)(2,1)}, f32[128,512]{1,0:T(8,128)S(1)}, f32[128,512]{1,0:T(8,128)S(1)}) custom-call(f32[16,128]{1,0:T(8,128)S(1)} %get-tuple-element.25.spans_ref, f32[16,8,128]{2,1,0:T(8,128)S(1)} %all_to_all.26.stats_ref, f32[128,512]{1,0:T(8,128)S(1)} %get-tuple-element.31.attention_ref, ...), custom_call_target="tpu_custom_call" | custom-call | flops 167772160 | bytes 1835008 | tf_op jit(solution)/shard_map/early_grads/pallas_call | solution.py:268
  101.9 12.7 %all-to-all-done.4 = f32[64,9,1,128]{3,2,1,0:T(1,128)S(1)} async-done(((f32[64,9,1,128]{3,2,1,0:T(1,128)}), f32[64,9,1,128]{3,2,1,0:T(1,128)S(1)}, u32[]{:S(2)}, u32[]{:S(2)}) %all-to-all-start.4) | async-done | bytes 294944 | tf_op jit(solution)/shard_map/all_to_all | solution.py:21
  114.6 1.0 final.1
Async XLA Ops:
  31.5 6.0 %copy-start.4 = (bf16[128,512]{1,0:T(8,128)(2,1)S(1)}, bf16[128,512]{1,0:T(8,128)(2,1)}, u32[]{:S(2)}) copy-start(bf16[128,512]{1,0:T(8,128)(2,1)} %grad_ref.1) | copy-start | bytes 393220
  31.5 6.0 %copy-start.5 = (f32[512]{0:T(512)S(1)}, f32[512]{0:T(512)}, u32[]{:S(2)}) copy-start(f32[512]{0:T(512)} %param.13) | copy-start | bytes 6148
  32.2 5.2 %copy-start = (bf16[128,512]{1,0:T(8,128)(2,1)S(1)}, bf16[128,512]{1,0:T(8,128)(2,1)}, u32[]{:S(2)}) copy-start(bf16[128,512]{1,0:T(8,128)(2,1)} %k_ref.7) | copy-start | bytes 393220
  32.2 5.2 %copy-start.1 = (bf16[128,512]{1,0:T(8,128)(2,1)S(1)}, bf16[128,512]{1,0:T(8,128)(2,1)}, u32[]{:S(2)}) copy-start(bf16[128,512]{1,0:T(8,128)(2,1)} %v_ref.7) | copy-start | bytes 393220
  32.2 5.3 %copy-start.2 = (bf16[128,512]{1,0:T(8,128)(2,1)S(1)}, bf16[128,512]{1,0:T(8,128)(2,1)}, u32[]{:S(2)}) copy-start(bf16[128,512]{1,0:T(8,128)(2,1)} %q_ref.5) | copy-start | bytes 393220
  32.2 5.3 %copy-start.3 = (bf16[128,512]{1,0:T(8,128)(2,1)S(1)}, bf16[128,512]{1,0:T(8,128)(2,1)}, u32[]{:S(2)}) copy-start(bf16[128,512]{1,0:T(8,128)(2,1)} %gate_ref.3) | copy-start | bytes 393220
  32.2 18.3 %all-to-all-start.1 = ((f32[64,8,128]{2,1,0:T(8,128)}), f32[64,8,128]{2,1,0:T(8,128)S(1)}, u32[]{:S(2)}, u32[]{:S(2)}) async-start(f32[64,8,128]{2,1,0:T(8,128)} %bitcast.2), calls=%async_computation.1 | async-start | bytes 524288 | tf_op jit(solution)/shard_map/all_to_all | solution.py:21
  95.1 19.5 %all-to-all-start.4 = ((f32[64,9,1,128]{3,2,1,0:T(1,128)}), f32[64,9,1,128]{3,2,1,0:T(1,128)S(1)}, u32[]{:S(2)}, u32[]{:S(2)}) async-start(f32[64,9,1,128]{3,2,1,0:T(1,128)} %bitcast.7), calls=%async_computation.4 | async-start | bytes 589824 | tf_op jit(solution)/shard_map/all_to_all | solution.py:21

commit v4 on v3

--- a/solution.py
+++ b/solution.py
@@ -13,12 +13,13 @@
 
 rate_unit = 2.0 ** (-20)
 norm_eps = 1e-06
+SIDE = 8
 wide = jnp.float32
 half = jnp.bfloat16
 
 
-def swap(array, axis):
-    return lax.all_to_all(array, axis, 0, 0)
+def swap(array, axis, groups=None):
+    return lax.all_to_all(array, axis, 0, 0, axis_index_groups=groups)
 
 
 def halves(array, axis):
@@ -78,11 +79,65 @@
         late = decay_column(rate_of(ints, head), rows, True)
         weighted = late * values[:, cols(head)].astype(wide)
         out_ref[cols(head), :] = dot(twice(keys[:, cols(head)].T, 1), halves(weighted, 0))
-    owned = lax.axis_index("ctx") * (features // members) // DH
-    power = lax.broadcasted_iota(jnp.int32, (8, DH), 0).astype(wide) + 1.0
-    spans_ref[0:8, :] = jnp.exp(-(rate_of(ints, owned) * rows) * power)
+    place = lax.axis_index("ctx")
+    line = lax.broadcasted_iota(jnp.int32, (8, DH), 0)
+    owned = place * (features // members) // DH
+    spans_ref[0:8, :] = jnp.exp(-(rate_of(ints, owned) * rows) * (line.astype(wide) + 1.0))
     for head in range(heads):
         spans_ref[8 + head : 9 + head, :] = jnp.full((1, DH), rate_of(ints, head), wide)
+    side = SIDE
+    across, down = place % side, place // side
+    owned = across * (features // side) // DH
+    span_rate = rate_of(ints, owned) * rows
+    spans_ref[16:24, :] = jnp.exp(jnp.full((8, DH), -span_rate, wide))
+    for at, gap in ((24, line - down - 1), (32, down - line - 1)):
+        power = jnp.maximum(gap, 0).astype(wide) * side
+        spans_ref[at : at + 8, :] = jnp.where(gap >= 0, jnp.exp(-span_rate * power), 0.0)
+
+
+def add_up(terms):
+    while len(terms) > 1:
+        pairs = [terms[at] + terms[at + 1] for at in range(0, len(terms) - 1, 2)]
+        terms = pairs + terms[2 * len(pairs) :]
+    return terms[0]
+
+
+def line_order(backward):
+    return list(reversed(range(SIDE))) if backward else list(range(SIDE))
+
+
+def line_total_kernel(backward, width, spans_ref, in_ref, out_ref):
+    step = in_ref.shape[0] // SIDE
+    span = spans_ref[16:17, :]
+    state = None
+    for block in line_order(backward):
+        term = in_ref[block * step : block * step + width, :]
+        state = term if state is None else span * state + term
+    for block in range(SIDE):
+        out_ref[block * step : block * step + width, :] = state
+    if step > width:
+        gain = add_up([in_ref[block * step + width : (block + 1) * step, :] for block in range(SIDE)])
+        for block in range(SIDE):
+            out_ref[block * step + width : (block + 1) * step, :] = gain
+
+
+def line_scan_kernel(backward, width, spans_ref, totals_ref, in_ref, out_ref):
+    step = in_ref.shape[0] // SIDE
+    span = spans_ref[16:17, :]
+    first = 24 if backward else 32
+    state = add_up(
+        [
+            spans_ref[first + block : first + block + 1, :] * totals_ref[block * step : block * step + width, :]
+            for block in range(SIDE)
+        ]
+    )
+    for block in line_order(backward):
+        out_ref[block * step : block * step + width, :] = state
+        state = span * state + in_ref[block * step : block * step + width, :]
+    if step > width:
+        gain = add_up([totals_ref[block * step + width : (block + 1) * step, :] for block in range(SIDE)])
+        for block in range(SIDE):
+            out_ref[block * step + width : (block + 1) * step, :] = gain
 
 
 def scan_blocks(order, span, leap, take, put, zero):
@@ -113,25 +168,6 @@
 
     order = list(range(members))
     scan_blocks(order, spans_ref[0:1, :], spans_ref[7:8, :], take, put, jnp.zeros((chunk, DH), wide))
-
-
-def backward_kernel(members, spans_ref, in_ref, out_ref):
-    step = in_ref.shape[0] // members
-    chunk = step - 1
-
-    def take(block):
-        return in_ref[block * step : block * step + chunk, :]
-
-    def put(block, state):
-        out_ref[block * step : block * step + chunk, :] = state
-
-    order = list(reversed(range(members)))
-    scan_blocks(order, spans_ref[0:1, :], spans_ref[7:8, :], take, put, jnp.zeros((chunk, DH), wide))
-    gains = [in_ref[block * step + chunk : (block + 1) * step, :] for block in range(members)]
-    while len(gains) > 1:
-        gains = [gains[at] + gains[at + 1] for at in range(0, len(gains), 2)]
-    for block in range(members):
-        out_ref[block * step + chunk : (block + 1) * step, :] = gains[0]
 
 
 def local_kernel(
@@ -185,12 +221,13 @@
 
 
 def ahead_kernel(
-    members, stats_ref, attention_ref, gated_ref, scaled_ref, qt_ref, early_ref, grad_ref, out_ref
+    stats_ref, attention_ref, gated_ref, scaled_ref, qt_ref, early_ref, grad_ref, out_ref
 ):
     rows, features = attention_ref.shape
     heads = features // DH
-    step = out_ref.shape[0] // members
-    chunk = step - 1
+    step = out_ref.shape[0] // SIDE
+    width = features // SIDE
+    pieces = DH // width
     inverse, pull = token_scales(stats_ref)
     for head in range(heads):
         at = cols(head)
@@ -198,12 +235,12 @@
         grad = (inverse * scaled_ref[:, at] - pull * attention).astype(half)
         grad_ref[:, at] = grad
         ahead = dot(twice(qt_ref[at, :], 1), halves(early_ref[:, at] * grad.astype(wide), 0))
-        for piece in range(DH // chunk):
-            start = (head * (DH // chunk) + piece) * step
-            out_ref[start : start + chunk, :] = ahead[piece * chunk : (piece + 1) * chunk, :]
+        for piece in range(pieces):
+            start = (head * pieces + piece) * step
+            out_ref[start : start + width, :] = ahead[piece * width : (piece + 1) * width, :]
         gain_row = jnp.sum(gated_ref[:, at] * (attention * inverse), axis=0, keepdims=True)
-        for block in range(head, members, heads):
-            out_ref[block * step + chunk : (block + 1) * step, :] = gain_row
+        for block in range(head, SIDE, heads):
+            out_ref[block * step + width : (block + 1) * step, :] = jnp.broadcast_to(gain_row, (step - width, DH))
 
 
 def early_grads_kernel(
@@ -228,7 +265,7 @@
 
 
 def final_kernel(
-    members, back_ref, k_ref, v_ref, local_k_ref, local_v_ref, late_ref, grad_k_ref, grad_v_ref, gain_ref,
+    back_ref, k_ref, v_ref, local_k_ref, local_v_ref, late_ref, grad_k_ref, grad_v_ref, gain_ref,
     keys, values, gain, left,
 ):
     rows, features = k_ref.shape
@@ -240,17 +277,17 @@
         copy.start()
         copies.append(copy)
 
-    step = back_ref.shape[0] // members
-    chunk = step - 1
-    pieces = DH // chunk
+    step = back_ref.shape[0] // SIDE
+    width = features // SIDE
+    pieces = DH // width
     for head in range(heads):
-        gain[:, cols(head)] = back_ref[head * step + chunk : (head + 1) * step, :]
+        gain[:, cols(head)] = back_ref[head * step + width : head * step + width + 1, :]
     send(gain, gain_ref)
     for head in range(heads):
         at = cols(head)
         late = late_ref[:, at]
         starts = [block * step for block in range(head * pieces, (head + 1) * pieces)]
-        suffix = jnp.concatenate([back_ref[start : start + chunk, :] for start in starts], axis=0)
+        suffix = jnp.concatenate([back_ref[start : start + width, :] for start in starts], axis=0)
         high = suffix.astype(half)
         low = (suffix - high.astype(wide)).astype(half)
         carried_k = dot_nt(twice(v_ref[:, at], 1), jnp.concatenate([high, low], axis=1))
@@ -283,16 +320,21 @@
     members = lax.axis_size("ctx")
     head_members = lax.axis_size("head")
     chunk = features // members
-    step = chunk + 1
+    width = features // SIDE
+    step = width + 8
+    lanes = [[down * SIDE + across for across in range(SIDE)] for down in range(SIDE)]
+    columns = [[down * SIDE + across for down in range(SIDE)] for across in range(SIDE)]
     area = rows * features
     flat = ((features, DH), wide)
-    long = ((members * step, DH), wide)
+    long = ((SIDE * step, DH), wide)
     block_wide = ((rows, features), wide)
     block_half = ((rows, features), half)
 
-    def across(array, width):
-        shape = (members, width, DH) if width % 8 == 0 else (members, width, 1, DH)
-        return swap(array.reshape(shape), "ctx").reshape(members * width, DH)
+    def everywhere(array):
+        return swap(array.reshape(members, -1, DH), "ctx").reshape(-1, DH)
+
+    def along(array, groups):
+        return swap(array.reshape(SIDE, -1, DH), "ctx", groups).reshape(-1, DH)
 
     def sized(kernel):
         return functools.partial(kernel, members)
@@ -300,7 +342,7 @@
     summary, spans = call(
         sized(summary_kernel),
         "summary",
-        [flat, ((16, DH), wide)],
+        [flat, ((40, DH), wide)],
         *[pltpu.with_memory_space_constraint(a, pltpu.HBM) for a in (decay_ints, key_rows, value_rows)],
         place=pltpu.HBM,
         scratch=[
@@ -310,7 +352,7 @@
             pltpu.SemaphoreType.DMA((3,)),
         ],
     )
-    there = across(summary, chunk)
+    there = everywhere(summary)
     local, weights, gated, scaled, queries_t, early, late = call(
         local_kernel,
         "local_attention",
@@ -318,7 +360,7 @@
         spans, queries, key_rows, value_rows, gate_in, grad_out, norm_gain.reshape(1, features),
         flops=8 * area * DH, bytes_moved=28 * area,
     )
-    prefix = across(call(sized(forward_kernel), "forward_scan", [flat], spans, there), chunk)
+    prefix = everywhere(call(sized(forward_kernel), "forward_scan", [flat], spans, there))
     attention, stats = call(
         attend_kernel,
         "attend",
@@ -327,12 +369,14 @@
     )
     stats = swap(stats, "head")
     grad, message = call(
-        sized(ahead_kernel),
+        ahead_kernel,
         "ahead",
         [block_half, long],
         stats, attention, gated, scaled, queries_t, early,
     )
-    there = across(message, step)
+    there = along(message, lanes)
+    total = call(functools.partial(line_total_kernel, True, width), "line_total", [long], spans, there)
+    totals = along(total, columns)
     grad_q, grad_gate, local_k, local_v = call(
         early_grads_kernel,
         "early_grads",
@@ -341,9 +385,10 @@
         weights, prefix, early,
         flops=20 * area * DH, bytes_moved=28 * area,
     )
-    back = across(call(sized(backward_kernel), "backward_scan", [long], spans, there), step)
+    scanned = call(functools.partial(line_scan_kernel, True, width), "line_scan", [long], spans, totals, there)
+    back = along(scanned, lanes)
     grad_k, grad_v, grad_gain = call(
-        sized(final_kernel),
+        final_kernel,
         "final",
         [block_half, block_half, ((1, features), wide)],
         back, key_rows, value_rows, local_k, local_v, late,

time: 116 us -> 121 us (1.043)
  blocking collectives: 72.5 us -> 82.9 us
  waiting for transfers between devices: 25.1 us -> 20 us
    all_to_all x3 -> x4, blocking collectives: 72.5 us -> 82.9 us  [swap(): return lax.all_to_all(array, axis, 0, 0, axis_index_groups=groups)]
    all_to_all x2, waiting for transfers between devices: 25.1 us -> 20 us  [swap(): return lax.all_to_all(array, axis, 0, 0, axis_index_groups=groups)]
    pallas_call x8 -> x9, Pallas kernels: 6.94 us -> 6.97 us  [call(): pl.pallas_call(kernel, out_shape=out_shape, in_specs=[pl.BlockSpec(memory...]
where the time goes in v4:
time: 121 us
  blocking collectives  82.9 us (69%)
  waiting for transfers between devices  20 us (17%)
  starting transfers between devices  9.98 us (8%)
  Pallas kernels  6.97 us (6%)
    all_to_all x4, blocking collectives, swap(): return lax.all_to_all(array, axis, 0, 0, axis_index_groups=groups)  82.9 us
    all_to_all x2, waiting for transfers between devices, swap(): return lax.all_to_all(array, axis, 0, 0, axis_index_groups=groups)  20 us
    all_to_all x2, starting transfers between devices, swap(): return lax.all_to_all(array, axis, 0, 0, axis_index_groups=groups)  9.98 us
    pallas_call x9, Pallas kernels, call(): pl.pallas_call(kernel, out_shape=out_shape, in_specs=[pl.BlockSpec(memory...  6.97 us
  transfers between devices with their start and end apart: 2, of which 2 were waited for; matrix products, arithmetic and copies ran while one was open for 0% of the time, Pallas kernels for 2%

profile of v4, /device:TPU:2, one launch (start us, length us, event | category | flops | bytes accessed | tf_op | source)
XLA Modules:
  0.0 120.6 jit_solution(3309306198250276716)
XLA Ops:
  0.6 1.3 %summary.1 = (f32[512,128]{1,0:T(8,128)S(1)}, f32[40,128]{1,0:T(8,128)S(1)}) custom-call(s32[4]{0:T(128)} %ints_ref.1, bf16[128,512]{1,0:T(8,128)(2,1)} %k_ref.7, bf16[128,512]{1,0:T(8,128)(2,1)} %v_ref.7), custom_call_target="tpu_custom_call" | custom-call | tf_op jit(solution)/shard_map/summary/pallas_call | solution.py:305
  1.9 29.6 %all_to_all.30 = f32[64,8,128]{2,1,0:T(8,128)S(1)} all-to-all(f32[64,8,128]{2,1,0:T(8,128)S(1)} %bitcast.21), channel_id=1, replica_groups=mesh['ctx'=64,'head'=16] {'ctx'}, dimensions={0} | all-to-all | bytes 524288 | tf_op jit(solution)/shard_map/all_to_all | solution.py:22
  31.5 0.0 copy-start.4
  31.5 0.0 copy-start.5
  31.5 0.7 forward_scan.1
  32.2 0.0 copy-start
  32.2 0.0 copy-start.1
  32.2 0.0 copy-start.2
  32.2 0.0 copy-start.3
  32.2 5.2 %all-to-all-start.1 = ((f32[64,8,128]{2,1,0:T(8,128)}), f32[64,8,128]{2,1,0:T(8,128)S(1)}, u32[]{:S(2)}, u32[]{:S(2)}) async-start(f32[64,8,128]{2,1,0:T(8,128)} %bitcast.2), calls=%async_computation.1 | async-start | bytes 524288 | tf_op jit(solution)/shard_map/all_to_all | solution.py:22
  37.4 0.0 copy-done.4
  37.4 0.0 copy-done.5
  37.5 0.0 copy-done
  37.5 0.0 copy-done.1
  37.5 0.0 copy-done.2
  37.5 0.0 copy-done.3
  37.5 0.7 local_attention.1
  38.2 12.3 %all-to-all-done.1 = f32[64,8,128]{2,1,0:T(8,128)S(1)} async-done(((f32[64,8,128]{2,1,0:T(8,128)}), f32[64,8,128]{2,1,0:T(8,128)S(1)}, u32[]{:S(2)}, u32[]{:S(2)}) %all-to-all-start.1) | async-done | bytes 262176 | tf_op jit(solution)/shard_map/all_to_all | solution.py:22
  50.6 0.3 attend.1
  50.9 23.0 %all_to_all.31.stats_ref = f32[16,8,128]{2,1,0:T(8,128)S(1)} all-to-all(f32[16,8,128]{2,1,0:T(8,128)S(1)} %get-tuple-element.30), channel_id=1, replica_groups=mesh['ctx'=64,'head'=16] {'head'}, dimensions={0} | all-to-all | bytes 131072 | tf_op jit(solution)/shard_map/all_to_all | solution.py:22
  73.9 0.5 ahead.1
  74.3 15.3 %all_to_all.32 = f32[8,72,128]{2,1,0:T(8,128)S(1)} all-to-all(f32[8,72,128]{2,1,0:T(8,128)S(1)} %bitcast.20), channel_id=1, replica_groups={{0,16,32,48,64,80,96,112},{128,144,160,176,192,208,224,240},{256,272,28..., dimensions={0} | all-to-all | bytes 589824 | tf_op jit(solution)/shard_map/all_to_all | solution.py:22
  89.7 15.0 %all_to_all.33 = f32[8,72,128]{2,1,0:T(8,128)S(1)} all-to-all(f32[8,72,128]{2,1,0:T(8,128)S(1)} %bitcast.17), channel_id=1, replica_groups={{0,128,256,384,512,640,768,896},{16,144,272,400,528,656,784,912},{32,16..., dimensions={0} | all-to-all | bytes 589824 | tf_op jit(solution)/shard_map/all_to_all | solution.py:22
  104.7 0.7 line_scan.1
  105.5 4.8 %all-to-all-start.5 = ((f32[8,72,128]{2,1,0:T(8,128)}), f32[8,72,128]{2,1,0:T(8,128)S(1)}, u32[]{:S(2)}, u32[]{:S(2)}) async-start(f32[8,72,128]{2,1,0:T(8,128)} %bitcast.9), calls=%async_computation.5 | async-start | bytes 589824 | tf_op jit(solution)/shard_map/all_to_all | solution.py:22
  110.2 1.7 %early_grads.1 = (bf16[128,512]{1,0:T(8,128)(2,1)}, bf16[128,512]{1,0:T(8,128)(2,1)}, f32[128,512]{1,0:T(8,128)S(1)}, f32[128,512]{1,0:T(8,128)S(1)}) custom-call(f32[40,128]{1,0:T(8,128)S(1)} %get-tuple-element.25.spans_ref, f32[16,8,128]{2,1,0:T(8,128)S(1)} %all_to_all.31.stats_ref, f32[128,512]{1,0:T(8,128)S(1)} %get-tuple-element.31.attention_ref, ...), custom_call_target="tpu_custom_call" | custom-call | flops 167772160 | bytes 1835008 | tf_op jit(solution)/shard_map/early_grads/pallas_call | solution.py:305
  111.9 7.7 %all-to-all-done.5 = f32[8,72,128]{2,1,0:T(8,128)S(1)} async-done(((f32[8,72,128]{2,1,0:T(8,128)}), f32[8,72,128]{2,1,0:T(8,128)S(1)}, u32[]{:S(2)}, u32[]{:S(2)}) %all-to-all-start.5) | async-done | bytes 294944 | tf_op jit(solution)/shard_map/all_to_all | solution.py:22
  119.6 1.0 final.1
  (1 shorter events, 0.0 us)
Async XLA Ops:
  31.5 6.0 %copy-start.4 = (bf16[128,512]{1,0:T(8,128)(2,1)S(1)}, bf16[128,512]{1,0:T(8,128)(2,1)}, u32[]{:S(2)}) copy-start(bf16[128,512]{1,0:T(8,128)(2,1)} %grad_ref.1) | copy-start | bytes 393220
  31.5 6.0 %copy-start.5 = (f32[512]{0:T(512)S(1)}, f32[512]{0:T(512)}, u32[]{:S(2)}) copy-start(f32[512]{0:T(512)} %param.13) | copy-start | bytes 6148
  32.2 5.2 %copy-start = (bf16[128,512]{1,0:T(8,128)(2,1)S(1)}, bf16[128,512]{1,0:T(8,128)(2,1)}, u32[]{:S(2)}) copy-start(bf16[128,512]{1,0:T(8,128)(2,1)} %k_ref.7) | copy-start | bytes 393220
  32.2 5.2 %copy-start.1 = (bf16[128,512]{1,0:T(8,128)(2,1)S(1)}, bf16[128,512]{1,0:T(8,128)(2,1)}, u32[]{:S(2)}) copy-start(bf16[128,512]{1,0:T(8,128)(2,1)} %v_ref.7) | copy-start | bytes 393220
  32.2 5.3 %copy-start.2 = (bf16[128,512]{1,0:T(8,128)(2,1)S(1)}, bf16[128,512]{1,0:T(8,128)(2,1)}, u32[]{:S(2)}) copy-start(bf16[128,512]{1,0:T(8,128)(2,1)} %q_ref.5) | copy-start | bytes 393220
  32.2 5.3 %copy-start.3 = (bf16[128,512]{1,0:T(8,128)(2,1)S(1)}, bf16[128,512]{1,0:T(8,128)(2,1)}, u32[]{:S(2)}) copy-start(bf16[128,512]{1,0:T(8,128)(2,1)} %gate_ref.3) | copy-start | bytes 393220
  32.2 18.3 %all-to-all-start.1 = ((f32[64,8,128]{2,1,0:T(8,128)}), f32[64,8,128]{2,1,0:T(8,128)S(1)}, u32[]{:S(2)}, u32[]{:S(2)}) async-start(f32[64,8,128]{2,1,0:T(8,128)} %bitcast.2), calls=%async_computation.1 | async-start | bytes 524288 | tf_op jit(solution)/shard_map/all_to_all | solution.py:22
  105.5 14.2 %all-to-all-start.5 = ((f32[8,72,128]{2,1,0:T(8,128)}), f32[8,72,128]{2,1,0:T(8,128)S(1)}, u32[]{:S(2)}, u32[]{:S(2)}) async-start(f32[8,72,128]{2,1,0:T(8,128)} %bitcast.9), calls=%async_computation.5 | async-start | bytes 589824 | tf_op jit(solution)/shard_map/all_to_all | solution.py:22

commit v5 on v3

--- a/solution.py
+++ b/solution.py
@@ -63,7 +63,7 @@
     return slice(head * DH, (head + 1) * DH)
 
 
-def summary_kernel(members, ints_ref, k_ref, v_ref, out_ref, spans_ref, ints, keys, values, arrived):
+def summary_kernel(members, ints_ref, k_ref, v_ref, out_ref, spans_ref, ints, keys, values, late, arrived):
     rows, features = k_ref.shape
     heads = features // DH
     copies = [
@@ -72,34 +72,34 @@
     ]
     for copy in copies:
         copy.start()
-    for copy in copies:
-        copy.wait()
-    for head in range(heads):
-        late = decay_column(rate_of(ints, head), rows, True)
-        weighted = late * values[:, cols(head)].astype(wide)
-        out_ref[cols(head), :] = dot(twice(keys[:, cols(head)].T, 1), halves(weighted, 0))
+    copies[0].wait()
     owned = lax.axis_index("ctx") * (features // members) // DH
     power = lax.broadcasted_iota(jnp.int32, (8, DH), 0).astype(wide) + 1.0
     spans_ref[0:8, :] = jnp.exp(-(rate_of(ints, owned) * rows) * power)
     for head in range(heads):
         spans_ref[8 + head : 9 + head, :] = jnp.full((1, DH), rate_of(ints, head), wide)
+        late[:, cols(head)] = decay_column(rate_of(ints, head), rows, True)
+    copies[1].wait()
+    copies[2].wait()
+    for head in range(heads):
+        weighted = late[:, cols(head)] * values[:, cols(head)].astype(wide)
+        out_ref[cols(head), :] = dot(twice(keys[:, cols(head)].T, 1), halves(weighted, 0))
 
 
 def scan_blocks(order, span, leap, take, put, zero):
     chains = [order[at : at + 8] for at in range(0, len(order), 8)]
-    totals = []
-    for chain in chains:
-        state = take(chain[0])
-        for block in chain[1:]:
-            state = span * state + take(block)
-        totals.append(state)
-    starts = [zero]
+    totals = [take(chain[0]) for chain in chains]
+    for turn in range(1, 8):
+        blocks = [take(chain[turn]) for chain in chains]
+        totals = [span * total + block for total, block in zip(totals, blocks)]
+    states = [zero]
     for total in totals[:-1]:
-        starts.append(leap * starts[-1] + total)
-    for chain, state in zip(chains, starts):
-        for block in chain:
-            put(block, state)
-            state = span * state + take(block)
+        states.append(leap * states[-1] + total)
+    for turn in range(8):
+        blocks = [take(chain[turn]) for chain in chains]
+        for chain, state in zip(chains, states):
+            put(chain[turn], state)
+        states = [span * state + block for state, block in zip(states, blocks)]
 
 
 def forward_kernel(members, spans_ref, in_ref, out_ref):
@@ -307,6 +307,7 @@
             pltpu.SMEM(decay_ints.shape, jnp.int32),
             pltpu.VMEM((rows, features), half),
             pltpu.VMEM((rows, features), half),
+            pltpu.VMEM((rows, features), wide),
             pltpu.SemaphoreType.DMA((3,)),
         ],
     )

time: 116 us -> 116 us (level)
  no operation moved by 1% of the time
where the time goes in v5:
time: 116 us
  blocking collectives  72.5 us (62%)
  waiting for transfers between devices  25.1 us (22%)
  starting transfers between devices  10.3 us (9%)
  Pallas kernels  6.93 us (6%)
    all_to_all x3, blocking collectives, swap(): return lax.all_to_all(array, axis, 0, 0)  72.5 us
    all_to_all x2, waiting for transfers between devices, swap(): return lax.all_to_all(array, axis, 0, 0)  25.1 us
    all_to_all x2, starting transfers between devices, swap(): return lax.all_to_all(array, axis, 0, 0)  10.3 us
    pallas_call x8, Pallas kernels, call(): pl.pallas_call(kernel, out_shape=out_shape, in_specs=[pl.BlockSpec(memory...  6.93 us
  transfers between devices with their start and end apart: 2, of which 2 were waited for; matrix products, arithmetic and copies ran while one was open for 0% of the time, Pallas kernels for 2%

profile of v5, /device:TPU:2, one launch (start us, length us, event | category | flops | bytes accessed | tf_op | source)
XLA Modules:
  0.0 115.6 jit_solution(1140568135141768731)
XLA Ops:
  0.6 1.3 %summary.1 = (f32[512,128]{1,0:T(8,128)S(1)}, f32[16,128]{1,0:T(8,128)S(1)}) custom-call(s32[4]{0:T(128)} %ints_ref.1, bf16[128,512]{1,0:T(8,128)(2,1)} %k_ref.7, bf16[128,512]{1,0:T(8,128)(2,1)} %v_ref.7), custom_call_target="tpu_custom_call" | custom-call | tf_op jit(solution)/shard_map/summary/pallas_call | solution.py:268
  1.9 29.6 %all_to_all.25 = f32[64,8,128]{2,1,0:T(8,128)S(1)} all-to-all(f32[64,8,128]{2,1,0:T(8,128)S(1)} %bitcast.16), channel_id=1, replica_groups=mesh['ctx'=64,'head'=16] {'ctx'}, dimensions={0} | all-to-all | bytes 524288 | tf_op jit(solution)/shard_map/all_to_all | solution.py:21
  31.5 0.0 copy-start.4
  31.5 0.0 copy-start.5
  31.5 0.7 forward_scan.1
  32.2 0.0 copy-start
  32.2 0.0 copy-start.1
  32.2 0.0 copy-start.2
  32.2 0.0 copy-start.3
  32.2 5.2 %all-to-all-start.1 = ((f32[64,8,128]{2,1,0:T(8,128)}), f32[64,8,128]{2,1,0:T(8,128)S(1)}, u32[]{:S(2)}, u32[]{:S(2)}) async-start(f32[64,8,128]{2,1,0:T(8,128)} %bitcast.2), calls=%async_computation.1 | async-start | bytes 524288 | tf_op jit(solution)/shard_map/all_to_all | solution.py:21
  37.4 0.0 copy-done.4
  37.4 0.0 copy-done.5
  37.4 0.0 copy-done
  37.5 0.0 copy-done.1
  37.5 0.0 copy-done.2
  37.5 0.0 copy-done.3
  37.5 0.7 local_attention.1
  38.2 12.3 %all-to-all-done.1 = f32[64,8,128]{2,1,0:T(8,128)S(1)} async-done(((f32[64,8,128]{2,1,0:T(8,128)}), f32[64,8,128]{2,1,0:T(8,128)S(1)}, u32[]{:S(2)}, u32[]{:S(2)}) %all-to-all-start.1) | async-done | bytes 262176 | tf_op jit(solution)/shard_map/all_to_all | solution.py:21
  50.6 0.3 attend.1
  50.9 23.0 %all_to_all.26.stats_ref = f32[16,8,128]{2,1,0:T(8,128)S(1)} all-to-all(f32[16,8,128]{2,1,0:T(8,128)S(1)} %get-tuple-element.30), channel_id=1, replica_groups=mesh['ctx'=64,'head'=16] {'head'}, dimensions={0} | all-to-all | bytes 131072 | tf_op jit(solution)/shard_map/all_to_all | solution.py:21
  73.9 0.5 ahead.1
  74.3 19.9 %all_to_all.27 = f32[64,9,1,128]{3,2,1,0:T(1,128)S(1)} all-to-all(f32[64,9,1,128]{3,2,1,0:T(1,128)S(1)} %bitcast.15), channel_id=1, replica_groups=mesh['ctx'=64,'head'=16] {'ctx'}, dimensions={0} | all-to-all | bytes 589824 | tf_op jit(solution)/shard_map/all_to_all | solution.py:21
  94.3 0.8 backward_scan.1
  95.0 5.1 %all-to-all-start.4 = ((f32[64,9,1,128]{3,2,1,0:T(1,128)}), f32[64,9,1,128]{3,2,1,0:T(1,128)S(1)}, u32[]{:S(2)}, u32[]{:S(2)}) async-start(f32[64,9,1,128]{3,2,1,0:T(1,128)} %bitcast.7), calls=%async_computation.4 | async-start | bytes 589824 | tf_op jit(solution)/shard_map/all_to_all | solution.py:21
  100.1 1.7 %early_grads.1 = (bf16[128,512]{1,0:T(8,128)(2,1)}, bf16[128,512]{1,0:T(8,128)(2,1)}, f32[128,512]{1,0:T(8,128)S(1)}, f32[128,512]{1,0:T(8,128)S(1)}) custom-call(f32[16,128]{1,0:T(8,128)S(1)} %get-tuple-element.25.spans_ref, f32[16,8,128]{2,1,0:T(8,128)S(1)} %all_to_all.26.stats_ref, f32[128,512]{1,0:T(8,128)S(1)} %get-tuple-element.31.attention_ref, ...), custom_call_target="tpu_custom_call" | custom-call | flops 167772160 | bytes 1835008 | tf_op jit(solution)/shard_map/early_grads/pallas_call | solution.py:268
  101.8 12.8 %all-to-all-done.4 = f32[64,9,1,128]{3,2,1,0:T(1,128)S(1)} async-done(((f32[64,9,1,128]{3,2,1,0:T(1,128)}), f32[64,9,1,128]{3,2,1,0:T(1,128)S(1)}, u32[]{:S(2)}, u32[]{:S(2)}) %all-to-all-start.4) | async-done | bytes 294944 | tf_op jit(solution)/shard_map/all_to_all | solution.py:21
  114.6 1.0 final.1
Async XLA Ops:
  31.5 6.0 %copy-start.4 = (bf16[128,512]{1,0:T(8,128)(2,1)S(1)}, bf16[128,512]{1,0:T(8,128)(2,1)}, u32[]{:S(2)}) copy-start(bf16[128,512]{1,0:T(8,128)(2,1)} %grad_ref.1) | copy-start | bytes 393220
  31.5 6.0 %copy-start.5 = (f32[512]{0:T(512)S(1)}, f32[512]{0:T(512)}, u32[]{:S(2)}) copy-start(f32[512]{0:T(512)} %param.13) | copy-start | bytes 6148
  32.2 5.2 %copy-start = (bf16[128,512]{1,0:T(8,128)(2,1)S(1)}, bf16[128,512]{1,0:T(8,128)(2,1)}, u32[]{:S(2)}) copy-start(bf16[128,512]{1,0:T(8,128)(2,1)} %k_ref.7) | copy-start | bytes 393220
  32.2 5.2 %copy-start.1 = (bf16[128,512]{1,0:T(8,128)(2,1)S(1)}, bf16[128,512]{1,0:T(8,128)(2,1)}, u32[]{:S(2)}) copy-start(bf16[128,512]{1,0:T(8,128)(2,1)} %v_ref.7) | copy-start | bytes 393220
  32.2 5.3 %copy-start.2 = (bf16[128,512]{1,0:T(8,128)(2,1)S(1)}, bf16[128,512]{1,0:T(8,128)(2,1)}, u32[]{:S(2)}) copy-start(bf16[128,512]{1,0:T(8,128)(2,1)} %q_ref.5) | copy-start | bytes 393220
  32.2 5.3 %copy-start.3 = (bf16[128,512]{1,0:T(8,128)(2,1)S(1)}, bf16[128,512]{1,0:T(8,128)(2,1)}, u32[]{:S(2)}) copy-start(bf16[128,512]{1,0:T(8,128)(2,1)} %gate_ref.3) | copy-start | bytes 393220
  32.2 18.3 %all-to-all-start.1 = ((f32[64,8,128]{2,1,0:T(8,128)}), f32[64,8,128]{2,1,0:T(8,128)S(1)}, u32[]{:S(2)}, u32[]{:S(2)}) async-start(f32[64,8,128]{2,1,0:T(8,128)} %bitcast.2), calls=%async_computation.1 | async-start | bytes 524288 | tf_op jit(solution)/shard_map/all_to_all | solution.py:21
  95.0 19.6 %all-to-all-start.4 = ((f32[64,9,1,128]{3,2,1,0:T(1,128)}), f32[64,9,1,128]{3,2,1,0:T(1,128)S(1)}, u32[]{:S(2)}, u32[]{:S(2)}) async-start(f32[64,9,1,128]{3,2,1,0:T(1,128)} %bitcast.7), calls=%async_computation.4 | async-start | bytes 589824 | tf_op jit(solution)/shard_map/all_to_all | solution.py:21

commit v6 on v5

--- a/solution.py
+++ b/solution.py
@@ -134,37 +134,30 @@
         out_ref[block * step + chunk : (block + 1) * step, :] = gains[0]
 
 
-def local_kernel(
-    spans_ref, q_ref, k_ref, v_ref, gate_ref, grad_ref, gain_ref,
-    local_ref, weights_ref, gated_ref, scaled_ref, qt_ref, early_ref, late_ref,
+def attend_kernel(
+    spans_ref, q_ref, k_ref, v_ref, gate_ref, grad_ref, gain_ref, prefix_ref,
+    attention_ref, stats_ref, weights_ref, gated_ref, scaled_ref, early_ref,
 ):
-    rows, features = q_ref.shape
-    for head in range(features // DH):
-        at = cols(head)
-        rate = spans_ref[8 + head : 9 + head, :]
-        scores = dot_nt(q_ref[:, at], k_ref[:, at])
-        weights = (scores * decay_square(rate, rows)).astype(half)
-        weights_ref[:, at] = weights
-        local_ref[:, at] = dot(weights, v_ref[:, at])
-        qt_ref[at, :] = q_ref[:, at].T
-        gated = grad_ref[:, at].astype(wide) * jax.nn.sigmoid(gate_ref[:, at].astype(wide))
-        gated_ref[:, at] = gated
-        scaled_ref[:, at] = gated * gain_ref[:, at]
-        early_ref[:, at] = decay_column(rate, rows, False)
-        late_ref[:, at] = decay_column(rate, rows, True) * (1.0 / DH)
-
-
-def attend_kernel(q_ref, prefix_ref, local_ref, scaled_ref, early_ref, attention_ref, stats_ref):
     rows, features = q_ref.shape
     squares = jnp.zeros((rows, DH), wide)
     crossed = jnp.zeros((rows, DH), wide)
     for head in range(features // DH):
         at = cols(head)
-        carried = dot(twice(q_ref[:, at], 1), halves(prefix_ref[at, :], 0)) * (1.0 / DH)
-        attention = local_ref[:, at] + early_ref[:, at] * carried
+        rate = spans_ref[8 + head : 9 + head, :]
+        queries = q_ref[:, at]
+        weights = (dot_nt(queries, k_ref[:, at]) * decay_square(rate, rows)).astype(half)
+        weights_ref[:, at] = weights
+        gated = grad_ref[:, at].astype(wide) * jax.nn.sigmoid(gate_ref[:, at].astype(wide))
+        gated_ref[:, at] = gated
+        scaled = gated * gain_ref[:, at]
+        scaled_ref[:, at] = scaled
+        early = decay_column(rate, rows, False)
+        early_ref[:, at] = early
+        carried = dot(twice(queries, 1), halves(prefix_ref[at, :], 0)) * (1.0 / DH)
+        attention = dot(weights, v_ref[:, at]) + early * carried
         attention_ref[:, at] = attention
         squares = squares + attention * attention
-        crossed = crossed + scaled_ref[:, at] * attention
+        crossed = crossed + scaled * attention
     squares = jnp.sum(squares.T, axis=0, keepdims=True)
     crossed = jnp.sum(crossed.T, axis=0, keepdims=True)
     line = lax.broadcasted_iota(jnp.int32, (8, DH), 0)
@@ -185,7 +178,7 @@
 
 
 def ahead_kernel(
-    members, stats_ref, attention_ref, gated_ref, scaled_ref, qt_ref, early_ref, grad_ref, out_ref
+    members, stats_ref, attention_ref, gated_ref, scaled_ref, q_ref, early_ref, grad_ref, out_ref
 ):
     rows, features = attention_ref.shape
     heads = features // DH
@@ -197,7 +190,7 @@
         attention = attention_ref[:, at]
         grad = (inverse * scaled_ref[:, at] - pull * attention).astype(half)
         grad_ref[:, at] = grad
-        ahead = dot(twice(qt_ref[at, :], 1), halves(early_ref[:, at] * grad.astype(wide), 0))
+        ahead = dot(twice(q_ref[:, at].T, 1), halves(early_ref[:, at] * grad.astype(wide), 0))
         for piece in range(DH // chunk):
             start = (head * (DH // chunk) + piece) * step
             out_ref[start : start + chunk, :] = ahead[piece * chunk : (piece + 1) * chunk, :]
@@ -208,7 +201,7 @@
 
 def early_grads_kernel(
     spans_ref, stats_ref, attention_ref, scaled_ref, gate_ref, grad_ref, q_ref, k_ref, v_ref,
-    weights_ref, prefix_ref, early_ref, grad_q_ref, grad_gate_ref, local_k_ref, local_v_ref,
+    weights_ref, prefix_ref, early_ref, grad_q_ref, grad_gate_ref, local_k_ref, local_v_ref, late_ref,
 ):
     rows, features = q_ref.shape
     inverse, _ = token_scales(stats_ref)
@@ -218,7 +211,9 @@
         rest = 1.0 - jax.nn.sigmoid(gate_ref[:, at].astype(wide))
         grad_gate_ref[:, at] = (scaled_ref[:, at] * normed * rest).astype(half)
         grad = grad_ref[:, at]
-        square = decay_square(spans_ref[8 + head : 9 + head, :], rows)
+        rate = spans_ref[8 + head : 9 + head, :]
+        late_ref[:, at] = decay_column(rate, rows, True) * (1.0 / DH)
+        square = decay_square(rate, rows)
         grad_scores = (dot_nt(grad, v_ref[:, at]) * square).astype(half)
         carried = dot_nt(twice(grad, 1), halves(prefix_ref[at, :], 1)) * (1.0 / DH)
         grad_q = dot(grad_scores, k_ref[:, at]) + early_ref[:, at] * carried
@@ -312,32 +307,25 @@
         ],
     )
     there = across(summary, chunk)
-    local, weights, gated, scaled, queries_t, early, late = call(
-        local_kernel,
-        "local_attention",
-        [block_wide, block_half, block_wide, block_wide, ((features, rows), half), block_wide, block_wide],
-        spans, queries, key_rows, value_rows, gate_in, grad_out, norm_gain.reshape(1, features),
-        flops=8 * area * DH, bytes_moved=28 * area,
-    )
     prefix = across(call(sized(forward_kernel), "forward_scan", [flat], spans, there), chunk)
-    attention, stats = call(
+    attention, stats, weights, gated, scaled, early = call(
         attend_kernel,
         "attend",
-        [block_wide, ((head_members, 8, rows), wide)],
-        queries, prefix, local, scaled, early,
+        [block_wide, ((head_members, 8, rows), wide), block_half, block_wide, block_wide, block_wide],
+        spans, queries, key_rows, value_rows, gate_in, grad_out, norm_gain.reshape(1, features), prefix,
     )
     stats = swap(stats, "head")
     grad, message = call(
         sized(ahead_kernel),
         "ahead",
         [block_half, long],
-        stats, attention, gated, scaled, queries_t, early,
+        stats, attention, gated, scaled, queries, early,
     )
     there = across(message, step)
-    grad_q, grad_gate, local_k, local_v = call(
+    grad_q, grad_gate, local_k, local_v, late = call(
         early_grads_kernel,
         "early_grads",
-        [block_half, block_half, block_wide, block_wide],
+        [block_half, block_half, block_wide, block_wide, block_wide],
         spans, stats, attention, scaled, gate_in, grad, queries, key_rows, value_rows,
         weights, prefix, early,
         flops=20 * area * DH, bytes_moved=28 * area,

time: 116 us -> 116 us (level)
  blocking collectives: 72.5 us -> 90.7 us
  waiting for transfers between devices: 25.1 us -> 12.7 us
  starting transfers between devices: 10.3 us -> 5.13 us
    all_to_all x3 -> x4, blocking collectives: 72.5 us -> 90.7 us  [swap(): return lax.all_to_all(array, axis, 0, 0)]
    all_to_all x2 -> x1, waiting for transfers between devices: 25.1 us -> 12.7 us  [swap(): return lax.all_to_all(array, axis, 0, 0)]
    all_to_all x2 -> x1, starting transfers between devices: 10.3 us -> 5.13 us  [swap(): return lax.all_to_all(array, axis, 0, 0)]
    pallas_call x8 -> x7, Pallas kernels: 6.93 us -> 5.8 us  [call(): pl.pallas_call(kernel, out_shape=out_shape, in_specs=[pl.BlockSpec(memory...]
  transfers between devices with their start and end apart: 2 -> 1, of which waited for: 2 -> 1; matrix products, arithmetic and copies ran while one was open for 0% -> 0% of each run, Pallas kernels for 2% -> 1%
where the time goes in v6:
time: 116 us
  blocking collectives  90.7 us (78%)
  waiting for transfers between devices  12.7 us (11%)
  Pallas kernels  5.8 us (5%)
  starting transfers between devices  5.13 us (4%)
    all_to_all x4, blocking collectives, swap(): return lax.all_to_all(array, axis, 0, 0)  90.7 us
    all_to_all x1, waiting for transfers between devices, swap(): return lax.all_to_all(array, axis, 0, 0)  12.7 us
    pallas_call x7, Pallas kernels, call(): pl.pallas_call(kernel, out_shape=out_shape, in_specs=[pl.BlockSpec(memory...  5.8 us
    all_to_all x1, starting transfers between devices, swap(): return lax.all_to_all(array, axis, 0, 0)  5.13 us
  transfers between devices with their start and end apart: 1, of which 1 were waited for; matrix products, arithmetic and copies ran while one was open for 0% of the time, Pallas kernels for 1%

profile of v6, /device:TPU:2, one launch (start us, length us, event | category | flops | bytes accessed | tf_op | source)
XLA Modules:
  0.0 115.7 jit_solution(9216393599280947328)
XLA Ops:
  0.6 1.3 %summary.1 = (f32[512,128]{1,0:T(8,128)S(1)}, f32[16,128]{1,0:T(8,128)S(1)}) custom-call(s32[4]{0:T(128)} %ints_ref.1, bf16[128,512]{1,0:T(8,128)(2,1)} %k_ref.7, bf16[128,512]{1,0:T(8,128)(2,1)} %v_ref.7), custom_call_target="tpu_custom_call" | custom-call | tf_op jit(solution)/shard_map/summary/pallas_call | solution.py:263
  1.9 29.6 %all_to_all.25 = f32[64,8,128]{2,1,0:T(8,128)S(1)} all-to-all(f32[64,8,128]{2,1,0:T(8,128)S(1)} %bitcast.17), channel_id=1, replica_groups=mesh['ctx'=64,'head'=16] {'ctx'}, dimensions={0} | all-to-all | bytes 524288 | tf_op jit(solution)/shard_map/all_to_all | solution.py:21
  31.5 0.0 copy-start.4
  31.5 0.0 copy-start
  31.5 0.0 copy-start.1
  31.5 0.0 copy-start.2
  31.5 0.0 copy-start.3
  31.6 17.5 %all_to_all.26 = f32[64,8,128]{2,1,0:T(8,128)S(1)} all-to-all(f32[64,8,128]{2,1,0:T(8,128)S(1)} %bitcast.15), channel_id=1, replica_groups=mesh['ctx'=64,'head'=16] {'ctx'}, dimensions={0} | all-to-all | bytes 524288 | tf_op jit(solution)/shard_map/all_to_all | solution.py:21
  49.1 0.0 copy-start.5
  49.1 0.0 copy-done.4
  49.1 0.0 copy-done
  49.1 0.0 copy-done.1
  49.1 0.0 copy-done.2
  49.1 0.0 copy-done.3
  49.1 0.6 copy-done.5
  49.8 0.6 attend.1
  50.4 23.5 %all_to_all.27.stats_ref = f32[16,8,128]{2,1,0:T(8,128)S(1)} all-to-all(f32[16,8,128]{2,1,0:T(8,128)S(1)} %get-tuple-element.25), channel_id=1, replica_groups=mesh['ctx'=64,'head'=16] {'head'}, dimensions={0} | all-to-all | bytes 131072 | tf_op jit(solution)/shard_map/all_to_all | solution.py:21
  73.9 0.5 ahead.1
  74.3 20.1 %all_to_all.28 = f32[64,9,1,128]{3,2,1,0:T(1,128)S(1)} all-to-all(f32[64,9,1,128]{3,2,1,0:T(1,128)S(1)} %bitcast.16), channel_id=1, replica_groups=mesh['ctx'=64,'head'=16] {'ctx'}, dimensions={0} | all-to-all | bytes 589824 | tf_op jit(solution)/shard_map/all_to_all | solution.py:21
  94.4 0.8 backward_scan.1
  95.2 5.1 %all-to-all-start.4 = ((f32[64,9,1,128]{3,2,1,0:T(1,128)}), f32[64,9,1,128]{3,2,1,0:T(1,128)S(1)}, u32[]{:S(2)}, u32[]{:S(2)}) async-start(f32[64,9,1,128]{3,2,1,0:T(1,128)} %bitcast.7), calls=%async_computation.4 | async-start | bytes 589824 | tf_op jit(solution)/shard_map/all_to_all | solution.py:21
  100.3 1.7 %early_grads.1 = (bf16[128,512]{1,0:T(8,128)(2,1)}, bf16[128,512]{1,0:T(8,128)(2,1)}, f32[128,512]{1,0:T(8,128)S(1)}, f32[128,512]{1,0:T(8,128)S(1)}, f32[128,512]{1,0:T(8,128)S(1)}) custom-call(f32[16,128]{1,0:T(8,128)S(1)} %get-tuple-element.23.spans_ref, f32[16,8,128]{2,1,0:T(8,128)S(1)} %all_to_all.27.stats_ref, ...), custom_call_target="tpu_custom_call" | custom-call | flops 167772160 | bytes 1835008 | tf_op jit(solution)/shard_map/early_grads/pallas_call | solution.py:263
  102.0 12.7 %all-to-all-done.4 = f32[64,9,1,128]{3,2,1,0:T(1,128)S(1)} async-done(((f32[64,9,1,128]{3,2,1,0:T(1,128)}), f32[64,9,1,128]{3,2,1,0:T(1,128)S(1)}, u32[]{:S(2)}, u32[]{:S(2)}) %all-to-all-start.4) | async-done | bytes 294944 | tf_op jit(solution)/shard_map/all_to_all | solution.py:21
  114.7 1.0 final.1
  (1 shorter events, 0.0 us)
Async XLA Ops:
  31.5 17.6 %copy-start.4 = (bf16[128,512]{1,0:T(8,128)(2,1)S(1)}, bf16[128,512]{1,0:T(8,128)(2,1)}, u32[]{:S(2)}) copy-start(bf16[128,512]{1,0:T(8,128)(2,1)} %grad_ref.1) | copy-start | bytes 393220
  31.5 17.6 %copy-start = (bf16[128,512]{1,0:T(8,128)(2,1)S(1)}, bf16[128,512]{1,0:T(8,128)(2,1)}, u32[]{:S(2)}) copy-start(bf16[128,512]{1,0:T(8,128)(2,1)} %k_ref.7) | copy-start | bytes 393220
  31.5 17.6 %copy-start.1 = (bf16[128,512]{1,0:T(8,128)(2,1)S(1)}, bf16[128,512]{1,0:T(8,128)(2,1)}, u32[]{:S(2)}) copy-start(bf16[128,512]{1,0:T(8,128)(2,1)} %v_ref.7) | copy-start | bytes 393220
  31.5 17.6 %copy-start.2 = (bf16[128,512]{1,0:T(8,128)(2,1)S(1)}, bf16[128,512]{1,0:T(8,128)(2,1)}, u32[]{:S(2)}) copy-start(bf16[128,512]{1,0:T(8,128)(2,1)} %q_ref.5) | copy-start | bytes 393220
  31.5 17.6 %copy-start.3 = (bf16[128,512]{1,0:T(8,128)(2,1)S(1)}, bf16[128,512]{1,0:T(8,128)(2,1)}, u32[]{:S(2)}) copy-start(bf16[128,512]{1,0:T(8,128)(2,1)} %gate_ref.3) | copy-start | bytes 393220
  49.1 0.7 copy-start.5
  95.2 19.5 %all-to-all-start.4 = ((f32[64,9,1,128]{3,2,1,0:T(1,128)}), f32[64,9,1,128]{3,2,1,0:T(1,128)S(1)}, u32[]{:S(2)}, u32[]{:S(2)}) async-start(f32[64,9,1,128]{3,2,1,0:T(1,128)} %bitcast.7), calls=%async_computation.4 | async-start | bytes 589824 | tf_op jit(solution)/shard_map/all_to_all | solution.py:21

commit v7 on v6

--- a/solution.py
+++ b/solution.py
@@ -63,12 +63,16 @@
     return slice(head * DH, (head + 1) * DH)
 
 
-def summary_kernel(members, ints_ref, k_ref, v_ref, out_ref, spans_ref, ints, keys, values, late, arrived):
+def summary_kernel(
+    members, ints_ref, k_ref, v_ref, gain_ref, out_ref, spans_ref, gain_out_ref, ints, keys, values, late, arrived
+):
     rows, features = k_ref.shape
     heads = features // DH
     copies = [
         pltpu.make_async_copy(source, target, arrived.at[number])
-        for number, (source, target) in enumerate(((ints_ref, ints), (k_ref, keys), (v_ref, values)))
+        for number, (source, target) in enumerate(
+            ((ints_ref, ints), (k_ref, keys), (v_ref, values), (gain_ref, gain_out_ref))
+        )
     ]
     for copy in copies:
         copy.start()
@@ -84,6 +88,7 @@
     for head in range(heads):
         weighted = late[:, cols(head)] * values[:, cols(head)].astype(wide)
         out_ref[cols(head), :] = dot(twice(keys[:, cols(head)].T, 1), halves(weighted, 0))
+    copies[3].wait()
 
 
 def scan_blocks(order, span, leap, take, put, zero):
@@ -292,18 +297,19 @@
     def sized(kernel):
         return functools.partial(kernel, members)
 
-    summary, spans = call(
+    given = (decay_ints, key_rows, value_rows, norm_gain.reshape(1, features))
+    summary, spans, gain = call(
         sized(summary_kernel),
         "summary",
-        [flat, ((16, DH), wide)],
-        *[pltpu.with_memory_space_constraint(a, pltpu.HBM) for a in (decay_ints, key_rows, value_rows)],
+        [flat, ((16, DH), wide), ((1, features), wide)],
+        *[pltpu.with_memory_space_constraint(a, pltpu.HBM) for a in given],
         place=pltpu.HBM,
         scratch=[
             pltpu.SMEM(decay_ints.shape, jnp.int32),
             pltpu.VMEM((rows, features), half),
             pltpu.VMEM((rows, features), half),
             pltpu.VMEM((rows, features), wide),
-            pltpu.SemaphoreType.DMA((3,)),
+            pltpu.SemaphoreType.DMA((4,)),
         ],
     )
     there = across(summary, chunk)
@@ -312,7 +318,7 @@
         attend_kernel,
         "attend",
         [block_wide, ((head_members, 8, rows), wide), block_half, block_wide, block_wide, block_wide],
-        spans, queries, key_rows, value_rows, gate_in, grad_out, norm_gain.reshape(1, features), prefix,
+        spans, queries, key_rows, value_rows, gate_in, grad_out, gain, prefix,
     )
     stats = swap(stats, "head")
     grad, message = call(

time: 116 us -> 115 us (level)
  no operation moved by 1% of the time
where the time goes in v7:
time: 115 us
  blocking collectives  90.6 us (79%)
  waiting for transfers between devices  12.6 us (11%)
  Pallas kernels  5.8 us (5%)
  starting transfers between devices  5.15 us (4%)
    all_to_all x4, blocking collectives, swap(): return lax.all_to_all(array, axis, 0, 0)  90.6 us
    all_to_all x1, waiting for transfers between devices, swap(): return lax.all_to_all(array, axis, 0, 0)  12.6 us
    pallas_call x7, Pallas kernels, call(): pl.pallas_call(kernel, out_shape=out_shape, in_specs=[pl.BlockSpec(memory...  5.8 us
    all_to_all x1, starting transfers between devices, swap(): return lax.all_to_all(array, axis, 0, 0)  5.15 us
  transfers between devices with their start and end apart: 1, of which 1 were waited for; matrix products, arithmetic and copies ran while one was open for 0% of the time, Pallas kernels for 1%

profile of v7, /device:TPU:2, one launch (start us, length us, event | category | flops | bytes accessed | tf_op | source)
XLA Modules:
  0.0 114.9 jit_solution(7887914957328529473)
XLA Ops:
  0.6 1.3 %summary.1 = (f32[512,128]{1,0:T(8,128)S(1)}, f32[16,128]{1,0:T(8,128)S(1)}, f32[1,512]{1,0:T(1,128)S(1)}) custom-call(s32[4]{0:T(128)} %ints_ref.1, bf16[128,512]{1,0:T(8,128)(2,1)} %k_ref.7, bf16[128,512]{1,0:T(8,128)(2,1)} %v_ref.7, f32[1,512]{1,0:T(1,128)} %bitcast.18), custom_call_target="tpu_custom_call" | custom-call | tf_op jit(solution)/shard_map/summary/pallas_call | solution.py:268
  1.9 29.6 %all_to_all.25 = f32[64,8,128]{2,1,0:T(8,128)S(1)} all-to-all(f32[64,8,128]{2,1,0:T(8,128)S(1)} %bitcast.17), channel_id=1, replica_groups=mesh['ctx'=64,'head'=16] {'ctx'}, dimensions={0} | all-to-all | bytes 524288 | tf_op jit(solution)/shard_map/all_to_all | solution.py:21
  31.5 0.0 copy-start.4
  31.5 0.0 copy-start
  31.5 0.0 copy-start.1
  31.5 0.0 copy-start.2
  31.6 0.0 copy-start.3
  31.6 17.5 %all_to_all.26 = f32[64,8,128]{2,1,0:T(8,128)S(1)} all-to-all(f32[64,8,128]{2,1,0:T(8,128)S(1)} %bitcast.15), channel_id=1, replica_groups=mesh['ctx'=64,'head'=16] {'ctx'}, dimensions={0} | all-to-all | bytes 524288 | tf_op jit(solution)/shard_map/all_to_all | solution.py:21
  49.1 0.0 copy-done.4
  49.1 0.0 copy-done
  49.1 0.0 copy-done.1
  49.1 0.0 copy-done.2
  49.1 0.0 copy-done.3
  49.1 0.6 attend.1
  49.7 23.5 %all_to_all.27.stats_ref = f32[16,8,128]{2,1,0:T(8,128)S(1)} all-to-all(f32[16,8,128]{2,1,0:T(8,128)S(1)} %get-tuple-element.27), channel_id=1, replica_groups=mesh['ctx'=64,'head'=16] {'head'}, dimensions={0} | all-to-all | bytes 131072 | tf_op jit(solution)/shard_map/all_to_all | solution.py:21
  73.2 0.5 ahead.1
  73.7 20.0 %all_to_all.28 = f32[64,9,1,128]{3,2,1,0:T(1,128)S(1)} all-to-all(f32[64,9,1,128]{3,2,1,0:T(1,128)S(1)} %bitcast.16), channel_id=1, replica_groups=mesh['ctx'=64,'head'=16] {'ctx'}, dimensions={0} | all-to-all | bytes 589824 | tf_op jit(solution)/shard_map/all_to_all | solution.py:21
  93.7 0.8 backward_scan.1
  94.5 5.2 %all-to-all-start.4 = ((f32[64,9,1,128]{3,2,1,0:T(1,128)}), f32[64,9,1,128]{3,2,1,0:T(1,128)S(1)}, u32[]{:S(2)}, u32[]{:S(2)}) async-start(f32[64,9,1,128]{3,2,1,0:T(1,128)} %bitcast.7), calls=%async_computation.4 | async-start | bytes 589824 | tf_op jit(solution)/shard_map/all_to_all | solution.py:21
  99.7 1.7 %early_grads.1 = (bf16[128,512]{1,0:T(8,128)(2,1)}, bf16[128,512]{1,0:T(8,128)(2,1)}, f32[128,512]{1,0:T(8,128)S(1)}, f32[128,512]{1,0:T(8,128)S(1)}, f32[128,512]{1,0:T(8,128)S(1)}) custom-call(f32[16,128]{1,0:T(8,128)S(1)} %get-tuple-element.24.spans_ref, f32[16,8,128]{2,1,0:T(8,128)S(1)} %all_to_all.27.stats_ref, ...), custom_call_target="tpu_custom_call" | custom-call | flops 167772160 | bytes 1835008 | tf_op jit(solution)/shard_map/early_grads/pallas_call | solution.py:268
  101.3 12.6 %all-to-all-done.4 = f32[64,9,1,128]{3,2,1,0:T(1,128)S(1)} async-done(((f32[64,9,1,128]{3,2,1,0:T(1,128)}), f32[64,9,1,128]{3,2,1,0:T(1,128)S(1)}, u32[]{:S(2)}, u32[]{:S(2)}) %all-to-all-start.4) | async-done | bytes 294944 | tf_op jit(solution)/shard_map/all_to_all | solution.py:21
  113.9 1.0 final.1
  (1 shorter events, 0.0 us)
Async XLA Ops:
  31.5 17.6 %copy-start.4 = (bf16[128,512]{1,0:T(8,128)(2,1)S(1)}, bf16[128,512]{1,0:T(8,128)(2,1)}, u32[]{:S(2)}) copy-start(bf16[128,512]{1,0:T(8,128)(2,1)} %grad_ref.1) | copy-start | bytes 393220
  31.5 17.6 %copy-start = (bf16[128,512]{1,0:T(8,128)(2,1)S(1)}, bf16[128,512]{1,0:T(8,128)(2,1)}, u32[]{:S(2)}) copy-start(bf16[128,512]{1,0:T(8,128)(2,1)} %k_ref.7) | copy-start | bytes 393220
  31.5 17.6 %copy-start.1 = (bf16[128,512]{1,0:T(8,128)(2,1)S(1)}, bf16[128,512]{1,0:T(8,128)(2,1)}, u32[]{:S(2)}) copy-start(bf16[128,512]{1,0:T(8,128)(2,1)} %v_ref.7) | copy-start | bytes 393220
  31.5 17.6 %copy-start.2 = (bf16[128,512]{1,0:T(8,128)(2,1)S(1)}, bf16[128,512]{1,0:T(8,128)(2,1)}, u32[]{:S(2)}) copy-start(bf16[128,512]{1,0:T(8,128)(2,1)} %q_ref.5) | copy-start | bytes 393220
  31.6 17.6 %copy-start.3 = (bf16[128,512]{1,0:T(8,128)(2,1)S(1)}, bf16[128,512]{1,0:T(8,128)(2,1)}, u32[]{:S(2)}) copy-start(bf16[128,512]{1,0:T(8,128)(2,1)} %gate_ref.3) | copy-start | bytes 393220
  94.5 19.4 %all-to-all-start.4 = ((f32[64,9,1,128]{3,2,1,0:T(1,128)}), f32[64,9,1,128]{3,2,1,0:T(1,128)S(1)}, u32[]{:S(2)}, u32[]{:S(2)}) async-start(f32[64,9,1,128]{3,2,1,0:T(1,128)} %bitcast.7), calls=%async_computation.4 | async-start | bytes 589824 | tf_op jit(solution)/shard_map/all_to_all | solution.py:21

commit v8 on v7

--- a/solution.py
+++ b/solution.py
@@ -13,12 +13,19 @@
 
 rate_unit = 2.0 ** (-20)
 norm_eps = 1e-06
+first_place = {"ctx": 36, "head": 14}
 wide = jnp.float32
 half = jnp.bfloat16
 
 
 def swap(array, axis):
-    return lax.all_to_all(array, axis, 0, 0)
+    size, first = lax.axis_size(axis), first_place[axis]
+    groups = [[(first + slot) % size for slot in range(size)]]
+    return lax.all_to_all(array, axis, 0, 0, axis_index_groups=groups)
+
+
+def ctx_slots(members):
+    return [(block - first_place["ctx"]) % members for block in range(members)]
 
 
 def halves(array, axis):
@@ -77,7 +84,8 @@
     for copy in copies:
         copy.start()
     copies[0].wait()
-    owned = lax.axis_index("ctx") * (features // members) // DH
+    slot = (lax.axis_index("ctx") + (members - first_place["ctx"])) % members
+    owned = slot * (features // members) // DH
     power = lax.broadcasted_iota(jnp.int32, (8, DH), 0).astype(wide) + 1.0
     spans_ref[0:8, :] = jnp.exp(-(rate_of(ints, owned) * rows) * power)
     for head in range(heads):
@@ -116,7 +124,7 @@
     def put(block, state):
         out_ref[block * chunk : (block + 1) * chunk, :] = state
 
-    order = list(range(members))
+    order = ctx_slots(members)
     scan_blocks(order, spans_ref[0:1, :], spans_ref[7:8, :], take, put, jnp.zeros((chunk, DH), wide))
 
 
@@ -130,7 +138,7 @@
     def put(block, state):
         out_ref[block * step : block * step + chunk, :] = state
 
-    order = list(reversed(range(members)))
+    order = list(reversed(ctx_slots(members)))
     scan_blocks(order, spans_ref[0:1, :], spans_ref[7:8, :], take, put, jnp.zeros((chunk, DH), wide))
     gains = [in_ref[block * step + chunk : (block + 1) * step, :] for block in range(members)]
     while len(gains) > 1:

time: 115 us -> 108 us (0.939)
  blocking collectives: 90.6 us -> 83.1 us
  waiting for transfers between devices: 12.6 us -> 5.86 us
  starting transfers between devices: 5.15 us -> 11.8 us
    all_to_all x4, blocking collectives: 90.6 us -> 83.1 us  [swap(): return lax.all_to_all(array, axis, 0, 0, axis_index_groups=groups)]
    all_to_all x1, waiting for transfers between devices: 12.6 us -> 5.86 us  [swap(): return lax.all_to_all(array, axis, 0, 0, axis_index_groups=groups)]
    all_to_all x1, starting transfers between devices: 5.15 us -> 11.8 us  [swap(): return lax.all_to_all(array, axis, 0, 0, axis_index_groups=groups)]
  transfers between devices with their start and end apart: 1 -> 1, of which waited for: 1 -> 1; matrix products, arithmetic and copies ran while one was open for 0% -> 0% of each run, Pallas kernels for 1% -> 2%
where the time goes in v8:
time: 108 us; the launch traced here: 107 us
  blocking collectives  83.1 us (77%)
  starting transfers between devices  11.8 us (11%)
  waiting for transfers between devices  5.86 us (5%)
  Pallas kernels  5.8 us (5%)
    all_to_all x4, blocking collectives, swap(): return lax.all_to_all(array, axis, 0, 0, axis_index_groups=groups)  83.1 us
    all_to_all x1, starting transfers between devices, swap(): return lax.all_to_all(array, axis, 0, 0, axis_index_groups=groups)  11.8 us
    all_to_all x1, waiting for transfers between devices, swap(): return lax.all_to_all(array, axis, 0, 0, axis_index_groups=groups)  5.86 us
    pallas_call x7, Pallas kernels, call(): pl.pallas_call(kernel, out_shape=out_shape, in_specs=[pl.BlockSpec(memory...  5.8 us
  transfers between devices with their start and end apart: 1, of which 1 were waited for; matrix products, arithmetic and copies ran while one was open for 0% of the time, Pallas kernels for 2%

profile of v8, /device:TPU:2, one launch (start us, length us, event | category | flops | bytes accessed | tf_op | source)
XLA Modules:
  0.0 107.3 jit_solution(711309120023126002)
XLA Ops:
  0.6 1.3 %summary.1 = (f32[512,128]{1,0:T(8,128)S(1)}, f32[16,128]{1,0:T(8,128)S(1)}, f32[1,512]{1,0:T(1,128)S(1)}) custom-call(s32[4]{0:T(128)} %ints_ref.1, bf16[128,512]{1,0:T(8,128)(2,1)} %k_ref.7, bf16[128,512]{1,0:T(8,128)(2,1)} %v_ref.7, f32[1,512]{1,0:T(1,128)} %bitcast.18), custom_call_target="tpu_custom_call" | custom-call | tf_op jit(solution)/shard_map/summary/pallas_call | solution.py:276
  1.9 29.8 %all_to_all.25 = f32[64,8,128]{2,1,0:T(8,128)S(1)} all-to-all(f32[64,8,128]{2,1,0:T(8,128)S(1)} %bitcast.17), channel_id=1, replica_groups={{576,592,608,624,640,656,672,688,704,720,736,752,768,784,800,816,832,84..., dimensions={0} | all-to-all | bytes 524288 | tf_op jit(solution)/shard_map/all_to_all | solution.py:24
  31.7 0.0 copy-start.4
  31.8 0.0 copy-start
  31.8 0.0 copy-start.1
  31.8 0.0 copy-start.2
  31.8 0.0 copy-start.3
  31.8 17.6 %all_to_all.26 = f32[64,8,128]{2,1,0:T(8,128)S(1)} all-to-all(f32[64,8,128]{2,1,0:T(8,128)S(1)} %bitcast.15), channel_id=1, replica_groups={{576,592,608,624,640,656,672,688,704,720,736,752,768,784,800,816,832,84..., dimensions={0} | all-to-all | bytes 524288 | tf_op jit(solution)/shard_map/all_to_all | solution.py:24
  49.4 0.0 copy-done.4
  49.5 0.0 copy-done
  49.5 0.0 copy-done.1
  49.5 0.0 copy-done.2
  49.5 0.0 copy-done.3
  49.5 0.6 attend.1
  50.1 15.7 %all_to_all.27.stats_ref = f32[16,8,128]{2,1,0:T(8,128)S(1)} all-to-all(f32[16,8,128]{2,1,0:T(8,128)S(1)} %get-tuple-element.27), channel_id=1, replica_groups={{14,15,0,1,2,3,4,5,6,7,8,9,10,11,12,13},{30,31,16,17,18,19,20,21,22,23,..., dimensions={0} | all-to-all | bytes 131072 | tf_op jit(solution)/shard_map/all_to_all | solution.py:24
  65.8 0.5 ahead.1
  66.3 19.9 %all_to_all.28 = f32[64,9,1,128]{3,2,1,0:T(1,128)S(1)} all-to-all(f32[64,9,1,128]{3,2,1,0:T(1,128)S(1)} %bitcast.16), channel_id=1, replica_groups={{576,592,608,624,640,656,672,688,704,720,736,752,768,784,800,816,832,84..., dimensions={0} | all-to-all | bytes 589824 | tf_op jit(solution)/shard_map/all_to_all | solution.py:24
  86.2 0.8 backward_scan.1
  87.0 11.8 %all-to-all-start.4 = ((f32[64,9,1,128]{3,2,1,0:T(1,128)}), f32[64,9,1,128]{3,2,1,0:T(1,128)S(1)}, u32[]{:S(2)}, u32[]{:S(2)}) async-start(f32[64,9,1,128]{3,2,1,0:T(1,128)} %bitcast.7), calls=%async_computation.4 | async-start | bytes 589824 | tf_op jit(solution)/shard_map/all_to_all | solution.py:24
  98.7 1.7 %early_grads.1 = (bf16[128,512]{1,0:T(8,128)(2,1)}, bf16[128,512]{1,0:T(8,128)(2,1)}, f32[128,512]{1,0:T(8,128)S(1)}, f32[128,512]{1,0:T(8,128)S(1)}, f32[128,512]{1,0:T(8,128)S(1)}) custom-call(f32[16,128]{1,0:T(8,128)S(1)} %get-tuple-element.24.spans_ref, f32[16,8,128]{2,1,0:T(8,128)S(1)} %all_to_all.27.stats_ref, ...), custom_call_target="tpu_custom_call" | custom-call | flops 167772160 | bytes 1835008 | tf_op jit(solution)/shard_map/early_grads/pallas_call | solution.py:276
  100.4 5.9 %all-to-all-done.4 = f32[64,9,1,128]{3,2,1,0:T(1,128)S(1)} async-done(((f32[64,9,1,128]{3,2,1,0:T(1,128)}), f32[64,9,1,128]{3,2,1,0:T(1,128)S(1)}, u32[]{:S(2)}, u32[]{:S(2)}) %all-to-all-start.4) | async-done | bytes 294944 | tf_op jit(solution)/shard_map/all_to_all | solution.py:24
  106.3 1.0 final.1
  (1 shorter events, 0.0 us)
Async XLA Ops:
  31.7 17.7 %copy-start.4 = (bf16[128,512]{1,0:T(8,128)(2,1)S(1)}, bf16[128,512]{1,0:T(8,128)(2,1)}, u32[]{:S(2)}) copy-start(bf16[128,512]{1,0:T(8,128)(2,1)} %grad_ref.1) | copy-start | bytes 393220
  31.8 17.7 %copy-start = (bf16[128,512]{1,0:T(8,128)(2,1)S(1)}, bf16[128,512]{1,0:T(8,128)(2,1)}, u32[]{:S(2)}) copy-start(bf16[128,512]{1,0:T(8,128)(2,1)} %k_ref.7) | copy-start | bytes 393220
  31.8 17.6 %copy-start.1 = (bf16[128,512]{1,0:T(8,128)(2,1)S(1)}, bf16[128,512]{1,0:T(8,128)(2,1)}, u32[]{:S(2)}) copy-start(bf16[128,512]{1,0:T(8,128)(2,1)} %v_ref.7) | copy-start | bytes 393220
  31.8 17.6 %copy-start.2 = (bf16[128,512]{1,0:T(8,128)(2,1)S(1)}, bf16[128,512]{1,0:T(8,128)(2,1)}, u32[]{:S(2)}) copy-start(bf16[128,512]{1,0:T(8,128)(2,1)} %q_ref.5) | copy-start | bytes 393220
  31.8 17.6 %copy-start.3 = (bf16[128,512]{1,0:T(8,128)(2,1)S(1)}, bf16[128,512]{1,0:T(8,128)(2,1)}, u32[]{:S(2)}) copy-start(bf16[128,512]{1,0:T(8,128)(2,1)} %gate_ref.3) | copy-start | bytes 393220
  87.0 19.3 %all-to-all-start.4 = ((f32[64,9,1,128]{3,2,1,0:T(1,128)}), f32[64,9,1,128]{3,2,1,0:T(1,128)S(1)}, u32[]{:S(2)}, u32[]{:S(2)}) async-start(f32[64,9,1,128]{3,2,1,0:T(1,128)} %bitcast.7), calls=%async_computation.4 | async-start | bytes 589824 | tf_op jit(solution)/shard_map/all_to_all | solution.py:24

commit v9 on v8

--- a/solution.py
+++ b/solution.py
@@ -214,9 +214,10 @@
 
 def early_grads_kernel(
     spans_ref, stats_ref, attention_ref, scaled_ref, gate_ref, grad_ref, q_ref, k_ref, v_ref,
-    weights_ref, prefix_ref, early_ref, grad_q_ref, grad_gate_ref, local_k_ref, local_v_ref, late_ref,
+    weights_ref, prefix_ref, early_ref, grad_q_ref, grad_gate_ref, local_k_ref, local_v_ref, late_ref, spans_out_ref,
 ):
     rows, features = q_ref.shape
+    spans_out_ref[...] = spans_ref[...]
     inverse, _ = token_scales(stats_ref)
     for head in range(features // DH):
         at = cols(head)
@@ -336,10 +337,10 @@
         stats, attention, gated, scaled, queries, early,
     )
     there = across(message, step)
-    grad_q, grad_gate, local_k, local_v, late = call(
+    grad_q, grad_gate, local_k, local_v, late, spans = call(
         early_grads_kernel,
         "early_grads",
-        [block_half, block_half, block_wide, block_wide, block_wide],
+        [block_half, block_half, block_wide, block_wide, block_wide, (spans.shape, wide)],
         spans, stats, attention, scaled, gate_in, grad, queries, key_rows, value_rows,
         weights, prefix, early,
         flops=20 * area * DH, bytes_moved=28 * area,

time: 108 us -> 108 us (level)
  no operation moved by 1% of the time
where the time goes in v9:
time: 108 us; the launch traced here: 107 us
  blocking collectives  82.5 us (76%)
  starting transfers between devices  11.8 us (11%)
  waiting for transfers between devices  6.58 us (6%)
  Pallas kernels  5.81 us (5%)
    all_to_all x4, blocking collectives, swap(): return lax.all_to_all(array, axis, 0, 0, axis_index_groups=groups)  82.5 us
    all_to_all x1, starting transfers between devices, swap(): return lax.all_to_all(array, axis, 0, 0, axis_index_groups=groups)  11.8 us
    all_to_all x1, waiting for transfers between devices, swap(): return lax.all_to_all(array, axis, 0, 0, axis_index_groups=groups)  6.58 us
    pallas_call x7, Pallas kernels, call(): pl.pallas_call(kernel, out_shape=out_shape, in_specs=[pl.BlockSpec(memory...  5.81 us
  transfers between devices with their start and end apart: 1, of which 1 were waited for; matrix products, arithmetic and copies ran while one was open for 0% of the time, Pallas kernels for 2%

profile of v9, /device:TPU:2, one launch (start us, length us, event | category | flops | bytes accessed | tf_op | source)
XLA Modules:
  0.0 107.4 jit_solution(17074941341140577229)
XLA Ops:
  0.6 1.3 %summary.1 = (f32[512,128]{1,0:T(8,128)S(1)}, f32[16,128]{1,0:T(8,128)S(1)}, f32[1,512]{1,0:T(1,128)S(1)}) custom-call(s32[4]{0:T(128)} %ints_ref.1, bf16[128,512]{1,0:T(8,128)(2,1)} %k_ref.7, bf16[128,512]{1,0:T(8,128)(2,1)} %v_ref.7, f32[1,512]{1,0:T(1,128)} %bitcast.18), custom_call_target="tpu_custom_call" | custom-call | tf_op jit(solution)/shard_map/summary/pallas_call | solution.py:277
  1.9 29.8 %all_to_all.25 = f32[64,8,128]{2,1,0:T(8,128)S(1)} all-to-all(f32[64,8,128]{2,1,0:T(8,128)S(1)} %bitcast.17), channel_id=1, replica_groups={{576,592,608,624,640,656,672,688,704,720,736,752,768,784,800,816,832,84..., dimensions={0} | all-to-all | bytes 524288 | tf_op jit(solution)/shard_map/all_to_all | solution.py:24
  31.7 0.0 copy-start.4
  31.8 0.0 copy-start
  31.8 0.0 copy-start.1
  31.8 0.0 copy-start.2
  31.8 0.0 copy-start.3
  31.8 17.6 %all_to_all.26 = f32[64,8,128]{2,1,0:T(8,128)S(1)} all-to-all(f32[64,8,128]{2,1,0:T(8,128)S(1)} %bitcast.16), channel_id=1, replica_groups={{576,592,608,624,640,656,672,688,704,720,736,752,768,784,800,816,832,84..., dimensions={0} | all-to-all | bytes 524288 | tf_op jit(solution)/shard_map/all_to_all | solution.py:24
  49.4 0.0 copy-done.4
  49.5 0.0 copy-done
  49.5 0.0 copy-done.1
  49.5 0.0 copy-done.2
  49.5 0.0 copy-done.3
  49.5 0.6 attend.1
  50.1 15.7 %all_to_all.27.stats_ref = f32[16,8,128]{2,1,0:T(8,128)S(1)} all-to-all(f32[16,8,128]{2,1,0:T(8,128)S(1)} %get-tuple-element.28), channel_id=1, replica_groups={{14,15,0,1,2,3,4,5,6,7,8,9,10,11,12,13},{30,31,16,17,18,19,20,21,22,23,..., dimensions={0} | all-to-all | bytes 131072 | tf_op jit(solution)/shard_map/all_to_all | solution.py:24
  65.8 1.2 %ahead.1 = (bf16[128,512]{1,0:T(8,128)(2,1)S(1)}, f32[576,128]{1,0:T(8,128)}) custom-call(f32[16,8,128]{2,1,0:T(8,128)S(1)} %all_to_all.27.stats_ref, f32[128,512]{1,0:T(8,128)S(1)} %get-tuple-element.29.attention_ref, f32[128,512]{1,0:T(8,128)S(1)} %get-tuple-element.31.gated_ref, f32[128,512]{1,0:T(8,128)S(1)} %get-tuple-element.30.scaled_ref, ...), custom_call_target="tpu_custom_call" | custom-call | tf_op jit(solution)/shard_map/ahead/pallas_call | solution.py:277
  67.0 11.8 %all-to-all-start.3 = ((f32[64,9,1,128]{3,2,1,0:T(1,128)}), f32[64,9,1,128]{3,2,1,0:T(1,128)S(1)}, u32[]{:S(2)}, u32[]{:S(2)}) async-start(f32[64,9,1,128]{3,2,1,0:T(1,128)} %bitcast.5), calls=%async_computation.3 | async-start | bytes 589824 | tf_op jit(solution)/shard_map/all_to_all | solution.py:24
  78.8 1.7 %early_grads.1 = (bf16[128,512]{1,0:T(8,128)(2,1)}, bf16[128,512]{1,0:T(8,128)(2,1)}, f32[128,512]{1,0:T(8,128)S(1)}, f32[128,512]{1,0:T(8,128)S(1)}, f32[128,512]{1,0:T(8,128)S(1)}, /*index=5*/f32[16,128]{1,0:T(8,128)S(1)}) custom-call(f32[16,128]{1,0:T(8,128)S(1)} %get-tuple-element.25.spans_ref, f32[16,8,128]{2,1,0:T(8,128)S(1)} %all_to_all.27.stats_ref, ...), custom_call_target="tpu_custom_call" | custom-call | flops 167772160 | bytes 1835008 | tf_op jit(solution)/shard_map/early_grads/pallas_call | solution.py:277
  80.5 6.6 %all-to-all-done.3 = f32[64,9,1,128]{3,2,1,0:T(1,128)S(1)} async-done(((f32[64,9,1,128]{3,2,1,0:T(1,128)}), f32[64,9,1,128]{3,2,1,0:T(1,128)S(1)}, u32[]{:S(2)}, u32[]{:S(2)}) %all-to-all-start.3) | async-done | bytes 294944 | tf_op jit(solution)/shard_map/all_to_all | solution.py:24
  87.1 0.1 backward_scan.1
  87.1 19.3 %all_to_all.28 = f32[64,9,1,128]{3,2,1,0:T(1,128)S(1)} all-to-all(f32[64,9,1,128]{3,2,1,0:T(1,128)S(1)} %bitcast.13), channel_id=1, replica_groups={{576,592,608,624,640,656,672,688,704,720,736,752,768,784,800,816,832,84..., dimensions={0} | all-to-all | bytes 589824 | tf_op jit(solution)/shard_map/all_to_all | solution.py:24
  106.4 1.0 final.1
  (1 shorter events, 0.0 us)
Async XLA Ops:
  31.7 17.7 %copy-start.4 = (bf16[128,512]{1,0:T(8,128)(2,1)S(1)}, bf16[128,512]{1,0:T(8,128)(2,1)}, u32[]{:S(2)}) copy-start(bf16[128,512]{1,0:T(8,128)(2,1)} %grad_ref.1) | copy-start | bytes 393220
  31.8 17.7 %copy-start = (bf16[128,512]{1,0:T(8,128)(2,1)S(1)}, bf16[128,512]{1,0:T(8,128)(2,1)}, u32[]{:S(2)}) copy-start(bf16[128,512]{1,0:T(8,128)(2,1)} %k_ref.7) | copy-start | bytes 393220
  31.8 17.6 %copy-start.1 = (bf16[128,512]{1,0:T(8,128)(2,1)S(1)}, bf16[128,512]{1,0:T(8,128)(2,1)}, u32[]{:S(2)}) copy-start(bf16[128,512]{1,0:T(8,128)(2,1)} %v_ref.7) | copy-start | bytes 393220
  31.8 17.6 %copy-start.2 = (bf16[128,512]{1,0:T(8,128)(2,1)S(1)}, bf16[128,512]{1,0:T(8,128)(2,1)}, u32[]{:S(2)}) copy-start(bf16[128,512]{1,0:T(8,128)(2,1)} %q_ref.5) | copy-start | bytes 393220
  31.8 17.6 %copy-start.3 = (bf16[128,512]{1,0:T(8,128)(2,1)S(1)}, bf16[128,512]{1,0:T(8,128)(2,1)}, u32[]{:S(2)}) copy-start(bf16[128,512]{1,0:T(8,128)(2,1)} %gate_ref.3) | copy-start | bytes 393220
  67.0 20.1 %all-to-all-start.3 = ((f32[64,9,1,128]{3,2,1,0:T(1,128)}), f32[64,9,1,128]{3,2,1,0:T(1,128)S(1)}, u32[]{:S(2)}, u32[]{:S(2)}) async-start(f32[64,9,1,128]{3,2,1,0:T(1,128)} %bitcast.5), calls=%async_computation.3 | async-start | bytes 589824 | tf_op jit(solution)/shard_map/all_to_all | solution.py:24

commit v10 on v8

--- a/solution.py
+++ b/solution.py
@@ -173,16 +173,13 @@
         crossed = crossed + scaled * attention
     squares = jnp.sum(squares.T, axis=0, keepdims=True)
     crossed = jnp.sum(crossed.T, axis=0, keepdims=True)
-    line = lax.broadcasted_iota(jnp.int32, (8, DH), 0)
-    pair = jnp.where(line == 0, squares, jnp.where(line == 1, crossed, 0.0))
+    pair = jnp.concatenate([squares, crossed], axis=0)
     for member in range(stats_ref.shape[0]):
         stats_ref[member] = pair
 
 
 def token_scales(stats_ref):
-    total = stats_ref[0]
-    for member in range(1, stats_ref.shape[0]):
-        total = total + stats_ref[member]
+    total = jnp.sum(stats_ref[...], axis=0)
     inverse = lax.rsqrt(total[0:1] * (1.0 / HD) + norm_eps)
     pull = inverse * inverse * inverse * total[1:2] * (1.0 / HD)
     line = lax.broadcasted_iota(jnp.int32, (8, DH), 0)
@@ -325,7 +322,7 @@
     attention, stats, weights, gated, scaled, early = call(
         attend_kernel,
         "attend",
-        [block_wide, ((head_members, 8, rows), wide), block_half, block_wide, block_wide, block_wide],
+        [block_wide, ((head_members, 2, rows), wide), block_half, block_wide, block_wide, block_wide],
         spans, queries, key_rows, value_rows, gate_in, grad_out, gain, prefix,
     )
     stats = swap(stats, "head")

time: 108 us -> 107 us (level)
  no operation moved by 1% of the time
where the time goes in v10:
time: 107 us
  blocking collectives  82.6 us (77%)
  starting transfers between devices  11.8 us (11%)
  Pallas kernels  5.8 us (5%)
  waiting for transfers between devices  5.8 us (5%)
    all_to_all x4, blocking collectives, swap(): return lax.all_to_all(array, axis, 0, 0, axis_index_groups=groups)  82.6 us
    all_to_all x1, starting transfers between devices, swap(): return lax.all_to_all(array, axis, 0, 0, axis_index_groups=groups)  11.8 us
    all_to_all x1, waiting for transfers between devices, swap(): return lax.all_to_all(array, axis, 0, 0, axis_index_groups=groups)  5.8 us
    pallas_call x7, Pallas kernels, call(): pl.pallas_call(kernel, out_shape=out_shape, in_specs=[pl.BlockSpec(memory...  5.8 us
  transfers between devices with their start and end apart: 1, of which 1 were waited for; matrix products, arithmetic and copies ran while one was open for 0% of the time, Pallas kernels for 2%

profile of v10, /device:TPU:2, one launch (start us, length us, event | category | flops | bytes accessed | tf_op | source)
XLA Modules:
  0.0 106.7 jit_solution(18070411832977349290)
XLA Ops:
  0.6 1.3 %summary.1 = (f32[512,128]{1,0:T(8,128)S(1)}, f32[16,128]{1,0:T(8,128)S(1)}, f32[1,512]{1,0:T(1,128)S(1)}) custom-call(s32[4]{0:T(128)} %ints_ref.1, bf16[128,512]{1,0:T(8,128)(2,1)} %k_ref.7, bf16[128,512]{1,0:T(8,128)(2,1)} %v_ref.7, f32[1,512]{1,0:T(1,128)} %bitcast.18), custom_call_target="tpu_custom_call" | custom-call | tf_op jit(solution)/shard_map/summary/pallas_call | solution.py:273
  1.9 29.8 %all_to_all.25 = f32[64,8,128]{2,1,0:T(8,128)S(1)} all-to-all(f32[64,8,128]{2,1,0:T(8,128)S(1)} %bitcast.17), channel_id=1, replica_groups={{576,592,608,624,640,656,672,688,704,720,736,752,768,784,800,816,832,84..., dimensions={0} | all-to-all | bytes 524288 | tf_op jit(solution)/shard_map/all_to_all | solution.py:24
  31.7 0.0 copy-start.4
  31.8 0.0 copy-start
  31.8 0.0 copy-start.1
  31.8 0.0 copy-start.2
  31.8 0.0 copy-start.3
  31.8 17.6 %all_to_all.26 = f32[64,8,128]{2,1,0:T(8,128)S(1)} all-to-all(f32[64,8,128]{2,1,0:T(8,128)S(1)} %bitcast.15), channel_id=1, replica_groups={{576,592,608,624,640,656,672,688,704,720,736,752,768,784,800,816,832,84..., dimensions={0} | all-to-all | bytes 524288 | tf_op jit(solution)/shard_map/all_to_all | solution.py:24
  49.4 0.0 copy-done.4
  49.5 0.0 copy-done
  49.5 0.0 copy-done.1
  49.5 0.0 copy-done.2
  49.5 0.0 copy-done.3
  49.5 0.6 attend.1
  50.1 15.4 %all_to_all.27.stats_ref = f32[16,2,128]{2,1,0:T(2,128)S(1)} all-to-all(f32[16,2,128]{2,1,0:T(2,128)S(1)} %get-tuple-element.27), channel_id=1, replica_groups={{14,15,0,1,2,3,4,5,6,7,8,9,10,11,12,13},{30,31,16,17,18,19,20,21,22,23,..., dimensions={0} | all-to-all | bytes 32768 | tf_op jit(solution)/shard_map/all_to_all | solution.py:24
  65.5 0.5 ahead.1
  65.9 19.8 %all_to_all.28 = f32[64,9,1,128]{3,2,1,0:T(1,128)S(1)} all-to-all(f32[64,9,1,128]{3,2,1,0:T(1,128)S(1)} %bitcast.16), channel_id=1, replica_groups={{576,592,608,624,640,656,672,688,704,720,736,752,768,784,800,816,832,84..., dimensions={0} | all-to-all | bytes 589824 | tf_op jit(solution)/shard_map/all_to_all | solution.py:24
  85.7 0.8 backward_scan.1
  86.5 11.8 %all-to-all-start.4 = ((f32[64,9,1,128]{3,2,1,0:T(1,128)}), f32[64,9,1,128]{3,2,1,0:T(1,128)S(1)}, u32[]{:S(2)}, u32[]{:S(2)}) async-start(f32[64,9,1,128]{3,2,1,0:T(1,128)} %bitcast.7), calls=%async_computation.4 | async-start | bytes 589824 | tf_op jit(solution)/shard_map/all_to_all | solution.py:24
  98.3 1.7 %early_grads.1 = (bf16[128,512]{1,0:T(8,128)(2,1)}, bf16[128,512]{1,0:T(8,128)(2,1)}, f32[128,512]{1,0:T(8,128)S(1)}, f32[128,512]{1,0:T(8,128)S(1)}, f32[128,512]{1,0:T(8,128)S(1)}) custom-call(f32[16,128]{1,0:T(8,128)S(1)} %get-tuple-element.24.spans_ref, f32[16,2,128]{2,1,0:T(2,128)S(1)} %all_to_all.27.stats_ref, ...), custom_call_target="tpu_custom_call" | custom-call | flops 167772160 | bytes 1835008 | tf_op jit(solution)/shard_map/early_grads/pallas_call | solution.py:273
  99.9 5.8 %all-to-all-done.4 = f32[64,9,1,128]{3,2,1,0:T(1,128)S(1)} async-done(((f32[64,9,1,128]{3,2,1,0:T(1,128)}), f32[64,9,1,128]{3,2,1,0:T(1,128)S(1)}, u32[]{:S(2)}, u32[]{:S(2)}) %all-to-all-start.4) | async-done | bytes 294944 | tf_op jit(solution)/shard_map/all_to_all | solution.py:24
  105.7 1.0 final.1
  (1 shorter events, 0.0 us)
Async XLA Ops:
  31.7 17.7 %copy-start.4 = (bf16[128,512]{1,0:T(8,128)(2,1)S(1)}, bf16[128,512]{1,0:T(8,128)(2,1)}, u32[]{:S(2)}) copy-start(bf16[128,512]{1,0:T(8,128)(2,1)} %grad_ref.1) | copy-start | bytes 393220
  31.8 17.7 %copy-start = (bf16[128,512]{1,0:T(8,128)(2,1)S(1)}, bf16[128,512]{1,0:T(8,128)(2,1)}, u32[]{:S(2)}) copy-start(bf16[128,512]{1,0:T(8,128)(2,1)} %k_ref.7) | copy-start | bytes 393220
  31.8 17.6 %copy-start.1 = (bf16[128,512]{1,0:T(8,128)(2,1)S(1)}, bf16[128,512]{1,0:T(8,128)(2,1)}, u32[]{:S(2)}) copy-start(bf16[128,512]{1,0:T(8,128)(2,1)} %v_ref.7) | copy-start | bytes 393220
  31.8 17.6 %copy-start.2 = (bf16[128,512]{1,0:T(8,128)(2,1)S(1)}, bf16[128,512]{1,0:T(8,128)(2,1)}, u32[]{:S(2)}) copy-start(bf16[128,512]{1,0:T(8,128)(2,1)} %q_ref.5) | copy-start | bytes 393220
  31.8 17.6 %copy-start.3 = (bf16[128,512]{1,0:T(8,128)(2,1)S(1)}, bf16[128,512]{1,0:T(8,128)(2,1)}, u32[]{:S(2)}) copy-start(bf16[128,512]{1,0:T(8,128)(2,1)} %gate_ref.3) | copy-start | bytes 393220
  86.5 19.2 %all-to-all-start.4 = ((f32[64,9,1,128]{3,2,1,0:T(1,128)}), f32[64,9,1,128]{3,2,1,0:T(1,128)S(1)}, u32[]{:S(2)}, u32[]{:S(2)}) async-start(f32[64,9,1,128]{3,2,1,0:T(1,128)} %bitcast.7), calls=%async_computation.4 | async-start | bytes 589824 | tf_op jit(solution)/shard_map/all_to_all | solution.py:24

commit v11 on v10

--- a/solution.py
+++ b/solution.py
@@ -261,9 +261,11 @@
         carried_k = dot_nt(twice(v_ref[:, at], 1), jnp.concatenate([high, low], axis=1))
         carried_v = dot(twice(k_ref[:, at], 1), jnp.concatenate([high, low], axis=0))
         keys[:, at] = (local_k_ref[:, at] + late * carried_k).astype(half)
-        send(keys.at[:, at], grad_k_ref.at[:, at])
         values[:, at] = (local_v_ref[:, at] + late * carried_v).astype(half)
-        send(values.at[:, at], grad_v_ref.at[:, at])
+        if head % 2 == 1:
+            both = slice((head - 1) * DH, (head + 1) * DH)
+            send(keys.at[:, both], grad_k_ref.at[:, both])
+            send(values.at[:, both], grad_v_ref.at[:, both])
     for copy in copies:
         copy.wait()
 
@@ -352,7 +354,7 @@
             pltpu.VMEM((rows, features), half),
             pltpu.VMEM((rows, features), half),
             pltpu.VMEM((1, features), wide),
-            pltpu.SemaphoreType.DMA((2 * features // DH + 1,)),
+            pltpu.SemaphoreType.DMA((features // DH + 1,)),
         ],
     )
     return grad_q, grad_k, grad_v, grad_gate, grad_gain.reshape(features)

time: 107 us -> 107 us (level)
  no operation moved by 1% of the time
where the time goes in v11:
time: 107 us
  blocking collectives  82.6 us (77%)
  starting transfers between devices  11.8 us (11%)
  waiting for transfers between devices  5.8 us (5%)
  Pallas kernels  5.79 us (5%)
    all_to_all x4, blocking collectives, swap(): return lax.all_to_all(array, axis, 0, 0, axis_index_groups=groups)  82.6 us
    all_to_all x1, starting transfers between devices, swap(): return lax.all_to_all(array, axis, 0, 0, axis_index_groups=groups)  11.8 us
    all_to_all x1, waiting for transfers between devices, swap(): return lax.all_to_all(array, axis, 0, 0, axis_index_groups=groups)  5.8 us
    pallas_call x7, Pallas kernels, call(): pl.pallas_call(kernel, out_shape=out_shape, in_specs=[pl.BlockSpec(memory...  5.79 us
  transfers between devices with their start and end apart: 1, of which 1 were waited for; matrix products, arithmetic and copies ran while one was open for 0% of the time, Pallas kernels for 2%

profile of v11, /device:TPU:2, one launch (start us, length us, event | category | flops | bytes accessed | tf_op | source)
XLA Modules:
  0.0 106.7 jit_solution(11678689310592520558)
XLA Ops:
  0.6 1.3 %summary.1 = (f32[512,128]{1,0:T(8,128)S(1)}, f32[16,128]{1,0:T(8,128)S(1)}, f32[1,512]{1,0:T(1,128)S(1)}) custom-call(s32[4]{0:T(128)} %ints_ref.1, bf16[128,512]{1,0:T(8,128)(2,1)} %k_ref.7, bf16[128,512]{1,0:T(8,128)(2,1)} %v_ref.7, f32[1,512]{1,0:T(1,128)} %bitcast.18), custom_call_target="tpu_custom_call" | custom-call | tf_op jit(solution)/shard_map/summary/pallas_call | solution.py:275
  1.9 29.8 %all_to_all.25 = f32[64,8,128]{2,1,0:T(8,128)S(1)} all-to-all(f32[64,8,128]{2,1,0:T(8,128)S(1)} %bitcast.17), channel_id=1, replica_groups={{576,592,608,624,640,656,672,688,704,720,736,752,768,784,800,816,832,84..., dimensions={0} | all-to-all | bytes 524288 | tf_op jit(solution)/shard_map/all_to_all | solution.py:24
  31.7 0.0 copy-start.4
  31.8 0.0 copy-start
  31.8 0.0 copy-start.1
  31.8 0.0 copy-start.2
  31.8 0.0 copy-start.3
  31.8 17.6 %all_to_all.26 = f32[64,8,128]{2,1,0:T(8,128)S(1)} all-to-all(f32[64,8,128]{2,1,0:T(8,128)S(1)} %bitcast.15), channel_id=1, replica_groups={{576,592,608,624,640,656,672,688,704,720,736,752,768,784,800,816,832,84..., dimensions={0} | all-to-all | bytes 524288 | tf_op jit(solution)/shard_map/all_to_all | solution.py:24
  49.4 0.0 copy-done.4
  49.5 0.0 copy-done
  49.5 0.0 copy-done.1
  49.5 0.0 copy-done.2
  49.5 0.0 copy-done.3
  49.5 0.6 attend.1
  50.1 15.4 %all_to_all.27.stats_ref = f32[16,2,128]{2,1,0:T(2,128)S(1)} all-to-all(f32[16,2,128]{2,1,0:T(2,128)S(1)} %get-tuple-element.27), channel_id=1, replica_groups={{14,15,0,1,2,3,4,5,6,7,8,9,10,11,12,13},{30,31,16,17,18,19,20,21,22,23,..., dimensions={0} | all-to-all | bytes 32768 | tf_op jit(solution)/shard_map/all_to_all | solution.py:24
  65.5 0.5 ahead.1
  65.9 19.8 %all_to_all.28 = f32[64,9,1,128]{3,2,1,0:T(1,128)S(1)} all-to-all(f32[64,9,1,128]{3,2,1,0:T(1,128)S(1)} %bitcast.16), channel_id=1, replica_groups={{576,592,608,624,640,656,672,688,704,720,736,752,768,784,800,816,832,84..., dimensions={0} | all-to-all | bytes 589824 | tf_op jit(solution)/shard_map/all_to_all | solution.py:24
  85.7 0.8 backward_scan.1
  86.5 11.8 %all-to-all-start.4 = ((f32[64,9,1,128]{3,2,1,0:T(1,128)}), f32[64,9,1,128]{3,2,1,0:T(1,128)S(1)}, u32[]{:S(2)}, u32[]{:S(2)}) async-start(f32[64,9,1,128]{3,2,1,0:T(1,128)} %bitcast.7), calls=%async_computation.4 | async-start | bytes 589824 | tf_op jit(solution)/shard_map/all_to_all | solution.py:24
  98.3 1.7 %early_grads.1 = (bf16[128,512]{1,0:T(8,128)(2,1)}, bf16[128,512]{1,0:T(8,128)(2,1)}, f32[128,512]{1,0:T(8,128)S(1)}, f32[128,512]{1,0:T(8,128)S(1)}, f32[128,512]{1,0:T(8,128)S(1)}) custom-call(f32[16,128]{1,0:T(8,128)S(1)} %get-tuple-element.24.spans_ref, f32[16,2,128]{2,1,0:T(2,128)S(1)} %all_to_all.27.stats_ref, ...), custom_call_target="tpu_custom_call" | custom-call | flops 167772160 | bytes 1835008 | tf_op jit(solution)/shard_map/early_grads/pallas_call | solution.py:275
  99.9 5.8 %all-to-all-done.4 = f32[64,9,1,128]{3,2,1,0:T(1,128)S(1)} async-done(((f32[64,9,1,128]{3,2,1,0:T(1,128)}), f32[64,9,1,128]{3,2,1,0:T(1,128)S(1)}, u32[]{:S(2)}, u32[]{:S(2)}) %all-to-all-start.4) | async-done | bytes 294944 | tf_op jit(solution)/shard_map/all_to_all | solution.py:24
  105.7 1.0 final.1
  (1 shorter events, 0.0 us)
Async XLA Ops:
  31.7 17.7 %copy-start.4 = (bf16[128,512]{1,0:T(8,128)(2,1)S(1)}, bf16[128,512]{1,0:T(8,128)(2,1)}, u32[]{:S(2)}) copy-start(bf16[128,512]{1,0:T(8,128)(2,1)} %grad_ref.1) | copy-start | bytes 393220
  31.8 17.7 %copy-start = (bf16[128,512]{1,0:T(8,128)(2,1)S(1)}, bf16[128,512]{1,0:T(8,128)(2,1)}, u32[]{:S(2)}) copy-start(bf16[128,512]{1,0:T(8,128)(2,1)} %k_ref.7) | copy-start | bytes 393220
  31.8 17.6 %copy-start.1 = (bf16[128,512]{1,0:T(8,128)(2,1)S(1)}, bf16[128,512]{1,0:T(8,128)(2,1)}, u32[]{:S(2)}) copy-start(bf16[128,512]{1,0:T(8,128)(2,1)} %v_ref.7) | copy-start | bytes 393220
  31.8 17.6 %copy-start.2 = (bf16[128,512]{1,0:T(8,128)(2,1)S(1)}, bf16[128,512]{1,0:T(8,128)(2,1)}, u32[]{:S(2)}) copy-start(bf16[128,512]{1,0:T(8,128)(2,1)} %q_ref.5) | copy-start | bytes 393220
  31.8 17.6 %copy-start.3 = (bf16[128,512]{1,0:T(8,128)(2,1)S(1)}, bf16[128,512]{1,0:T(8,128)(2,1)}, u32[]{:S(2)}) copy-start(bf16[128,512]{1,0:T(8,128)(2,1)} %gate_ref.3) | copy-start | bytes 393220
  86.5 19.2 %all-to-all-start.4 = ((f32[64,9,1,128]{3,2,1,0:T(1,128)}), f32[64,9,1,128]{3,2,1,0:T(1,128)S(1)}, u32[]{:S(2)}, u32[]{:S(2)}) async-start(f32[64,9,1,128]{3,2,1,0:T(1,128)} %bitcast.7), calls=%async_computation.4 | async-start | bytes 589824 | tf_op jit(solution)/shard_map/all_to_all | solution.py:24
